TPU v7x, 512 devices: a whole 4x8x8 slice. The times are simulated.
512 devices in a mesh: dp: 128 (over z, y, core), mp: 4 (over x).
Axes of the slice: x: 4, y: 8, z: 8, core: 2. Of those that a mesh axis runs over, the one named last changes fastest.
Arguments:
- tokens: int32 [1024, 5, 31], P(('dp', 'mp')), may hold values from 0 to 27
- accept: int32 [1024], P(('dp', 'mp')), may hold values from 0 to 1, as said below
- dest: int32 [153600, 1], P(('dp', 'mp')), may hold values from 0 to 127; in each aligned block of 300 rows (0 to 299, 300 to 599, ...) at most 5 rows name the same one
- mem_keys: bfloat16 [1024, 150, 512], P(('dp', 'mp')), may hold values from -6 to 6
- mem_values: bfloat16 [1024, 150, 512], P(('dp', 'mp')), may hold values from -6 to 6
- embed: bfloat16 [28, 512], replicated, may hold values from -6 to 6
- w_query: bfloat16 [512, 512], replicated, may hold values from -0.25 to 0.25
- w_key: bfloat16 [512, 512], replicated, may hold values from -0.25 to 0.25
- w_value: bfloat16 [512, 512], replicated, may hold values from -0.25 to 0.25
- w_self: bfloat16 [512, 512], replicated, may hold values from -0.25 to 0.25
- cross_query: bfloat16 [512, 512], replicated, may hold values from -0.25 to 0.25
- cross_out: bfloat16 [512, 512], replicated, may hold values from -0.25 to 0.25
- gain_self: float32 [512], replicated, may hold values from 0.5 to 1.5
- gain_cross: float32 [512], replicated, may hold values from 0.5 to 1.5
- w_in: bfloat16 [512, 1024], P(None, 'mp'), may hold values from -0.25 to 0.25
- w_down: bfloat16 [1024, 512], P('mp'), may hold values from -0.1875 to 0.1875
- gain_ff: float32 [512], replicated, may hold values from 0.5 to 1.5
- head: bfloat16 [512, 28], replicated, may hold values from -0.796875 to 0.796875
- momentum: float32 [1024, 1024], P(('dp', 'mp')), may hold values from -2.7 to 2.7
Outputs:
- new_momentum: float32 [1024, 1024], P(('dp', 'mp'))
- slot_loss: float32 [512, 640], P(('dp', 'mp'))
Inputs may be any that keep to these rules, and one draw needn't show every extreme that they name: `dest`: at most 5 tokens of one device name the same index, and some name one exactly 5 times. `accept`: among the spectra of the devices of one index of mp, drawn from the seed, exactly one is accepted; every other spectrum is accepted with probability one half.
All inputs are finite; a program needn't handle non-finite values.
Results may differ from a plain program's by a relative error of at most 0.0095.
Values may be sent and summed in bfloat16 or wider, within the bound.
No kernel may reach another device: no remote copies, remote signals or barrier semaphores. Data moves between devices by JAX's collectives and lax.ppermute only.
A program may use at most 64 MiB of HBM per device.

v0:
```python
import jax
import jax.numpy as jnp
from jax import lax
from jax.sharding import PartitionSpec as P

HEADS = 8


def layer_norm(values, gain):
    mean = jnp.mean(values, -1, keepdims=True)
    centered = values - mean
    variance = jnp.mean(centered * centered, -1, keepdims=True)
    return centered * lax.rsqrt(variance + 1e-05) * gain


def head_logp(total, gain_ff, head):
    normed = layer_norm(total, gain_ff)
    logits = jnp.dot(normed, head.astype(total.dtype), precision=lax.Precision.HIGHEST)
    return jax.nn.log_softmax(logits, -1)


def feed(states, w_in, w_down):
    pre = jnp.dot(states, w_in, preferred_element_type=jnp.float32)
    hidden = jax.nn.gelu(pre).astype(jnp.bfloat16)
    total = states.astype(jnp.float32) + jnp.dot(hidden, w_down, preferred_element_type=jnp.float32)
    return (pre, total)


def label_pick(labels, logp):
    vocab = logp.shape[-1]
    picks = (labels[:, None] == jnp.arange(vocab, dtype=jnp.int32)[None, :]).astype(logp.dtype)
    return jnp.sum(picks * logp, -1)


def decode(
    tokens,
    accept,
    keys,
    values,
    embed,
    w_query,
    w_key,
    w_value,
    w_self,
    cross_query,
    cross_out,
    gain_self,
    gain_cross,
    w_in,
    w_down,
    gain_ff,
    head,
):
    spec, beam, plus = tokens.shape
    steps = plus - 1
    rows = spec * beam * steps
    width = embed.shape[1]
    vocab = embed.shape[0]
    size = width // HEADS
    peaks = keys.shape[1]
    inputs = tokens[:, :, :steps].reshape(rows)
    labels = tokens[:, :, 1:].reshape(rows)
    picks = (inputs[:, None] == jnp.arange(vocab, dtype=jnp.int32)[None, :]).astype(jnp.bfloat16)
    embedded = jnp.dot(picks, embed, preferred_element_type=jnp.float32).astype(jnp.bfloat16)
    query = (
        jnp.dot(embedded, w_query, preferred_element_type=jnp.float32)
        .astype(jnp.bfloat16)
        .reshape(spec * beam, steps, HEADS, size)
    )
    keyed = (
        jnp.dot(embedded, w_key, preferred_element_type=jnp.float32)
        .astype(jnp.bfloat16)
        .reshape(spec * beam, steps, HEADS, size)
    )
    valued = (
        jnp.dot(embedded, w_value, preferred_element_type=jnp.float32)
        .astype(jnp.bfloat16)
        .reshape(spec * beam, steps, HEADS, size)
    )
    scores = jnp.einsum(
        "nqhd,nkhd->nhqk", query, keyed, preferred_element_type=jnp.float32
    ) / jnp.sqrt(jnp.float32(size))
    causal = jnp.arange(steps)[:, None] >= jnp.arange(steps)[None, :]
    scores = jnp.where(causal[None, None], scores, -1e30)
    probs = jax.nn.softmax(scores, -1).astype(jnp.bfloat16)
    context = (
        jnp.einsum("nhqk,nkhd->nqhd", probs, valued, preferred_element_type=jnp.float32)
        .astype(jnp.bfloat16)
        .reshape(rows, width)
    )
    attended = layer_norm(
        embedded.astype(jnp.float32) + jnp.dot(context, w_self, preferred_element_type=jnp.float32),
        gain_self,
    ).astype(jnp.bfloat16)
    cross_q = (
        jnp.dot(attended, cross_query, preferred_element_type=jnp.float32)
        .astype(jnp.bfloat16)
        .reshape(spec, beam * steps, HEADS, size)
    )
    mem_k = keys.reshape(spec, peaks, HEADS, size)
    mem_v = values.reshape(spec, peaks, HEADS, size)
    cross_s = jnp.einsum(
        "sqhd,skhd->shqk", cross_q, mem_k, preferred_element_type=jnp.float32
    ) / jnp.sqrt(jnp.float32(size))
    cross_p = jax.nn.softmax(cross_s, -1).astype(jnp.bfloat16)
    cross_c = (
        jnp.einsum("shqk,skhd->sqhd", cross_p, mem_v, preferred_element_type=jnp.float32)
        .astype(jnp.bfloat16)
        .reshape(rows, width)
    )
    states = layer_norm(
        attended.astype(jnp.float32)
        + jnp.dot(cross_c, cross_out, preferred_element_type=jnp.float32),
        gain_cross,
    ).astype(jnp.bfloat16)
    pre, total = feed(states, w_in, w_down)
    taken = label_pick(labels, head_logp(total, gain_ff, head))
    score = taken.reshape(spec, beam, steps).sum(-1)
    beam_weight = jax.nn.softmax(score / steps, -1)
    weight = (
        accept.astype(jnp.float32)[:, None, None]
        * beam_weight[:, :, None]
        * jnp.ones((1, 1, steps), jnp.float32)
    )
    return (states, labels, weight.reshape(rows), pre, total, taken)


def gradient(states, labels, coef, pre, total, w_down, gain_ff, head):

    def loss_of(value):
        return -jnp.sum(coef * label_pick(labels, head_logp(value, gain_ff, head)))

    unused, pull = jax.vjp(loss_of, total)
    (d_total,) = pull(jnp.ones((), total.dtype))
    d_out = d_total.astype(jnp.bfloat16)
    hidden = jax.nn.gelu(pre).astype(jnp.bfloat16)
    grad_down = lax.dot_general(
        hidden, d_out, (((0,), (0,)), ((), ())), preferred_element_type=jnp.float32
    )
    d_hidden = lax.dot_general(
        d_out, w_down, (((1,), (1,)), ((), ())), preferred_element_type=jnp.float32
    )
    unused_g, pull_gelu = jax.vjp(jax.nn.gelu, pre)
    (d_pre,) = pull_gelu(d_hidden)
    grad_in = lax.dot_general(
        d_pre.astype(jnp.bfloat16),
        states,
        (((0,), (0,)), ((), ())),
        preferred_element_type=jnp.float32,
    )
    return jnp.concatenate([grad_in, grad_down], 1)


def per_device(
    tokens,
    accept,
    dest,
    mem_keys,
    mem_values,
    embed,
    w_query,
    w_key,
    w_value,
    w_self,
    cross_query,
    cross_out,
    gain_self,
    gain_cross,
    w_in,
    w_down,
    gain_ff,
    head,
    momentum,
):
    w_in_all, w_down_all = (
        lax.all_gather(w_in, "mp", axis=1, tiled=True),
        lax.all_gather(w_down, "mp", axis=0, tiled=True),
    )
    states, labels, weight, pre, total, taken = decode(
        tokens,
        accept,
        mem_keys,
        mem_values,
        embed,
        w_query,
        w_key,
        w_value,
        w_self,
        cross_query,
        cross_out,
        gain_self,
        gain_cross,
        w_in_all,
        w_down_all,
        gain_ff,
        head,
    )
    rows = states.shape[0]
    width = states.shape[1]
    n_dp = lax.axis_size("dp")
    capacity = max(2, (2 * rows + n_dp - 1) // n_dp)
    target = dest[:, 0]
    hits = (target[:, None] == jnp.arange(n_dp, dtype=jnp.int32)[None, :]).astype(jnp.int32)
    rank = jnp.sum(jnp.cumsum(hits, 0) * hits, -1) - 1
    position = target * capacity + rank
    send_states = (
        jnp.zeros((n_dp * capacity, width), jnp.bfloat16)
        .at[position]
        .set(states)
        .reshape(n_dp, capacity, width)
    )
    send_labels = (
        jnp.zeros((n_dp * capacity,), jnp.int32).at[position].set(labels).reshape(n_dp, capacity)
    )
    send_weight = (
        jnp.zeros((n_dp * capacity,), jnp.float32).at[position].set(weight).reshape(n_dp, capacity)
    )
    got_states, got_labels, got_weight = (
        lax.all_to_all(send_states, "dp", split_axis=0, concat_axis=0, tiled=True),
        lax.all_to_all(send_labels, "dp", split_axis=0, concat_axis=0, tiled=True),
        lax.all_to_all(
            send_weight.astype(jnp.bfloat16), "dp", split_axis=0, concat_axis=0, tiled=True
        ).astype(send_weight.dtype),
    )
    slot_states = got_states.reshape(n_dp * capacity, width)
    slot_labels = got_labels.reshape(-1)
    slot_weight = got_weight.reshape(-1)
    slot_pre, slot_total = feed(slot_states, w_in_all, w_down_all)
    slot_taken = label_pick(slot_labels, head_logp(slot_total, gain_ff, head))
    slot_loss = -slot_weight * slot_taken
    coef = slot_weight / jnp.maximum(jnp.sum(slot_weight), 1.0)
    term = gradient(slot_states, slot_labels, coef, slot_pre, slot_total, w_down_all, gain_ff, head)
    share = lax.psum_scatter(term, ("dp", "mp"), scatter_dimension=0, tiled=True)
    return (0.9 * momentum + share, slot_loss[None, :])


def solution(mesh):
    placed = (
        P(("dp", "mp"), None, None),
        P(("dp", "mp")),
        P(("dp", "mp"), None),
        P(("dp", "mp"), None, None),
        P(("dp", "mp"), None, None),
        P(),
        P(),
        P(),
        P(),
        P(),
        P(),
        P(),
        P(),
        P(),
        P(None, "mp"),
        P("mp", None),
        P(),
        P(),
        P(("dp", "mp"), None),
    )
    return jax.shard_map(
        per_device,
        mesh=mesh,
        in_specs=placed,
        out_specs=(P(("dp", "mp"), None), P(("dp", "mp"), None)),
        check_vma=False,
    )
```

profile of v0, /device:TPU:1, one launch (start us, length us, event | category | flops | bytes accessed | tf_op | source)
XLA Modules:
  0.0 428.5 jit_solution(7431660078377562751)
XLA Ops:
  7.3 0.7 all-gather.5.cloned.1.call-update
  7.9 0.8 fusion.88
  8.9 0.7 reduce.1
  10.3 2.9 scatter_custom_fusion
  13.2 0.8 all_to_all.13
  14.0 18.4 %all-to-all-start = ((s32[128,1,5]{2,1,0:T(1,128)}), s32[128,1,5]{2,1,0:T(1,128)S(1)}, u32[]{:S(2)}, u32[]{:S(2)}) async-start(s32[128,1,5]{2,1,0:T(1,128)} %bitcast.4), calls=%async_computation | async-start | bytes 131072 | tf_op jit(solution)/shard_map/all_to_all | solution.py:220
  32.7 0.5 all-gather.3.cloned.1.call-update
  33.3 0.3 convolution_convert_fusion.6
  33.6 0.3 convolution_convert_fusion.4
  33.9 0.3 reshape.268
  34.3 0.3 convolution_convert_fusion.3
  34.6 0.3 reshape.269
  34.9 0.3 convolution_convert_fusion.5
  35.3 0.3 reshape.267
  35.6 1.8 fusion.89
  37.3 1.7 fusion.20
  39.1 0.2 copy.83
  39.4 0.4 reshape.270
  39.8 0.4 fusion.90
  40.2 0.2 multiply_reduce_fusion.5
  40.5 0.4 convolution_convert_fusion.2
  40.9 0.3 reshape.271
  41.2 0.5 copy.102
  41.7 0.6 fusion.40
  42.3 2.1 fusion.91
  44.4 0.5 copy.103
  44.9 2.0 fusion.30
  46.9 0.4 copy.90
  47.4 0.4 reshape.274
  48.0 0.4 fusion.92
  48.4 0.2 multiply_reduce_fusion.4
  48.7 2.0 scatter_custom_fusion.2
  50.7 1.2 reshape.277
  51.9 13.7 %all-to-all-start.2 = ((bf16[128,5,512]{2,1,0:T(8,128)(2,1)}), bf16[128,5,512]{2,1,0:T(8,128)(2,1)S(1)}, u32[]{:S(2)}, u32[]{:S(2)}) async-start(bf16[128,5,512]{2,1,0:T(8,128)(2,1)} %reshape.277), calls=%async_computation.2 | async-start | bytes 2097152 | tf_op jit(solution)/shard_map/all_to_all | solution.py:219
  65.7 0.5 broadcast.300
  66.2 0.8 reduce.15
  67.2 29.3 %all-to-all-done.2 = bf16[128,5,512]{2,1,0:T(8,128)(2,1)S(1)} async-done(((bf16[128,5,512]{2,1,0:T(8,128)(2,1)}), bf16[128,5,512]{2,1,0:T(8,128)(2,1)S(1)}, u32[]{:S(2)}, u32[]{:S(2)}) %all-to-all-start.2) | async-done | bytes 655392 | tf_op jit(solution)/shard_map/all_to_all | solution.py:219
  96.5 0.3 reshape.278
  96.8 1.1 copy.92
  97.9 2.8 fusion.95
  100.7 0.2 multiply_reduce_fusion.3
  101.0 0.6 fusion.96
  102.4 2.9 scatter_custom_fusion.1
  105.3 0.9 convert_element_type.128
  106.2 6.5 %all-to-all-start.1 = ((bf16[128,1,5]{2,1,0:T(2,128)(2,1)}), bf16[128,1,5]{2,1,0:T(2,128)(2,1)S(1)}, u32[]{:S(2)}, u32[]{:S(2)}) async-start(bf16[128,1,5]{2,1,0:T(2,128)(2,1)} %convert_element_type.128), calls=%async_computation.1 | async-start | bytes 131072 | tf_op jit(solution)/shard_map/all_to_all | solution.py:221
  112.8 0.8 fusion.105
  113.8 0.3 copy-done.21
  114.2 1.4 fusion.93
  115.9 0.7 fusion.94
  116.7 7.4 %all-to-all-done.1 = bf16[128,1,5]{2,1,0:T(2,128)(2,1)S(1)} async-done(((bf16[128,1,5]{2,1,0:T(2,128)(2,1)}), bf16[128,1,5]{2,1,0:T(2,128)(2,1)S(1)}, u32[]{:S(2)}, u32[]{:S(2)}) %all-to-all-start.1) | async-done | bytes 1312 | tf_op jit(solution)/shard_map/all_to_all | solution.py:221
  124.1 0.7 convert_reduce_fusion
  125.5 0.4 negate_reduce_fusion
  126.2 0.9 multiply_reduce_fusion.1
  127.1 0.3 fusion.57
  127.4 0.3 add_convert_fusion
  127.8 0.8 copy-done.5
  128.6 0.8 copy-done.2
  129.4 1.2 fusion.87
  130.6 6.3 %fusion.18 = f32[1024,512]{0,1:T(8,128)} fusion(bf16[640,512]{1,0:T(8,128)(2,1)S(1)} %reshape.278, f32[640,1024]{1,0:T(8,128)} %copy-done.1, bf16[640,512]{0,1:T(8,128)(2,1)} %copy-done.5, bf16[1024,512]{1,0:T(8,128)(2,1)} %all-gather.5.cloned.1.call-done), kind=kOutput, calls=%fused_computation.36 | convolution fusion | flops 1355284480 | bytes 7077888 | tf_op jit(solution)/shard_map/dot_general | solution.py:145
  136.9 4.0 pad_maximum_fusion
  141.2 0.6 reshape_multiply_fusion
  141.8 278.1 %all-reduce.4.cloned.1.call-done = f32[1024,1024]{0,1:T(8,128)} async-done(((f32[1024,1024]{0,1:T(8,128)}), f32[1024,1024]{0,1:T(8,128)}) %all-reduce.4.cloned.1.call-update) | async-done | bytes 4194320
  419.9 1.2 constant_dynamic-slice_fusion
  421.3 0.6 multiply_add_fusion
  (96 shorter events, 3.6 us)
Async XLA Ops:
  7.2 32.6 %copy-start = (bf16[512,512]{1,0:T(8,128)(2,1)S(1)}, bf16[512,512]{1,0:T(8,128)(2,1)}, u32[]{:S(2)}) copy-start(bf16[512,512]{1,0:T(8,128)(2,1)} %param.28) | copy-start | bytes 1572868
  7.2 3.0 copy-start.19
  7.2 26.1 %copy-start.15 = (bf16[28,512]{1,0:T(8,128)(2,1)S(1)}, bf16[28,512]{1,0:T(8,128)(2,1)}, u32[]{:S(2)}) copy-start(bf16[28,512]{1,0:T(8,128)(2,1)} %param.24) | copy-start | bytes 86020
  7.2 26.4 %copy-start.6 = (bf16[512,512]{1,0:T(8,128)(2,1)S(1)}, bf16[512,512]{1,0:T(8,128)(2,1)}, u32[]{:S(2)}) copy-start(bf16[512,512]{1,0:T(8,128)(2,1)} %param.25) | copy-start | bytes 1572868
  7.2 90.7 %all-gather.5.cloned.1.call-start = ((), (), s32[]{:S(2)}) async-start(), calls=%async_computation.4 | async-start | bytes 1310720 | tf_op jit(solution)/shard_map/all_gather | solution.py:177
  9.9 24.4 %copy-start.7 = (bf16[512,512]{1,0:T(8,128)(2,1)S(1)}, bf16[512,512]{1,0:T(8,128)(2,1)}, u32[]{:S(2)}) copy-start(bf16[512,512]{1,0:T(8,128)(2,1)} %param.26) | copy-start | bytes 1572868
  14.0 37.9 %all-to-all-start = ((s32[128,1,5]{2,1,0:T(1,128)}), s32[128,1,5]{2,1,0:T(1,128)S(1)}, u32[]{:S(2)}, u32[]{:S(2)}) async-start(s32[128,1,5]{2,1,0:T(1,128)} %bitcast.4), calls=%async_computation | async-start | bytes 131072 | tf_op jit(solution)/shard_map/all_to_all | solution.py:220
  32.4 65.5 %all-gather.3.cloned.1.call-start = ((), (), s32[]{:S(2)}) async-start(), calls=%async_computation.3 | async-start | bytes 1310720 | tf_op jit(solution)/shard_map/all_gather | solution.py:176
  33.6 1.3 copy-start.8
  39.1 1.4 copy-start.9
  39.1 1.4 copy-start.18
  39.8 1.4 copy-start.11
  42.3 2.1 copy-start.12
  46.9 1.0 copy-start.10
  47.4 1.3 copy-start.20
  50.6 15.0 %copy-start.22 = (s32[2]{0:T(128)S(1)}, s32[2]{0:T(128)}, u32[]{:S(2)}) copy-start(s32[2]{0:T(128)} %param.20) | copy-start | bytes 28
  51.9 44.6 %all-to-all-start.2 = ((bf16[128,5,512]{2,1,0:T(8,128)(2,1)}), bf16[128,5,512]{2,1,0:T(8,128)(2,1)S(1)}, u32[]{:S(2)}, u32[]{:S(2)}) async-start(bf16[128,5,512]{2,1,0:T(8,128)(2,1)} %reshape.277), calls=%async_computation.2 | async-start | bytes 2097152 | tf_op jit(solution)/shard_map/all_to_all | solution.py:219
  97.9 3.1 copy-start.13
  97.9 3.1 copy-start.16
  97.9 14.8 %copy-start.3 = (bf16[512,1024]{1,0:T(8,128)(2,1)S(1)}, bf16[512,1024]{1,0:T(8,128)(2,1)}, u32[]{:S(2)}) copy-start(bf16[512,1024]{1,0:T(8,128)(2,1)} %all-gather.3.cloned.1.call-done) | copy-start | bytes 3145732
  106.2 17.9 %all-to-all-start.1 = ((bf16[128,1,5]{2,1,0:T(2,128)(2,1)}), bf16[128,1,5]{2,1,0:T(2,128)(2,1)S(1)}, u32[]{:S(2)}, u32[]{:S(2)}) async-start(bf16[128,1,5]{2,1,0:T(2,128)(2,1)} %convert_element_type.128), calls=%async_computation.1 | async-start | bytes 131072 | tf_op jit(solution)/shard_map/all_to_all | solution.py:221
  112.7 307.2 %all-reduce.4.cloned.1.call-start = ((), (), s32[]{:S(2)}) async-start(), calls=%async_computation.5 | async-start | bytes 8388608
  112.7 1.1 copy-start.4
  112.7 1.4 copy-start.21
  114.2 1.5 copy-start.1
  114.2 1.7 copy-start.14
  127.4 2.0 copy-start.2
  127.8 0.9 copy-start.5
  141.0 280.3 %copy-start.17 = (f32[2,1024]{1,0:T(2,128)S(1)}, f32[2,1024]{1,0:T(2,128)}, u32[]{:S(2)}) copy-start(f32[2,1024]{1,0:T(2,128)} %param.37) | copy-start | bytes 24580
Sparse Core Ops, SparseCore 0:
  10.1 33.8 all-gather.4
  46.1 31.5 all-gather.2
  141.1 278.7 all-reduce.3
where the time goes:
time: 430 us; the launch traced here: 428 us
  waiting for transfers between devices  316 us (73%)
  starting transfers between devices  38.9 us (9%)
  matrix products  23.4 us (5%)
  local copies, waits for them, and re-layouts  20.2 us (5%)
  between operations  15.1 us (4%)
  other arithmetic  14.8 us (3%)
    unnamed x4, waiting for transfers between devices  279 us
    all_to_all x1, waiting for transfers between devices, per_device(): lax.all_to_all(send_states, 'dp', split_axis=0, concat_axis=0, tiled=True)  29.3 us
    all_to_all x1, starting transfers between devices, per_device(): lax.all_to_all(send_labels, 'dp', split_axis=0, concat_axis=0, tiled=True)  18.4 us
    all_to_all x1, starting transfers between devices, per_device(): lax.all_to_all(send_states, 'dp', split_axis=0, concat_axis=0, tiled=True)  13.7 us
  transfers between devices with their start and end apart: 6, of which 3 were waited for; matrix products, arithmetic and copies ran while one was open for 7% of the time, Pallas kernels for 0%

commit v1 on v0

v1 whole, which is shorter than its diff:
```python
import jax
import jax.numpy as jnp
import numpy as np
from jax import lax
from jax.sharding import Mesh
from jax.sharding import PartitionSpec as P

HEADS = 8
CAP = 5
f32 = jnp.float32
bf16 = jnp.bfloat16


def mm(a, b):
    return jnp.dot(a, b, preferred_element_type=f32)


def layer_norm(values, gain):
    mean = jnp.mean(values, -1, keepdims=True)
    centered = values - mean
    variance = jnp.mean(centered * centered, -1, keepdims=True)
    return centered * lax.rsqrt(variance + 1e-05) * gain


def split(v):
    high = v.astype(bf16)
    return high, (v - high.astype(f32)).astype(bf16)


def attend(tokens, keys, values, embed, w_query, w_key, w_value, w_self, cross_query, cross_out, gain_self, gain_cross):
    spec, beam, plus = tokens.shape
    steps = plus - 1
    rows = spec * beam * steps
    width = embed.shape[1]
    vocab = embed.shape[0]
    size = width // HEADS
    peaks = keys.shape[1]
    inputs = tokens[:, :, :steps].reshape(rows)
    picks = (inputs[:, None] == jnp.arange(vocab, dtype=jnp.int32)[None, :]).astype(bf16)
    embedded = mm(picks, embed).astype(bf16)
    query = mm(embedded, w_query).astype(bf16).reshape(spec * beam, steps, HEADS, size)
    keyed = mm(embedded, w_key).astype(bf16).reshape(spec * beam, steps, HEADS, size)
    valued = mm(embedded, w_value).astype(bf16).reshape(spec * beam, steps, HEADS, size)
    scores = jnp.einsum("nqhd,nkhd->nhqk", query, keyed, preferred_element_type=f32) / jnp.sqrt(f32(size))
    causal = jnp.arange(steps)[:, None] >= jnp.arange(steps)[None, :]
    scores = jnp.where(causal[None, None], scores, -1e30)
    probs = jax.nn.softmax(scores, -1).astype(bf16)
    context = (
        jnp.einsum("nhqk,nkhd->nqhd", probs, valued, preferred_element_type=f32).astype(bf16).reshape(rows, width)
    )
    attended = layer_norm(embedded.astype(f32) + mm(context, w_self), gain_self).astype(bf16)
    cross_q = mm(attended, cross_query).astype(bf16).reshape(spec, beam * steps, HEADS, size)
    mem_k = keys.reshape(spec, peaks, HEADS, size)
    mem_v = values.reshape(spec, peaks, HEADS, size)
    cross_s = jnp.einsum("sqhd,skhd->shqk", cross_q, mem_k, preferred_element_type=f32) / jnp.sqrt(f32(size))
    cross_p = jax.nn.softmax(cross_s, -1).astype(bf16)
    cross_c = jnp.einsum("shqk,skhd->sqhd", cross_p, mem_v, preferred_element_type=f32).astype(bf16).reshape(rows, width)
    return layer_norm(attended.astype(f32) + mm(cross_c, cross_out), gain_cross).astype(bf16)


def gather_weights(w_in, w_down):
    depth, part = w_in.shape
    mine_in = w_in.reshape(2, part, part)
    mine_down = jnp.stack([w_down[:, :part], w_down[:, part:]])
    core = lax.axis_index("core")
    first = core == 0
    mine = jnp.where(first, mine_in, mine_down)
    n_x = lax.axis_size("x")
    got = lax.all_to_all(jnp.broadcast_to(mine[None], (n_x,) + mine.shape), "x", 0, 0)
    other = lax.ppermute(got, "core", [(0, 1), (1, 0)])
    all_in = jnp.where(first, got, other)
    all_down = jnp.where(first, other, got)
    all_in = all_in.transpose(1, 2, 0, 3).reshape(depth, n_x * part)
    all_down = all_down.transpose(0, 2, 1, 3).reshape(n_x * part, depth)
    return all_in, all_down


def scatter_sum(term):
    units, cols = term.shape
    n_x = lax.axis_size("x")
    core = lax.axis_index("core")
    pairs = units // (2 * n_x * 2)
    term = term.astype(bf16).reshape(pairs, 2, n_x * 2, cols)
    keep = lax.dynamic_index_in_dim(term, core, 1, False)
    send = lax.dynamic_index_in_dim(term, 1 - core, 1, False)
    other = lax.ppermute(send, "core", [(0, 1), (1, 0)])
    both = (keep.astype(f32) + other.astype(f32)).astype(bf16)
    both = both.reshape(pairs, n_x, 2, cols).transpose(1, 2, 0, 3)
    got = lax.all_to_all(both, "x", 0, 0)
    mine = jnp.sum(got.astype(f32), 0).astype(bf16)
    mine = mine.transpose(1, 0, 2).reshape(pairs, 16, 128)
    got = lax.all_to_all(mine, ("z", "y"), 0, 0)
    return jnp.sum(got.astype(f32), 0).reshape(2, cols)


def per_device(
    tokens, accept, dest, mem_keys, mem_values, embed, w_query, w_key, w_value, w_self, cross_query, cross_out,
    gain_self, gain_cross, w_in, w_down, gain_ff, head, momentum,
):
    spec, beam, plus = tokens.shape
    steps = plus - 1
    rows = spec * beam * steps
    vocab, width = embed.shape
    dp = ("z", "y", "core")
    n_dp = lax.axis_size(dp)

    w_in_all, w_down_all = gather_weights(w_in, w_down)
    states = attend(
        tokens, mem_keys, mem_values, embed, w_query, w_key, w_value, w_self, cross_query, cross_out, gain_self, gain_cross
    )
    labels = tokens[:, :, 1:].reshape(rows)

    pre = mm(states, w_in_all)
    inner = 0.7978845608028654 * (pre + 0.044715 * pre * pre * pre)
    tanh = jnp.tanh(inner)
    hidden = (0.5 * pre * (1.0 + tanh)).astype(bf16)
    slope = 0.5 * (1.0 + tanh) + 0.5 * pre * (1.0 - tanh * tanh) * 0.7978845608028654 * (1.0 + 0.134145 * pre * pre)
    total = states.astype(f32) + mm(hidden, w_down_all)
    mean = jnp.mean(total, -1, keepdims=True)
    centered = total - mean
    scale = lax.rsqrt(jnp.mean(centered * centered, -1, keepdims=True) + 1e-05)
    unit = centered * scale
    high, low = split(unit * gain_ff)
    logits = mm(high, head) + mm(low, head)
    logp = jax.nn.log_softmax(logits, -1)
    is_label = (labels[:, None] == jnp.arange(vocab, dtype=jnp.int32)[None, :]).astype(f32)
    taken = jnp.sum(is_label * logp, -1)
    beam_weight = jax.nn.softmax(taken.reshape(spec, beam, steps).sum(-1) / steps, -1)
    weight = (accept.astype(f32)[:, None, None] * beam_weight[:, :, None] * jnp.ones((1, 1, steps), f32)).reshape(rows)

    target = dest[:, 0]
    hits = (target[:, None] == jnp.arange(n_dp, dtype=jnp.int32)[None, :])
    hits16 = hits.astype(bf16)
    earlier = jnp.asarray(np.tril(np.ones((rows, rows)), -1), bf16)
    rank = jnp.sum(mm(earlier, hits16) * hits.astype(f32), -1).astype(jnp.int32)
    sums = jnp.sum(hits.astype(f32) * weight[:, None], 0)
    loss = -weight * taken
    at_rank = (rank[:, None] == jnp.arange(128, dtype=jnp.int32)[None, :]).astype(f32)
    slots = lax.dot_general(
        hits.astype(f32) * loss[:, None], at_rank, (((0,), (0,)), ((), ())), precision=lax.Precision.HIGHEST
    )
    message = jnp.concatenate([jnp.broadcast_to(sums[None, :], (n_dp, n_dp)), slots], 1)
    got = lax.all_to_all(message[:, None, :], dp, 0, 0)[:, 0]
    slot_loss = got[:, n_dp : n_dp + CAP].reshape(1, n_dp * CAP)
    inverse = 1.0 / jnp.maximum(jnp.sum(got[:, :n_dp], 0), 1.0)
    factor = jnp.sum(hits.astype(f32) * inverse[None, :], -1)

    high, low = split(weight[:, None] * (jnp.exp(logp) - is_label))
    flip = (((1,), (1,)), ((), ()))
    d_unit = gain_ff * (
        lax.dot_general(high, head, flip, preferred_element_type=f32)
        + lax.dot_general(low, head, flip, preferred_element_type=f32)
    )
    d_total = scale * (
        d_unit - jnp.mean(d_unit, -1, keepdims=True) - unit * jnp.mean(d_unit * unit, -1, keepdims=True)
    )
    d_hidden = lax.dot_general(d_total.astype(bf16), w_down_all, flip, preferred_element_type=f32)
    d_pre = (slope * d_hidden * factor[:, None]).astype(bf16)
    d_out = (d_total * factor[:, None]).astype(bf16)
    tall = (((0,), (0,)), ((), ()))
    grad_in = lax.dot_general(d_pre, states, tall, preferred_element_type=f32)
    grad_down = lax.dot_general(hidden, d_out, tall, preferred_element_type=f32)
    share = scatter_sum(jnp.concatenate([grad_in, grad_down], 1))
    return (0.9 * momentum + share, slot_loss)


def solution(mesh):
    n_dp, n_mp = mesh.devices.shape
    side = int(np.sqrt(n_dp // 2))
    fine = Mesh(mesh.devices.reshape(side, side, 2, n_mp), ("z", "y", "core", "x"))
    every = ("z", "y", "core", "x")
    placed = (
        P(every, None, None),
        P(every),
        P(every, None),
        P(every, None, None),
        P(every, None, None),
        P(),
        P(),
        P(),
        P(),
        P(),
        P(),
        P(),
        P(),
        P(),
        P(None, "x"),
        P("x", None),
        P(),
        P(),
        P(every, None),
    )
    return jax.shard_map(
        per_device,
        mesh=fine,
        in_specs=placed,
        out_specs=(P(every, None), P(every, None)),
        check_vma=False,
    )
```

time: 430 us -> 135 us (0.31)
  waiting for transfers between devices: 316 us -> 25.9 us
  blocking collectives: 0 us -> 18.6 us
  between operations: 15.1 us -> 1.2 us
  starting transfers between devices: 38.9 us -> 32.9 us
    unnamed x4 -> x0, waiting for transfers between devices: 279 us -> none
    all_to_all x0 -> x1, blocking collectives: none -> 18.6 us  [scatter_sum(): got = lax.all_to_all(both, 'x', 0, 0)]
    all_to_all x3, starting transfers between devices: 38.6 us -> 22 us  [the longest x1 12.4 us: per_device(): got = lax.all_to_all(message[:, None, :], dp, 0, 0)[:, 0]]
    all_to_all x3, waiting for transfers between devices: 36.8 us -> 23.3 us  [the longest x1 11.7 us: scatter_sum(): got = lax.all_to_all(mine, ('z', 'y'), 0, 0)]
    ppermute x0 -> x2, starting transfers between devices: none -> 10.9 us  [the longest x1 8.6 us: gather_weights(): other = lax.ppermute(got, 'core', [(0, 1), (1, 0)])]
    scatter x2 -> x0, local copies, waits for them, and re-layouts: 5.85 us -> none  [the longest x1 2.93 us: per_device(): jnp.zeros((n_dp * capacity,), jnp.float32).at[position].set(weight)]
    dot_general x18 -> x20, matrix products: 21.6 us -> 22 us  [the longest x12 7.74 us: mm(): return jnp.dot(a, b, preferred_element_type=f32)]
  transfers between devices with their start and end apart: 6 -> 5, of which waited for: 3 -> 3; matrix products, arithmetic and copies ran while one was open for 7% -> 18% of each run, Pallas kernels for 0% -> 0%
where the time goes in v1:
time: 135 us; the launch traced here: 133 us
  starting transfers between devices  32.9 us (24%)
  waiting for transfers between devices  25.9 us (19%)
  matrix products  23.7 us (18%)
  local copies, waits for them, and re-layouts  19.7 us (15%)
  blocking collectives  18.6 us (14%)
  other arithmetic  10.6 us (8%)
    all_to_all x1, blocking collectives, scatter_sum(): got = lax.all_to_all(both, 'x', 0, 0)  18.6 us
    all_to_all x1, starting transfers between devices, per_device(): got = lax.all_to_all(message[:, None, :], dp, 0, 0)[:, 0]  12.4 us
    all_to_all x1, waiting for transfers between devices, scatter_sum(): got = lax.all_to_all(mine, ('z', 'y'), 0, 0)  11.7 us
    all_to_all x1, waiting for transfers between devices, per_device(): got = lax.all_to_all(message[:, None, :], dp, 0, 0)[:, 0]  11.6 us
    ppermute x1, starting transfers between devices, gather_weights(): other = lax.ppermute(got, 'core', [(0, 1), (1, 0)])  8.6 us
    dot_general x12, matrix products, mm(): return jnp.dot(a, b, preferred_element_type=f32)  7.74 us
    all_to_all x1, starting transfers between devices, gather_weights(): lax.all_to_all(jnp.broadcast_to(mine[None], (n_x,) + mine.shape), 'x', 0, 0)  4.97 us
    all_to_all x1, starting transfers between devices, scatter_sum(): got = lax.all_to_all(mine, ('z', 'y'), 0, 0)  4.62 us
  transfers between devices with their start and end apart: 5, of which 3 were waited for; matrix products, arithmetic and copies ran while one was open for 18% of the time, Pallas kernels for 0%

profile of v1, /device:TPU:1, one launch (start us, length us, event | category | flops | bytes accessed | tf_op | source)
XLA Modules:
  0.0 132.6 jit_solution(7911104168651179845)
XLA Ops:
  0.6 1.0 slice_bitcast_fusion.1
  1.8 0.3 copy.77
  2.0 1.5 %broadcast_in_dim.22 = bf16[4,2,256,256]{3,1,2,0:T(2,128)(2,1)} broadcast(bf16[2,256,256]{2,0,1:T(2,128)(2,1)S(1)} %copy.77), dimensions={1,2,3} | broadcast | bytes 1310720 | tf_op jit(solution)/shard_map/broadcast_in_dim | solution.py:69
  3.6 5.0 %all-to-all-start = ((bf16[4,2,256,256]{3,1,2,0:T(2,128)(2,1)}), bf16[4,2,256,256]{3,1,2,0:T(2,128)(2,1)S(1)}, u32[]{:S(2)}, u32[]{:S(2)}) async-start(bf16[4,2,256,256]{3,1,2,0:T(2,128)(2,1)} %broadcast_in_dim.22), calls=%async_computation | async-start | bytes 2097152 | tf_op jit(solution)/shard_map/all_to_all | solution.py:69
  8.7 0.3 convolution_convert_fusion.8
  9.0 0.3 convolution_convert_fusion.6
  9.4 0.3 reshape.225
  9.7 0.3 convolution_convert_fusion.5
  10.0 0.3 reshape.226
  10.3 1.4 %convolution_convert_fusion.7 = bf16[300,512]{1,0:T(8,128)(2,1)S(1)} fusion(bf16[300,512]{1,0:T(8,128)(2,1)S(1)} %convolution_convert_fusion.8, bf16[512,512]{1,0:T(8,128)(2,1)} %param.28), kind=kOutput, calls=%fused_computation.46 | convolution fusion | flops 157440000 | bytes 1138688 | tf_op jit(solution)/shard_map/dot_general | solution.py:15
  11.7 1.2 reshape.224
  12.9 1.8 %fusion.79 = (f32[10,8,30]{2,1,0:T(8,128)S(1)}, f32[10,8,30,30]{2,3,1,0:T(8,128)}) fusion(bf16[10,30,8,64]{3,2,1,0:T(8,128)(2,1)S(1)} %reshape.226, bf16[10,30,8,64]{3,2,1,0:T(8,128)(2,1)S(1)} %reshape.225, pred[30,30]{0,1:T(8,128)(4,1)S(1)} %iota_compare_fusion.8), kind=kOutput, calls=%fused_computation.145 | convolution fusion | flops 9504029 | bytes 912900 | tf_op jit(solution)/shard_map/sub | solution.py:47
  14.6 1.9 %fusion.11 = bf16[10,30,8,64]{3,1,2,0:T(8,128)(2,1)S(1)} fusion(f32[10,8,30,30]{2,3,1,0:T(8,128)} %get-tuple-element.11, bf16[10,30,8,64]{3,2,1,0:T(8,128)(2,1)} %reshape.224, f32[10,8,30]{2,1,0:T(8,128)S(1)} %get-tuple-element.10), kind=kOutput, calls=%fused_computation.24 | convolution fusion | flops 9513600 | bytes 912000 | tf_op jit(solution)/shard_map/nhqk,nkhd->nqhd/dot_general | solution.py:49
  16.6 0.2 copy.69
  16.8 0.4 reshape.227
  17.2 0.4 fusion.80
  17.7 0.2 multiply_reduce_fusion.4
  17.9 0.3 copy-done.7
  18.3 0.4 convolution_convert_fusion.4
  18.6 0.3 reshape.228
  19.0 1.3 copy.90
  20.2 2.0 %copy.91 = bf16[2,150,512]{1,2,0:T(8,128)(2,1)} copy(bf16[2,150,512]{2,0,1:T(2,128)(2,1)} %param.24) | data formatting | bytes 614400 | tf_op jit(solution)/shard_map/reshape | solution.py:54
  22.2 0.5 fusion.35
  22.8 2.1 %fusion.81 = (f32[2,8,150]{2,1,0:T(8,128)S(1)}, f32[2,8,150,150]{2,3,1,0:T(8,128)}) fusion(f32[2,8,150,150]{2,3,1,0:T(8,128)S(1)} %fusion.35), kind=kOutput, calls=%fused_computation.147 | output fusion | flops 1440149 | bytes 2889600 | tf_op jit(solution)/shard_map/sub | solution.py:56
  24.9 8.6 %collective-permute-start = (bf16[4,2,256,256]{3,1,2,0:T(2,128)(2,1)S(1)}, bf16[4,2,256,256]{3,1,2,0:T(2,128)(2,1)}, u32[]{:S(2)}, u32[]{:S(2)}) collective-permute-start(bf16[4,2,256,256]{3,1,2,0:T(2,128)(2,1)S(1)} %all-to-all-done), channel_id=1, source_target_pairs={{0,4},{4,0},{1,5},{5,1},{2,6},{6,2},{3,7},{7,3},{8,12},{12,8},{9,1... | collective-permute-start | bytes 3145736 | tf_op jit(solution)/shard_map/ppermute | solution.py:70
  33.5 2.0 %fusion.25 = bf16[2,150,8,64]{1,3,2,0:T(8,128)(2,1)S(1)} fusion(bf16[2,150,8,64]{1,3,2,0:T(8,128)(2,1)S(1)} %bitcast.72, f32[2,8,150,150]{2,3,1,0:T(8,128)} %get-tuple-element.15, f32[2,8,150]{2,1,0:T(8,128)S(1)} %get-tuple-element.14), kind=kOutput, calls=%fused_computation.42 | convolution fusion | flops 46953600 | bytes 2064000 | tf_op jit(solution)/shard_map/shqk,skhd->sqhd/dot_general | solution.py:57
  35.5 0.4 copy.76
  36.0 0.4 reshape.231
  36.5 1.4 %fusion.29 = f32[300]{0:T(512)S(1)} fusion(bf16[300,300]{1,0:T(8,128)(2,1)} %constant.76.clone, s32[300]{0:T(512)S(1)} %reduce.1), kind=kOutput, calls=%fused_computation.51 | convolution fusion | flops 23193300 | bytes 182400 | tf_op jit(solution)/shard_map/dot_general | solution.py:15
  37.9 1.5 %fusion.82 = (f32[300]{0:T(512)S(1)}, f32[300,512]{1,0:T(8,128)S(1)}) fusion(bf16[300,512]{1,0:T(8,128)(2,1)S(1)} %reshape.231, bf16[512,512]{1,0:T(8,128)(2,1)} %param.31, f32[512]{0:T(512)S(1)} %copy-done.14, f32[300]{0:T(512)S(1)} %add_rsqrt_fusion.2, f32[300,512]{1,0:T(8,128)S(1)} %get-tuple-element.13, f32[300]{0:T(512)S(1)} %broadcast_multiply_fusion.4), kind=kOutput, calls=%fused_computation.148 | convolution fusion | flops 158361296 | bytes 2065936 | tf_op jit(solution)/shard_map/dot_general | solution.py:15
  39.4 0.2 multiply_reduce_fusion.3
  39.6 2.8 %fusion.30 = (bf16[2,256,4,256]{3,0,1,2:T(2,128)(2,1)S(1)}, bf16[4,2,256,256]{3,1,2,0:T(2,128)(2,1)S(1)}) fusion(bf16[4,2,256,256]{3,1,2,0:T(2,128)(2,1)S(1)} %all-to-all-done, bf16[4,2,256,256]{3,1,2,0:T(2,128)(2,1)} %collective-permute-done, pred[]{:T(512)S(6)} %eq.65), kind=kLoop, calls=%fused_computation.53 | loop fusion | flops 1048576 | bytes 4194305 | tf_op jit(solution)/shard_map/transpose | solution.py:73
  42.5 0.8 copy.78
  43.5 0.2 copy.94
  43.8 0.4 copy-done.15
  44.2 0.5 fusion.89
  44.8 0.7 fusion.83
  45.5 0.3 copy-done.1
  45.8 0.2 multiply_reduce_fusion.2
  46.1 0.3 fusion.43
  46.3 0.3 fusion.84
  47.5 0.3 fusion.67
  47.9 0.5 fusion.53
  48.6 0.8 copy.80
  49.3 12.4 %all-to-all-start.1 = ((f32[128,1,256]{2,1,0:T(1,128)}), f32[128,1,256]{2,1,0:T(1,128)S(1)}, u32[]{:S(2)}, u32[]{:S(2)}) async-start(f32[128,1,256]{2,1,0:T(1,128)} %copy.80), calls=%async_computation.1 | async-start | bytes 262144 | tf_op jit(solution)/shard_map/all_to_all | solution.py:143
  61.7 1.2 fusion.77
  62.9 11.6 %all-to-all-done.1 = f32[128,1,256]{2,1,0:T(1,128)S(1)} async-done(((f32[128,1,256]{2,1,0:T(1,128)}), f32[128,1,256]{2,1,0:T(1,128)S(1)}, u32[]{:S(2)}, u32[]{:S(2)}) %all-to-all-start.1) | async-done | bytes 131104 | tf_op jit(solution)/shard_map/all_to_all | solution.py:143
  74.5 0.2 select_reduce_fusion
  74.8 3.6 %convolution_convert_fusion = bf16[1024,512]{1,0:T(8,128)(2,1)} fusion(f32[300]{0:T(512)S(1)} %select_reduce_fusion, f32[300,1024]{1,0:T(8,128)} %copy-done.1, f32[300,512]{1,0:T(8,128)} %get-tuple-element.22, f32[300,512]{1,0:T(8,128)S(1)} %get-tuple-element.19, f32[300]{0:T(512)S(1)} %get-tuple-element.23, f32[300]{0:T(512)S(1)} %get-tuple-element.24, ...), kind=kOutput, calls=%fused_computation.13 | convolution fusion | flops 319090688 | bytes 3512176 | tf_op jit(solution)/shard_map/dot_general | solution.py:162
  78.4 4.2 %convolution_convert_fusion.1 = bf16[1024,512]{1,0:T(8,128)(2,1)} fusion(bf16[1024,512]{1,0:T(8,128)(2,1)} %bitcast.69, f32[300,1024]{1,0:T(8,128)S(1)} %copy-done.2, f32[300]{0:T(512)S(1)} %select_reduce_fusion, f32[300,512]{1,0:T(8,128)} %get-tuple-element.22, f32[300,512]{1,0:T(8,128)S(1)} %get-tuple-element.19, f32[300]{0:T(512)S(1)} %get-tuple-element.23, ...), kind=kOutput, calls=%fused_computation.14 | convolution fusion | flops 637503488 | bytes 5179600 | tf_op jit(solution)/shard_map/dot_general | solution.py:161
  82.6 1.9 %copy_dynamic-update-slice_fusion.1 = bf16[64,2,8,1024]{3,0,2,1:T(8,128)(2,1)S(1)} fusion(bf16[64,2,8,512]{3,2,1,0:T(8,128)(2,1)} %bitcast.71), kind=kLoop, calls=%fused_computation.55 | loop fusion | bytes 2097152
  84.5 0.6 copy_dynamic-update-slice_fusion
  85.1 1.1 dynamic-slice_bitcast_fusion
  86.2 2.3 %collective-permute-start.1 = (bf16[64,8,1024]{2,0,1:T(8,128)(2,1)}, bf16[64,8,1024]{2,0,1:T(8,128)(2,1)}, u32[]{:S(2)}, u32[]{:S(2)}) collective-permute-start(bf16[64,8,1024]{2,0,1:T(8,128)(2,1)} %dynamic-slice_bitcast_fusion), channel_id=1, source_target_pairs={{0,4},{4,0},{1,5},{5,1},{2,6},{6,2},{3,7},{7,3},{8,12},{12,8},{9,1... | collective-permute-start | bytes 3145736 | tf_op jit(solution)/shard_map/ppermute | solution.py:86
  88.5 2.6 %collective-permute-done.1 = bf16[64,8,1024]{2,0,1:T(8,128)(2,1)} collective-permute-done((bf16[64,8,1024]{2,0,1:T(8,128)(2,1)}, bf16[64,8,1024]{2,0,1:T(8,128)(2,1)}, u32[]{:S(2)}, u32[]{:S(2)}) %collective-permute-start.1) | collective-permute-done | bytes 1048608 | tf_op jit(solution)/shard_map/ppermute | solution.py:86
  91.1 1.6 %fusion.5 = bf16[64,8,1024]{2,0,1:T(8,128)(2,1)S(1)} fusion(bf16[64,8,1024]{2,0,1:T(8,128)(2,1)} %collective-permute-done.1, bf16[64,2,8,1024]{3,0,2,1:T(8,128)(2,1)S(1)} %copy_dynamic-update-slice_fusion, s32[]{:T(128)S(6)} %select_n.41), kind=kLoop, calls=%fused_computation.7 | loop fusion | flops 2097152 | bytes 3145732 | tf_op jit(solution)/shard_map/convert_element_type | solution.py:87
  92.7 1.1 copy.83
  93.8 18.6 %all_to_all.20 = bf16[4,2,64,1024]{3,1,2,0:T(2,128)(2,1)S(1)} all-to-all(bf16[4,2,64,1024]{3,1,2,0:T(2,128)(2,1)S(1)} %copy.83), channel_id=1, replica_groups=mesh['z'=8,'y'=8,'core'=2,'x'=4] {'x'}, dimensions={0} | all-to-all | bytes 2097152 | tf_op jit(solution)/shard_map/all_to_all | solution.py:89
  112.4 1.5 %reduce_sum.202 = bf16[2,64,1024]{2,0,1:T(2,128)(2,1)S(1)} reduce(bf16[4,2,64,1024]{3,1,2,0:T(2,128)(2,1)S(1)} %all_to_all.20, bf16[]{:T(256)} %constant.75.clone.1), dimensions={0}, to_apply=%region_22.23 | reduce | flops 393216 | bytes 1310722 | tf_op jit(solution)/shard_map/reduce_sum | solution.py:90
  113.9 0.9 reshape.237
  114.7 4.6 %all-to-all-start.3 = ((bf16[64,16,128]{2,1,0:T(8,128)(2,1)}), bf16[64,16,128]{2,1,0:T(8,128)(2,1)S(1)}, u32[]{:S(2)}, u32[]{:S(2)}) async-start(bf16[64,16,128]{2,1,0:T(8,128)(2,1)} %reshape.237), calls=%async_computation.3 | async-start | bytes 524288 | tf_op jit(solution)/shard_map/all_to_all | solution.py:92
  119.4 0.8 reshape.239
  120.1 11.7 %all-to-all-done.3 = bf16[64,16,128]{2,1,0:T(8,128)(2,1)S(1)} async-done(((bf16[64,16,128]{2,1,0:T(8,128)(2,1)}), bf16[64,16,128]{2,1,0:T(8,128)(2,1)S(1)}, u32[]{:S(2)}, u32[]{:S(2)}) %all-to-all-start.3) | async-done | bytes 262176 | tf_op jit(solution)/shard_map/all_to_all | solution.py:92
  132.0 0.6 multiply_add_fusion.1
  (73 shorter events, 1.9 us)
Async XLA Ops:
  0.6 16.6 %copy-start = (bf16[512,512]{1,0:T(8,128)(2,1)S(1)}, bf16[512,512]{1,0:T(8,128)(2,1)}, u32[]{:S(2)}) copy-start(bf16[512,512]{1,0:T(8,128)(2,1)} %param.29) | copy-start | bytes 1572868
  3.6 5.0 %copy-start.11 = (s32[2,5,31]{2,0,1:T(2,128)S(1)}, s32[2,5,31]{2,0,1:T(2,128)}, u32[]{:S(2)}) copy-start(s32[2,5,31]{2,0,1:T(2,128)} %param.20) | copy-start | bytes 3724
  3.6 5.2 %copy-start.10 = (bf16[28,512]{1,0:T(8,128)(2,1)S(1)}, bf16[28,512]{1,0:T(8,128)(2,1)}, u32[]{:S(2)}) copy-start(bf16[28,512]{1,0:T(8,128)(2,1)} %param.25) | copy-start | bytes 86020
  3.6 5.5 %copy-start.5 = (bf16[512,512]{1,0:T(8,128)(2,1)S(1)}, bf16[512,512]{1,0:T(8,128)(2,1)}, u32[]{:S(2)}) copy-start(bf16[512,512]{1,0:T(8,128)(2,1)} %param.26) | copy-start | bytes 1572868
  3.6 21.3 %all-to-all-start = ((bf16[4,2,256,256]{3,1,2,0:T(2,128)(2,1)}), bf16[4,2,256,256]{3,1,2,0:T(2,128)(2,1)S(1)}, u32[]{:S(2)}, u32[]{:S(2)}) async-start(bf16[4,2,256,256]{3,1,2,0:T(2,128)(2,1)} %broadcast_in_dim.22), calls=%async_computation | async-start | bytes 2097152 | tf_op jit(solution)/shard_map/all_to_all | solution.py:69
  8.5 1.1 copy-start.6
  17.2 1.0 copy-start.7
  17.2 1.0 copy-start.14
  22.8 10.7 %copy-start.8 = (bf16[2,150,512]{1,2,0:T(8,128)(2,1)S(1)}, bf16[2,150,512]{1,2,0:T(8,128)(2,1)}, u32[]{:S(2)}) copy-start(bf16[2,150,512]{1,2,0:T(8,128)(2,1)} %copy.91) | copy-start | bytes 921604
  24.9 14.8 %collective-permute-start = (bf16[4,2,256,256]{3,1,2,0:T(2,128)(2,1)S(1)}, bf16[4,2,256,256]{3,1,2,0:T(2,128)(2,1)}, u32[]{:S(2)}, u32[]{:S(2)}) collective-permute-start(bf16[4,2,256,256]{3,1,2,0:T(2,128)(2,1)S(1)} %all-to-all-done), channel_id=1, source_target_pairs={{0,4},{4,0},{1,5},{5,1},{2,6},{6,2},{3,7},{7,3},{8,12},{12,8},{9,1... | collective-permute-start | bytes 3145736 | tf_op jit(solution)/shard_map/ppermute | solution.py:70
  35.5 1.0 copy-start.17
  35.5 1.0 copy-start.16
  43.5 0.7 copy-start.15
  43.8 1.0 copy-start.3
  44.8 1.0 copy-start.1
  44.8 1.3 copy-start.9
  44.8 1.3 copy-start.12
  49.3 25.2 %all-to-all-start.1 = ((f32[128,1,256]{2,1,0:T(1,128)}), f32[128,1,256]{2,1,0:T(1,128)S(1)}, u32[]{:S(2)}, u32[]{:S(2)}) async-start(f32[128,1,256]{2,1,0:T(1,128)} %copy.80), calls=%async_computation.1 | async-start | bytes 262144 | tf_op jit(solution)/shard_map/all_to_all | solution.py:143
  74.8 3.6 %copy-start.2 = (f32[300,1024]{1,0:T(8,128)S(1)}, f32[300,1024]{1,0:T(8,128)}, u32[]{:S(2)}) copy-start(f32[300,1024]{1,0:T(8,128)} %copy-done.1) | copy-start | bytes 3686404
  82.6 1.9 %copy-start.4 = (bf16[1024,512]{1,0:T(8,128)(2,1)S(1)}, bf16[1024,512]{1,0:T(8,128)(2,1)}, u32[]{:S(2)}) copy-start(bf16[1024,512]{1,0:T(8,128)(2,1)} %convolution_convert_fusion) | copy-start | bytes 3145732
  86.2 4.9 %collective-permute-start.1 = (bf16[64,8,1024]{2,0,1:T(8,128)(2,1)}, bf16[64,8,1024]{2,0,1:T(8,128)(2,1)}, u32[]{:S(2)}, u32[]{:S(2)}) collective-permute-start(bf16[64,8,1024]{2,0,1:T(8,128)(2,1)} %dynamic-slice_bitcast_fusion), channel_id=1, source_target_pairs={{0,4},{4,0},{1,5},{5,1},{2,6},{6,2},{3,7},{7,3},{8,12},{12,8},{9,1... | collective-permute-start | bytes 3145736 | tf_op jit(solution)/shard_map/ppermute | solution.py:86
  112.3 19.6 %copy-start.13 = (f32[2,1024]{1,0:T(2,128)S(1)}, f32[2,1024]{1,0:T(2,128)}, u32[]{:S(2)}) copy-start(f32[2,1024]{1,0:T(2,128)} %param.38) | copy-start | bytes 24580
  114.7 17.2 %all-to-all-start.3 = ((bf16[64,16,128]{2,1,0:T(8,128)(2,1)}), bf16[64,16,128]{2,1,0:T(8,128)(2,1)S(1)}, u32[]{:S(2)}, u32[]{:S(2)}) async-start(bf16[64,16,128]{2,1,0:T(8,128)(2,1)} %reshape.237), calls=%async_computation.3 | async-start | bytes 524288 | tf_op jit(solution)/shard_map/all_to_all | solution.py:92

commit v2 on v1

v2 whole, which is shorter than its diff:
```python
import functools

import jax
import jax.numpy as jnp
import numpy as np
from jax import lax
from jax.experimental import pallas as pl
from jax.experimental.pallas import tpu as pltpu
from jax.sharding import Mesh
from jax.sharding import PartitionSpec as P

HEADS = 8
BEAM = 5
STEPS = 30
CAP = 5
SEG = BEAM * (STEPS + 1)
PAD = 160
ROWS = 2 * PAD
WIDTH = 512
FF = 1024
VOCAB = 28
PEAKS = 150
LANES = 128
N_DP = 128
N_X = 4
PART = FF // N_X
HALF = FF // 2
PAY = 4 * WIDTH + LANES
f32 = jnp.float32
bf16 = jnp.bfloat16
FLIP = (((1,), (1,)), ((), ()))
TALL = (((0,), (0,)), ((), ()))
DP = ("z", "y", "core")
EVERY = ("z", "y", "core", "x")


def mm(a, b):
    return jnp.dot(a, b, preferred_element_type=f32)


def mm_flip(a, b):
    return lax.dot_general(a, b, FLIP, preferred_element_type=f32)


def mm_tall(a, b):
    return lax.dot_general(a, b, TALL, preferred_element_type=f32)


def iota(shape, dim):
    return lax.broadcasted_iota(jnp.int32, shape, dim)


def norm_parts(values):
    mean = jnp.mean(values, -1, keepdims=True)
    centered = values - mean
    scale = lax.rsqrt(jnp.mean(centered * centered, -1, keepdims=True) + 1e-05)
    return centered * scale, scale


def split(v):
    high = v.astype(bf16)
    return high, (v - high.astype(f32)).astype(bf16)


def call(body, outs, scratch=(), cost=4.0, n_smem=0, n_in=0, name=None):
    smem = [pl.BlockSpec(memory_space=pltpu.SMEM)] * n_smem
    vmem = [pl.BlockSpec(memory_space=pltpu.VMEM)] * n_in
    shapes = [jax.ShapeDtypeStruct(s, d) for s, d in outs]
    specs = [pl.BlockSpec(memory_space=pltpu.VMEM)] * len(outs)
    single = len(outs) == 1
    return pl.pallas_call(
        body,
        out_shape=shapes[0] if single else shapes,
        in_specs=smem + vmem,
        out_specs=specs[0] if single else specs,
        scratch_shapes=list(scratch),
        compiler_params=pltpu.CompilerParams(vmem_limit_bytes=40 * 1024 * 1024),
        cost_estimate=pl.CostEstimate(flops=int(cost * 5e8), bytes_accessed=int(cost * 2e6), transcendentals=0),
        name=name,
    )


def prepare_body(core_ref, perm_ref, w_in_ref, w_down_ref, out_ref):
    core = core_ref[0]

    @pl.when(core == 0)
    def _():
        mine = mm(w_in_ref[...], perm_ref[...]).astype(bf16).reshape(2, PART, PART)
        for k in range(N_X):
            out_ref[k] = mine

    @pl.when(core != 0)
    def _():
        mine = mm_tall(perm_ref[...], w_down_ref[...]).astype(bf16)
        for k in range(N_X):
            out_ref[k, 0] = mine[:, :PART]
            out_ref[k, 1] = mine[:, PART:]


def attend_body(
    cols_ref, rows_ref, same_ref, keys_ref, values_ref, embed_ref, w_query_ref, w_key_ref, w_value_ref, w_self_ref,
    cross_query_ref, cross_out_ref, gain_self_ref, gain_cross_ref, states_ref, ctx_ref,
):
    embed = embed_ref[...]
    names = (iota((32, VOCAB), 0) == iota((32, VOCAB), 1)).astype(bf16)
    table = mm(names, embed).astype(bf16)
    picks = (cols_ref[:, 0:1] == iota((ROWS, 32), 1)).astype(bf16)
    picks_t = (rows_ref[0:1, :] == iota((32, ROWS), 0)).astype(bf16)
    embedded = mm(picks, table)
    query = mm(embedded.astype(bf16), w_query_ref[...]).astype(bf16)
    keyed = mm(table, w_key_ref[...])
    valued = mm(table, w_value_ref[...])
    own = iota((HEADS * 32, WIDTH), 0) // 32 == iota((HEADS * 32, WIDTH), 1) // 64
    key_blocks = jnp.where(own, jnp.concatenate([keyed] * HEADS, 0), 0.0).astype(bf16)
    value_blocks = jnp.where(own, jnp.concatenate([valued] * HEADS, 0), 0.0).astype(bf16)
    scores = (mm_flip(key_blocks, query) * 0.125).reshape(HEADS, 32, ROWS)
    counts = mm(picks_t, same_ref[...])[None]
    scores = jnp.where(counts > 0.0, scores, -1e30)
    probs = jnp.exp(scores - jnp.max(scores, 1, keepdims=True)) * counts
    probs = probs / jnp.sum(probs, 1, keepdims=True)
    context = mm_tall(probs.reshape(HEADS * 32, ROWS).astype(bf16), value_blocks).astype(bf16)
    unit, _ = norm_parts(embedded + mm(context, w_self_ref[...]))
    attended = (unit * gain_self_ref[...]).astype(bf16)
    cross_q = mm(attended, cross_query_ref[...]).astype(bf16)
    left = iota((PAD, LANES), 1) < 64
    for s in range(2):
        for pair in range(HEADS // 2):
            lanes = slice(pair * LANES, (pair + 1) * LANES)
            q = cross_q[s * PAD : (s + 1) * PAD, lanes]
            k = keys_ref[s, :, lanes]
            v = values_ref[s, :, lanes]
            both = []
            for mine in (left, jnp.logical_not(left)):
                logit = mm_flip(jnp.where(mine, q, jnp.zeros_like(q)), k) * 0.125
                e = jnp.exp(logit - jnp.max(logit, -1, keepdims=True))
                p = (e / jnp.sum(e, -1, keepdims=True)).astype(bf16)
                both.append(mm(p, v))
            ctx_ref[s * PAD : (s + 1) * PAD, lanes] = jnp.where(left, both[0], both[1]).astype(bf16)
    unit, _ = norm_parts(attended.astype(f32) + mm(ctx_ref[...], cross_out_ref[...]))
    states_ref[...] = (unit * gain_cross_ref[...]).astype(bf16)


def forward_body(
    core_ref, accept_ref, cols_ref, rows_ref, beams_ref, states_ref, got_ref, other_ref, gain_ref, head_ref,
    message_ref, hidden_ref, slope_ref, unit_ref, w_down_ref, signal_ref, scale_ref,
):
    first = core_ref[0] == 0
    states = states_ref[...]
    total = [states[:, :PART].astype(f32), states[:, PART:].astype(f32)]
    for m in range(N_X):
        got, other = got_ref[m], other_ref[m]
        w_in = jnp.where(first, got, other).reshape(WIDTH, PART)
        w_down = jnp.where(first, other, got)
        w_down_ref[m] = w_down
        pre = mm(states, w_in)
        tanh = jnp.tanh(0.7978845608028654 * (pre + 0.044715 * pre * pre * pre))
        hidden = (0.5 * pre * (1.0 + tanh)).astype(bf16)
        slope = 0.5 * (1.0 + tanh) + 0.5 * pre * (1.0 - tanh * tanh) * 0.7978845608028654 * (1.0 + 0.134145 * pre * pre)
        for c in range(2):
            here = slice(c * HALF + m * LANES, c * HALF + (m + 1) * LANES)
            hidden_ref[:, here] = hidden[:, c * LANES : (c + 1) * LANES]
            slope_ref[:, here] = slope[:, c * LANES : (c + 1) * LANES]
        for k in range(2):
            total[k] = total[k] + mm(hidden, w_down[k])
    unit, scale = norm_parts(jnp.concatenate(total, 1))
    unit_ref[...] = unit
    scale_ref[...] = jnp.broadcast_to(scale, (ROWS, LANES))
    high, low = split(unit * gain_ref[...])
    logits = mm(high, head_ref[...]) + mm(low, head_ref[...])
    lane = iota((ROWS, LANES), 1)
    logits = jnp.where(lane < VOCAB, logits, -1e30)
    top = jnp.max(logits, -1, keepdims=True)
    grown = jnp.exp(logits - top)
    mass = jnp.sum(grown, -1, keepdims=True)
    is_label = cols_ref[:, 1:2] == lane
    taken = jnp.sum(jnp.where(is_label, logits, 0.0), -1, keepdims=True) - top - jnp.log(mass)
    beams = beams_ref[...]
    score = jnp.sum(beams * taken, 0, keepdims=True) / STEPS
    place = iota((1, LANES), 1)
    shares = jnp.zeros((1, LANES), f32)
    for s in range(2):
        inside = (place >= s * BEAM) & (place < (s + 1) * BEAM)
        e = jnp.where(inside, jnp.exp(score - jnp.max(jnp.where(inside, score, -1e30), -1, keepdims=True)), 0.0)
        share = e / jnp.sum(e, -1, keepdims=True) * accept_ref[s].astype(f32)
        shares = jnp.where(inside, share, shares)
    weight = jnp.sum(beams * shares, -1, keepdims=True)
    signal_ref[...] = weight * (grown / mass - is_label.astype(f32))
    hits = cols_ref[:, 2:3] == lane
    earlier = (iota((ROWS, ROWS), 0) > iota((ROWS, ROWS), 1)).astype(bf16)
    before = mm(earlier, hits.astype(bf16))
    rank = jnp.sum(jnp.where(hits, before, 0.0), -1, keepdims=True).astype(jnp.int32)
    sums = jnp.sum(jnp.where(hits, weight, 0.0), 0, keepdims=True)
    placed = jnp.where(rank == lane, -weight * taken, 0.0)
    hits_t = (rows_ref[2:3, :] == iota((LANES, ROWS), 0)).astype(bf16)
    high, low = split(placed)
    message_ref[:, 0, :] = jnp.broadcast_to(sums, (N_DP, LANES))
    message_ref[:, 1, :] = mm(hits_t, high) + mm(hits_t, low)


def backward_body(
    core_ref, cols_ref, states_ref, hidden_ref, slope_ref, unit_ref, w_down_ref, signal_ref, scale_ref, gain_ref, head_ref,
    keep_ref, send_ref, d_pre_ref,
):
    core = core_ref[0]
    unit = unit_ref[...]
    high, low = split(signal_ref[...])
    d_unit = gain_ref[...] * (mm_flip(high, head_ref[...]) + mm_flip(low, head_ref[...]))
    along = jnp.mean(d_unit * unit, -1, keepdims=True)
    d_total = scale_ref[:, 0:1] * (d_unit - jnp.mean(d_unit, -1, keepdims=True) - unit * along)
    d_out = d_total.astype(bf16)
    for m in range(N_X):
        d_hidden = mm_flip(d_out[:, :PART], w_down_ref[m, 0]) + mm_flip(d_out[:, PART:], w_down_ref[m, 1])
        for c in range(2):
            here = slice(m * LANES, (m + 1) * LANES)
            there = slice(c * HALF + m * LANES, c * HALF + (m + 1) * LANES)
            d_pre_ref[c, :, here] = (d_hidden[:, c * LANES : (c + 1) * LANES] * slope_ref[:, there]).astype(bf16)
    states = states_ref[...]
    dest = jnp.broadcast_to(cols_ref[:, 2:3], (ROWS, LANES)).astype(f32).astype(bf16)
    for ref, half in ((keep_ref, core), (send_ref, 1 - core)):
        ref[:, 0:WIDTH] = d_pre_ref[half]
        ref[:, WIDTH : 2 * WIDTH] = hidden_ref[:, pl.ds(pl.multiple_of(half * HALF, HALF), HALF)]
        ref[:, 2 * WIDTH : 3 * WIDTH] = states
        ref[:, 3 * WIDTH : 4 * WIDTH] = d_out
        ref[:, 4 * WIDTH :] = dest


def term_body(keep_ref, other_ref, got_ref, term_ref, loss_ref, all_ref):
    sums = jnp.sum(got_ref[:, 0, :], 0, keepdims=True)
    loss_ref[...] = got_ref[:, 1, :]
    inverse = 1.0 / jnp.maximum(sums, 1.0)
    lane = iota((ROWS, LANES), 1).astype(f32)
    for place, ref in ((0, keep_ref), (1, other_ref)):
        rows = slice(place * ROWS, (place + 1) * ROWS)
        hits = ref[:, 4 * WIDTH :].astype(f32) == lane
        factor = jnp.sum(jnp.where(hits, inverse, 0.0), -1, keepdims=True)
        all_ref[rows, : 2 * WIDTH] = ref[:, : 2 * WIDTH]
        all_ref[rows, 2 * WIDTH :] = (ref[:, 2 * WIDTH : 4 * WIDTH].astype(f32) * factor).astype(bf16)
    for k in range(2):
        grad = mm_tall(all_ref[:, k * WIDTH : (k + 1) * WIDTH], all_ref[:, (k + 2) * WIDTH : (k + 3) * WIDTH])
        grad = grad.astype(bf16)
        for m in range(N_X):
            for x in range(N_X):
                start = m * LANES + x * 32
                term_ref[x, m * 32 : (m + 1) * 32, k * WIDTH : (k + 1) * WIDTH] = grad[start : start + 32]


def middle_body(got_ref, out_ref, held_ref):
    total = got_ref[0].astype(f32)
    for k in range(1, N_X):
        total = total + got_ref[k].astype(f32)
    for m in range(N_X):
        for r in range(2):
            for c in range(8):
                block = total[m * 32 + r * 16 : m * 32 + (r + 1) * 16, c * LANES : (c + 1) * LANES]
                held_ref[m * 16 : (m + 1) * 16, r * 8 + c, :] = block
    out_ref[...] = held_ref[...].astype(bf16)


def final_body(got_ref, momentum_ref, out_ref):
    total = jnp.sum(got_ref[...].astype(f32), 0)
    for r in range(2):
        for c in range(8):
            lanes = slice(c * LANES, (c + 1) * LANES)
            out_ref[r : r + 1, lanes] = 0.9 * momentum_ref[r : r + 1, lanes] + total[r * 8 + c : r * 8 + c + 1]


def constants():
    unit = np.arange(PART)
    target = unit.reshape(2, 4, 2, 16).transpose(3, 0, 1, 2).reshape(-1)
    perm = np.zeros((PART, PART), np.float32)
    perm[unit, target] = 1.0
    row = np.arange(ROWS)
    inside = row % PAD
    group = row // PAD * 6 + inside // (STEPS + 1)
    same = (group[:, None] == group[None, :]) & (row[:, None] <= row[None, :])
    valid = (inside < SEG) & (inside % (STEPS + 1) < STEPS)
    beam = np.where(valid, row // PAD * BEAM + inside // (STEPS + 1), -1)
    beams = beam[:, None] == np.arange(LANES)[None, :]
    return jnp.asarray(perm, bf16), jnp.asarray(same, bf16), jnp.asarray(beams, f32)


def per_device(
    tokens, accept, dest, mem_keys, mem_values, embed, w_query, w_key, w_value, w_self, cross_query, cross_out,
    gain_self, gain_cross, w_in, w_down, gain_ff, head, momentum,
):
    perm, same, beams = constants()
    core = lax.axis_index("core").astype(jnp.int32).reshape(1)
    swap = [(0, 1), (1, 0)]

    mine = call(prepare_body, [((N_X, 2, PART, PART), bf16)], n_smem=1, n_in=3, cost=1, name="prepare")(core, perm, w_in, w_down)
    got_w = lax.all_to_all(mine, "x", 0, 0)
    other_w = lax.ppermute(got_w, "core", swap)

    flat = jnp.pad(tokens.reshape(2, SEG), ((0, 0), (0, PAD - SEG))).reshape(ROWS)
    nexts = jnp.concatenate([flat[1:], flat[:1]])
    place = jnp.pad(dest.reshape(2, BEAM, STEPS), ((0, 0), (0, 0), (0, 1)), constant_values=-1).reshape(2, SEG)
    place = jnp.pad(place, ((0, 0), (0, PAD - SEG)), constant_values=-1).reshape(ROWS)
    rows = jnp.stack([flat, nexts, place, place, place, place, place, place])
    cols = rows.T
    states = call(
        attend_body, [((ROWS, WIDTH), bf16)], scratch=[pltpu.VMEM((ROWS, WIDTH), bf16)], n_in=14, cost=8, name="attend"
    )(
        cols, rows, same, mem_keys, mem_values, embed, w_query, w_key, w_value, w_self, cross_query, cross_out,
        gain_self.reshape(1, WIDTH), gain_cross.reshape(1, WIDTH),
    )
    gain = gain_ff.reshape(1, WIDTH)
    head = jnp.pad(head, ((0, 0), (0, LANES - VOCAB)))
    message, hidden, slope, unit, down, signal, scale = call(
        forward_body,
        [
            ((N_DP, 2, LANES), f32),
            ((ROWS, FF), bf16),
            ((ROWS, FF), f32),
            ((ROWS, WIDTH), f32),
            ((N_X, 2, PART, PART), bf16),
            ((ROWS, LANES), f32),
            ((ROWS, LANES), f32),
        ],
        n_smem=2, n_in=8, cost=5, name="forward",
    )(core, accept, cols, rows, beams, states, got_w, other_w, gain, head)
    got = lax.all_to_all(message, DP, 0, 0)
    keep, send = call(
        backward_body,
        [((ROWS, PAY), bf16), ((ROWS, PAY), bf16)],
        scratch=[pltpu.VMEM((2, ROWS, HALF), bf16)],
        n_smem=1, n_in=10, cost=4, name="backward",
    )(core, cols, states, hidden, slope, unit, down, signal, scale, gain, head)
    other = lax.ppermute(send, "core", swap)
    term, loss = call(
        term_body,
        [((N_X, LANES, 2 * WIDTH), bf16), ((N_DP, LANES), f32)],
        scratch=[pltpu.VMEM((2 * ROWS, 4 * WIDTH), bf16)],
        n_in=3, cost=4, name="term",
    )(keep, other, got)
    got = lax.all_to_all(term, "x", 0, 0)
    middle = call(
        middle_body, [((64, 16, LANES), bf16)], scratch=[pltpu.VMEM((64, 16, LANES), f32)], n_in=1, cost=1, name="middle"
    )(got)
    got = lax.all_to_all(middle, ("z", "y"), 0, 0)
    out = call(final_body, [((2, 2 * WIDTH), f32)], n_in=2, cost=1, name="final")(got, momentum)
    return out, loss[:, :CAP].reshape(1, N_DP * CAP)


def solution(mesh):
    n_dp, n_mp = mesh.devices.shape
    side = int(np.sqrt(n_dp // 2))
    fine = Mesh(mesh.devices.reshape(side, side, 2, n_mp), EVERY)
    placed = (
        P(EVERY, None, None),
        P(EVERY),
        P(EVERY, None),
        P(EVERY, None, None),
        P(EVERY, None, None),
        P(),
        P(),
        P(),
        P(),
        P(),
        P(),
        P(),
        P(),
        P(),
        P(None, "x"),
        P("x", None),
        P(),
        P(),
        P(EVERY, None),
    )
    return jax.shard_map(
        per_device,
        mesh=fine,
        in_specs=placed,
        out_specs=(P(EVERY, None), P(EVERY, None)),
        check_vma=False,
    )
```

time: 135 us -> 114 us (0.84)
  blocking collectives: 18.6 us -> 62.5 us
  matrix products: 23.7 us -> 0 us
  starting transfers between devices: 32.9 us -> 14.1 us
  waiting for transfers between devices: 25.9 us -> 11.7 us
  Pallas kernels: 0 us -> 11.7 us
  other arithmetic: 10.6 us -> 0.74 us
  local copies, waits for them, and re-layouts: 19.7 us -> 10.3 us
    all_to_all x1 -> x3, blocking collectives: 18.6 us -> 62.5 us  [the longest x1 30 us: per_device(): got = lax.all_to_all(message, DP, 0, 0)]
    dot_general x20 -> x0, matrix products: 22 us -> none  [the longest x12 7.74 us: mm(): return jnp.dot(a, b, preferred_element_type=f32)]
    all_to_all x3 -> x1, starting transfers between devices: 22 us -> 4.61 us  [per_device(): got = lax.all_to_all(middle, ('z', 'y'), 0, 0)]
    pallas_call x0 -> x7, Pallas kernels: none -> 11.7 us  [the longest x1 3.91 us: per_device(): call(attend_body, [((ROWS, WIDTH), bf16)], scratch=[pltpu.VMEM((ROWS, WID...]
    all_to_all x3 -> x1, waiting for transfers between devices: 23.3 us -> 11.7 us  [per_device(): got = lax.all_to_all(middle, ('z', 'y'), 0, 0)]
    reshape x12 -> x5, local copies, waits for them, and re-layouts: 7.86 us -> 1.11 us  [the longest x1 0.79 us: per_device(): return (out, loss[:, :CAP].reshape(1, N_DP * CAP))]
    unnamed x40 -> x44, local copies, waits for them, and re-layouts: 3.53 us -> 8.2 us
    reduce_sum x12 -> x0, other arithmetic: 3.04 us -> none  [the longest x1 1.51 us: scatter_sum(): mine = jnp.sum(got.astype(f32), 0).astype(bf16)]
  transfers between devices with their start and end apart: 5 -> 3, of which waited for: 3 -> 1; matrix products, arithmetic and copies ran while one was open for 18% -> 5% of each run, Pallas kernels for 0% -> 3%
where the time goes in v2:
time: 114 us; the launch traced here: 112 us
  blocking collectives  62.5 us (55%)
  starting transfers between devices  14.1 us (12%)
  Pallas kernels  11.7 us (10%)
  waiting for transfers between devices  11.7 us (10%)
  local copies, waits for them, and re-layouts  10.3 us (9%)
    all_to_all x1, blocking collectives, per_device(): got = lax.all_to_all(message, DP, 0, 0)  30 us
    all_to_all x1, blocking collectives, per_device(): got = lax.all_to_all(term, 'x', 0, 0)  17.2 us
    all_to_all x1, blocking collectives, per_device(): got_w = lax.all_to_all(mine, 'x', 0, 0)  15.3 us
    all_to_all x1, waiting for transfers between devices, per_device(): got = lax.all_to_all(middle, ('z', 'y'), 0, 0)  11.7 us
    unnamed x44, local copies, waits for them, and re-layouts  8.2 us
    ppermute x1, starting transfers between devices, per_device(): other_w = lax.ppermute(got_w, 'core', swap)  7.6 us
    all_to_all x1, starting transfers between devices, per_device(): got = lax.all_to_all(middle, ('z', 'y'), 0, 0)  4.61 us
    pallas_call x1, Pallas kernels, per_device(): call(attend_body, [((ROWS, WIDTH), bf16)], scratch=[pltpu.VMEM((ROWS, WID...  3.91 us
  transfers between devices with their start and end apart: 3, of which 1 were waited for; matrix products, arithmetic and copies ran while one was open for 5% of the time, Pallas kernels for 3%

profile of v2, /device:TPU:1, one launch (start us, length us, event | category | flops | bytes accessed | tf_op | source)
XLA Modules:
  0.0 112.0 jit_solution(11739830435713486484)
XLA Ops:
  0.6 0.0 copy-start.6
  0.6 0.9 copy-done.6
  1.6 0.0 copy-start.7
  1.6 0.9 copy-done.7
  2.5 0.0 copy-start.16
  2.5 0.9 copy-done.16
  3.4 0.2 prepare.1
  3.7 0.0 copy-start.18
  3.7 0.0 copy-start.19
  3.7 0.0 copy-start.17
  3.7 15.3 %all_to_all.20.got_ref = bf16[4,2,256,256]{3,2,1,0:T(8,128)(2,1)S(1)} all-to-all(bf16[4,2,256,256]{3,2,1,0:T(8,128)(2,1)S(1)} %prepare.1), channel_id=1, replica_groups=mesh['z'=8,'y'=8,'core'=2,'x'=4] {'x'}, dimensions={0} | all-to-all | bytes 2097152 | tf_op jit(solution)/shard_map/all_to_all | solution.py:291
  19.0 0.0 copy-start
  19.0 0.0 copy-start.1
  19.0 0.0 copy-start.8
  19.0 0.0 copy-start.10
  19.0 0.0 copy-start.11
  19.0 7.6 %collective-permute-start = (bf16[4,2,256,256]{3,2,1,0:T(8,128)(2,1)S(1)}, bf16[4,2,256,256]{3,2,1,0:T(8,128)(2,1)S(1)}, u32[]{:S(2)}, u32[]{:S(2)}) collective-permute-start(bf16[4,2,256,256]{3,2,1,0:T(8,128)(2,1)S(1)} %all_to_all.20.got_ref), channel_id=1, source_target_pairs={{0,4},{4,0},{1,5},{5,1},{2,6},{6,2},{3,7},{7,3},{8,12},{12,8},{9,1... | collective-permute-start | bytes 3145736 | tf_op jit(solution)/shard_map/ppermute | solution.py:292
  26.6 0.0 copy-done.18
  26.6 0.1 reshape.32
  26.7 0.1 stack_reshape.4
  26.8 0.1 reshape.33
  26.9 0.5 slice.10
  27.4 0.1 slice.9
  27.5 0.0 copy-done.19
  27.5 0.1 reshape.34
  27.6 0.1 reshape.35
  27.7 0.1 stack_reshape.5
  27.8 0.7 pad_add_fusion
  28.5 0.0 copy-done.17
  28.5 0.1 copy.47
  28.7 0.1 copy.44
  28.8 0.0 copy-start.2
  28.9 0.0 copy-start.14
  28.9 1.1 copy.45.keys_ref
  29.9 1.0 copy.46.values_ref
  31.0 0.0 copy-done
  31.0 0.0 copy-done.1
  31.0 0.0 copy-done.8
  31.0 0.0 copy-done.10
  31.0 0.0 copy-done.11
  31.0 0.0 copy-done.2
  31.0 0.0 copy-done.14
  31.1 0.0 copy-start.3
  31.1 1.0 copy-done.3
  32.1 1.0 copy-done.4
  33.1 1.0 copy-done.5
  34.2 3.9 %attend.1.states_ref = bf16[320,512]{1,0:T(8,128)(2,1)S(1)} custom-call(s32[320,8]{1,0:T(8,128)S(1)} %bitcast.6, s32[8,320]{1,0:T(8,128)S(1)} %stack.7.rows_ref, bf16[320,320]{1,0:T(8,128)(2,1)S(1)} %copy-done.14, bf16[2,150,512]{2,1,0:T(8,128)(2,1)S(1)} %copy.45.keys_ref, bf16[2,150,512]{2,1,0:T(8,128)(2,1)S(1)} %copy.46.values_ref, ...), custom_call_target="tpu_custom_call" | custom-call | flops 4000000000 | bytes 16000000 | tf_op jit(solution)/shard_map/attend/pallas_call | solution.py:300
  38.1 0.0 collective-permute-done.other_ref
  38.1 0.0 copy-done.12
  38.1 0.0 copy-done.13
  38.1 0.0 copy-done.15
  38.1 3.4 %forward.1 = (f32[128,2,128]{2,1,0:T(2,128)S(1)}, bf16[320,1024]{1,0:T(8,128)(2,1)S(1)}, f32[320,1024]{1,0:T(8,128)S(1)}, f32[320,512]{1,0:T(8,128)S(1)}, bf16[4...) custom-call(s32[1]{0:T(128)} %bitcast.core_ref, s32[2]{0:T(128)S(1)} %copy-done.13, ...), custom_call_target="tpu_custom_call" | custom-call | flops 2500000000 | bytes 10000000 | tf_op jit(solution)/shard_map/forward/pallas_call | solution.py:308
  41.6 1.1 backward.1
  42.6 1.9 %collective-permute-start.1 = (bf16[320,2176]{1,0:T(8,128)(2,1)S(1)}, bf16[320,2176]{1,0:T(8,128)(2,1)S(1)}, u32[]{:S(2)}, u32[]{:S(2)}) collective-permute-start(bf16[320,2176]{1,0:T(8,128)(2,1)S(1)} %get-tuple-element.20), channel_id=1, source_target_pairs={{0,4},{4,0},{1,5},{5,1},{2,6},{6,2},{3,7},{7,3},{8,12},{12,8},{9,1... | collective-permute-start | bytes 4177928 | tf_op jit(solution)/shard_map/ppermute | solution.py:328
  44.6 30.0 %all_to_all.21.got_ref = f32[128,2,128]{2,1,0:T(2,128)S(1)} all-to-all(f32[128,2,128]{2,1,0:T(2,128)S(1)} %get-tuple-element.21), channel_id=1, replica_groups=mesh['z'=8,'y'=8,'core'=2,'x'=4] {'z','y','core'}, dimensions={0} | all-to-all | bytes 262144 | tf_op jit(solution)/shard_map/all_to_all | solution.py:321
  74.5 0.0 collective-permute-done.1.other_ref
  74.5 1.2 %term.1 = (bf16[4,128,1024]{2,1,0:T(8,128)(2,1)S(1)}, f32[128,128]{1,0:T(8,128)S(1)}) custom-call(bf16[320,2176]{1,0:T(8,128)(2,1)S(1)} %get-tuple-element.19.keep_ref, bf16[320,2176]{1,0:T(8,128)(2,1)S(1)} %collective-permute-done.1.other_ref, f32[128,2,128]{2,1,0:T(2,128)S(1)} %all_to_all.21.got_ref), custom_call_target="tpu_custom_call" | custom-call | flops 2000000000 | bytes 8000000 | tf_op jit(solution)/shard_map/term/pallas_call | solution.py:329
  75.7 17.2 %all_to_all.22.got_ref = bf16[4,128,1024]{2,1,0:T(8,128)(2,1)S(1)} all-to-all(bf16[4,128,1024]{2,1,0:T(8,128)(2,1)S(1)} %get-tuple-element.22), channel_id=1, replica_groups=mesh['z'=8,'y'=8,'core'=2,'x'=4] {'x'}, dimensions={0} | all-to-all | bytes 2097152 | tf_op jit(solution)/shard_map/all_to_all | solution.py:335
  92.9 1.2 %middle.1 = bf16[64,16,128]{2,1,0:T(8,128)(2,1)} custom-call(bf16[4,128,1024]{2,1,0:T(8,128)(2,1)S(1)} %all_to_all.22.got_ref), custom_call_target="tpu_custom_call" | custom-call | flops 500000000 | bytes 2000000 | tf_op jit(solution)/shard_map/middle/pallas_call | solution.py:336
  94.2 4.6 %all-to-all-start.3 = ((bf16[64,16,128]{2,1,0:T(8,128)(2,1)}), bf16[64,16,128]{2,1,0:T(8,128)(2,1)S(1)}, u32[]{:S(2)}, u32[]{:S(2)}) async-start(bf16[64,16,128]{2,1,0:T(8,128)(2,1)} %middle.1), calls=%async_computation.3 | async-start | bytes 524288 | tf_op jit(solution)/shard_map/all_to_all | solution.py:339
  98.8 0.8 reshape.39
  99.6 11.7 %all-to-all-done.3.got_ref = bf16[64,16,128]{2,1,0:T(8,128)(2,1)S(1)} async-done(((bf16[64,16,128]{2,1,0:T(8,128)(2,1)}), bf16[64,16,128]{2,1,0:T(8,128)(2,1)S(1)}, u32[]{:S(2)}, u32[]{:S(2)}) %all-to-all-start.3) | async-done | bytes 262176 | tf_op jit(solution)/shard_map/all_to_all | solution.py:339
  111.3 0.0 copy-done.9
  111.3 0.7 final.1
  (14 shorter events, 0.1 us)
Async XLA Ops:
  0.6 1.0 copy-start.6
  1.6 0.9 copy-start.7
  2.5 0.9 copy-start.16
  3.7 22.9 %copy-start.18 = (s32[2,5,31]{2,0,1:T(2,128)S(1)}, s32[2,5,31]{2,0,1:T(2,128)}, u32[]{:S(2)}) copy-start(s32[2,5,31]{2,0,1:T(2,128)} %param.22) | copy-start | bytes 3724
  3.7 23.8 %copy-start.19 = (s32[300,1]{0,1:T(1,128)S(1)}, s32[300,1]{0,1:T(1,128)}, u32[]{:S(2)}) copy-start(s32[300,1]{0,1:T(1,128)} %param.24) | copy-start | bytes 3604
  3.7 24.8 %copy-start.17 = (bf16[512,28]{0,1:T(8,128)(2,1)S(1)}, bf16[512,28]{0,1:T(8,128)(2,1)}, u32[]{:S(2)}) copy-start(bf16[512,28]{0,1:T(8,128)(2,1)} %param.39) | copy-start | bytes 86020
  19.0 12.0 %copy-start = (bf16[512,512]{1,0:T(8,128)(2,1)S(1)}, bf16[512,512]{1,0:T(8,128)(2,1)}, u32[]{:S(2)}) copy-start(bf16[512,512]{1,0:T(8,128)(2,1)} %w_query_ref.1) | copy-start | bytes 1572868
  19.0 12.0 %copy-start.1 = (bf16[512,512]{1,0:T(8,128)(2,1)S(1)}, bf16[512,512]{1,0:T(8,128)(2,1)}, u32[]{:S(2)}) copy-start(bf16[512,512]{1,0:T(8,128)(2,1)} %w_key_ref.1) | copy-start | bytes 1572868
  19.0 12.0 %copy-start.8 = (bf16[28,512]{1,0:T(8,128)(2,1)S(1)}, bf16[28,512]{1,0:T(8,128)(2,1)}, u32[]{:S(2)}) copy-start(bf16[28,512]{1,0:T(8,128)(2,1)} %embed_ref.1) | copy-start | bytes 86020
  19.0 12.0 %copy-start.10 = (f32[512]{0:T(512)S(1)}, f32[512]{0:T(512)}, u32[]{:S(2)}) copy-start(f32[512]{0:T(512)} %param.34) | copy-start | bytes 6148
  19.0 12.0 %copy-start.11 = (f32[512]{0:T(512)S(1)}, f32[512]{0:T(512)}, u32[]{:S(2)}) copy-start(f32[512]{0:T(512)} %param.35) | copy-start | bytes 6148
  19.0 19.1 %collective-permute-start = (bf16[4,2,256,256]{3,2,1,0:T(8,128)(2,1)S(1)}, bf16[4,2,256,256]{3,2,1,0:T(8,128)(2,1)S(1)}, u32[]{:S(2)}, u32[]{:S(2)}) collective-permute-start(bf16[4,2,256,256]{3,2,1,0:T(8,128)(2,1)S(1)} %all_to_all.20.got_ref), channel_id=1, source_target_pairs={{0,4},{4,0},{1,5},{5,1},{2,6},{6,2},{3,7},{7,3},{8,12},{12,8},{9,1... | collective-permute-start | bytes 3145736 | tf_op jit(solution)/shard_map/ppermute | solution.py:292
  28.8 2.2 %copy-start.2 = (bf16[512,512]{1,0:T(8,128)(2,1)S(1)}, bf16[512,512]{1,0:T(8,128)(2,1)}, u32[]{:S(2)}) copy-start(bf16[512,512]{1,0:T(8,128)(2,1)} %w_value_ref.1) | copy-start | bytes 1572868
  28.9 2.2 %copy-start.14 = (bf16[320,320]{1,0:T(8,128)(2,1)S(1)}, bf16[320,320]{1,0:T(8,128)(2,1)}, u32[]{:S(2)}) copy-start(bf16[320,320]{1,0:T(8,128)(2,1)} %constant.19.clone.same_ref) | copy-start | bytes 614404
  31.1 1.0 copy-start.3
  32.1 1.0 copy-start.4
  33.1 1.0 copy-start.5
  34.2 3.9 %copy-start.12 = (f32[512]{0:T(512)S(1)}, f32[512]{0:T(512)}, u32[]{:S(2)}) copy-start(f32[512]{0:T(512)} %param.38) | copy-start | bytes 6148
  34.2 3.9 %copy-start.13 = (s32[2]{0:T(128)S(1)}, s32[2]{0:T(128)}, u32[]{:S(2)}) copy-start(s32[2]{0:T(128)} %accept_ref.1) | copy-start | bytes 28
  34.2 4.0 %copy-start.15 = (f32[320,128]{1,0:T(8,128)S(1)}, f32[320,128]{1,0:T(8,128)}, u32[]{:S(2)}) copy-start(f32[320,128]{1,0:T(8,128)} %constant.20.clone.beams_ref) | copy-start | bytes 491524
  42.6 31.9 %collective-permute-start.1 = (bf16[320,2176]{1,0:T(8,128)(2,1)S(1)}, bf16[320,2176]{1,0:T(8,128)(2,1)S(1)}, u32[]{:S(2)}, u32[]{:S(2)}) collective-permute-start(bf16[320,2176]{1,0:T(8,128)(2,1)S(1)} %get-tuple-element.20), channel_id=1, source_target_pairs={{0,4},{4,0},{1,5},{5,1},{2,6},{6,2},{3,7},{7,3},{8,12},{12,8},{9,1... | collective-permute-start | bytes 4177928 | tf_op jit(solution)/shard_map/ppermute | solution.py:328
  92.9 18.3 %copy-start.9 = (f32[2,1024]{1,0:T(2,128)S(1)}, f32[2,1024]{1,0:T(2,128)}, u32[]{:S(2)}) copy-start(f32[2,1024]{1,0:T(2,128)} %momentum_ref.1) | copy-start | bytes 24580
  94.2 17.1 %all-to-all-start.3 = ((bf16[64,16,128]{2,1,0:T(8,128)(2,1)}), bf16[64,16,128]{2,1,0:T(8,128)(2,1)S(1)}, u32[]{:S(2)}, u32[]{:S(2)}) async-start(bf16[64,16,128]{2,1,0:T(8,128)(2,1)} %middle.1), calls=%async_computation.3 | async-start | bytes 524288 | tf_op jit(solution)/shard_map/all_to_all | solution.py:339

commit v3 on v2

v3 whole, which is shorter than its diff:
```python
import jax
import jax.numpy as jnp
import numpy as np
from jax import lax
from jax.experimental import pallas as pl
from jax.experimental.pallas import tpu as pltpu
from jax.sharding import Mesh
from jax.sharding import PartitionSpec as P

HEADS = 8
BEAM = 5
STEPS = 30
CAP = 5
SEG = BEAM * (STEPS + 1)
PAD = 160
ROWS = 2 * PAD
WIDTH = 512
FF = 1024
VOCAB = 28
PEAKS = 150
LANES = 128
N_DP = 128
N_X = 4
PART = FF // N_X
HALF = FF // 2
PAY = 4 * WIDTH + LANES
f32 = jnp.float32
bf16 = jnp.bfloat16
FLIP = (((1,), (1,)), ((), ()))
TALL = (((0,), (0,)), ((), ()))
DP = ("z", "y", "core")
EVERY = ("z", "y", "core", "x")


def mm(a, b):
    return jnp.dot(a, b, preferred_element_type=f32)


def mm_flip(a, b):
    return lax.dot_general(a, b, FLIP, preferred_element_type=f32)


def mm_tall(a, b):
    return lax.dot_general(a, b, TALL, preferred_element_type=f32)


def iota(shape, dim):
    return lax.broadcasted_iota(jnp.int32, shape, dim)


def norm_parts(values):
    mean = jnp.mean(values, -1, keepdims=True)
    centered = values - mean
    scale = lax.rsqrt(jnp.mean(centered * centered, -1, keepdims=True) + 1e-05)
    return centered * scale, scale


def split(v):
    high = v.astype(bf16)
    return high, (v - high.astype(f32)).astype(bf16)


def call(body, outs, scratch=(), cost=4.0, n_smem=0, n_in=0, n_any=0, name=None):
    smem = [pl.BlockSpec(memory_space=pltpu.SMEM)] * n_smem
    vmem = [pl.BlockSpec(memory_space=pltpu.VMEM)] * n_in + [pl.BlockSpec(memory_space=pl.ANY)] * n_any
    shapes = [jax.ShapeDtypeStruct(s, d) for s, d in outs]
    specs = [pl.BlockSpec(memory_space=pltpu.VMEM)] * len(outs)
    single = len(outs) == 1
    return pl.pallas_call(
        body,
        out_shape=shapes[0] if single else shapes,
        in_specs=smem + vmem,
        out_specs=specs[0] if single else specs,
        scratch_shapes=list(scratch),
        compiler_params=pltpu.CompilerParams(vmem_limit_bytes=16 * 1024 * 1024),
        cost_estimate=pl.CostEstimate(flops=int(cost * 5e8), bytes_accessed=int(cost * 2e6), transcendentals=0),
        name=name,
    )


def prepare_body(core_ref, w_in_ref, w_down_ref, out_ref, w_in, w_down, sems):
    loads = [
        pltpu.make_async_copy(w_in_ref, w_in, sems.at[0]),
        pltpu.make_async_copy(w_down_ref, w_down, sems.at[1]),
    ]
    for load in loads:
        load.start()
    unit, place = iota((PART, LANES), 0), iota((PART, LANES), 1)
    wanted = (place % 16) * 16 + core_ref[0] * 8 + place // 16
    chosen = (unit == wanted).astype(bf16)
    loads[0].wait()
    mine_in = lax.dot_general(chosen, w_in[...], (((0,), (1,)), ((), ())), preferred_element_type=f32).astype(bf16)
    loads[1].wait()
    mine_down = mm_tall(chosen, w_down[...]).astype(bf16)
    for k in range(N_X):
        out_ref[k, 0] = mine_in
        out_ref[k, 1] = mine_down


def attend_body(
    cols_ref, rows_ref, same_ref, keys_ref, values_ref, embed_ref, gain_self_ref, gain_cross_ref, w_query_hbm, w_key_hbm,
    w_value_hbm, w_self_hbm, cross_query_hbm, cross_out_hbm, states_ref, at_rank_ref, done_ref, ctx_ref, held, sems,
):
    sources = (w_query_hbm, w_key_hbm, w_value_hbm, w_self_hbm, cross_query_hbm, cross_out_hbm)
    loads = [pltpu.make_async_copy(source, held.at[k], sems.at[k]) for k, source in enumerate(sources)]
    for load in loads:
        load.start()
    lane = iota((ROWS, LANES), 1)
    hits = cols_ref[:, 2:3] == lane
    earlier = (iota((ROWS, ROWS), 0) > iota((ROWS, ROWS), 1)).astype(bf16)
    before = mm(earlier, hits.astype(bf16))
    rank = jnp.sum(jnp.where(hits, before, 0.0), -1, keepdims=True).astype(jnp.int32)
    at_rank_ref[...] = (rank == lane).astype(f32)
    embed = embed_ref[...]
    names = (iota((32, VOCAB), 0) == iota((32, VOCAB), 1)).astype(bf16)
    table = mm(names, embed).astype(bf16)
    picks = (cols_ref[:, 0:1] == iota((ROWS, 32), 1)).astype(bf16)
    picks_t = (rows_ref[0:1, :] == iota((32, ROWS), 0)).astype(bf16)
    embedded = mm(picks, table)
    for load in loads:
        load.wait()
    query = mm(embedded.astype(bf16), held[0]).astype(bf16)
    keyed = mm(table, held[1])
    valued = mm(table, held[2])
    own = iota((HEADS * 32, WIDTH), 0) // 32 == iota((HEADS * 32, WIDTH), 1) // 64
    key_blocks = jnp.where(own, jnp.concatenate([keyed] * HEADS, 0), 0.0).astype(bf16)
    value_blocks = jnp.where(own, jnp.concatenate([valued] * HEADS, 0), 0.0).astype(bf16)
    scores = (mm_flip(key_blocks, query) * 0.125).reshape(HEADS, 32, ROWS)
    counts = mm(picks_t, same_ref[...])[None]
    scores = jnp.where(counts > 0.0, scores, -1e30)
    probs = jnp.exp(scores - jnp.max(scores, 1, keepdims=True)) * counts
    probs = probs / jnp.sum(probs, 1, keepdims=True)
    context = mm_tall(probs.reshape(HEADS * 32, ROWS).astype(bf16), value_blocks).astype(bf16)
    unit, _ = norm_parts(embedded + mm(context, held[3]))
    attended = (unit * gain_self_ref[...]).astype(bf16)
    cross_q = mm(attended, held[4]).astype(bf16)
    left = iota((PAD, LANES), 1) < 64
    for s in range(2):
        for pair in range(HEADS // 2):
            lanes = slice(pair * LANES, (pair + 1) * LANES)
            q = cross_q[s * PAD : (s + 1) * PAD, lanes]
            k = keys_ref[s, :, lanes]
            v = values_ref[s, :, lanes]
            both = []
            for mine in (left, jnp.logical_not(left)):
                logit = mm_flip(jnp.where(mine, q, jnp.zeros_like(q)), k) * 0.125
                e = jnp.exp(logit - jnp.max(logit, -1, keepdims=True))
                p = (e / jnp.sum(e, -1, keepdims=True)).astype(bf16)
                both.append(mm(p, v))
            ctx_ref[s * PAD : (s + 1) * PAD, lanes] = jnp.where(left, both[0], both[1]).astype(bf16)
    unit, _ = norm_parts(attended.astype(f32) + mm(ctx_ref[...], held[5]))
    states = (unit * gain_cross_ref[...]).astype(bf16)
    states_ref[...] = states
    done_ref[...] = states[:16, :LANES]


def half_forward(states, weights_ref, hidden_ref, slope_ref):
    w_in = jnp.concatenate([weights_ref[m, 0] for m in range(N_X)], 0)
    w_down = jnp.concatenate([weights_ref[m, 1] for m in range(N_X)], 0)
    pre = mm_flip(states, w_in)
    tanh = jnp.tanh(0.7978845608028654 * (pre + 0.044715 * pre * pre * pre))
    hidden = (0.5 * pre * (1.0 + tanh)).astype(bf16)
    hidden_ref[...] = hidden
    slope_ref[...] = 0.5 * (1.0 + tanh) + 0.5 * pre * (1.0 - tanh * tanh) * 0.7978845608028654 * (1.0 + 0.134145 * pre * pre)
    return mm(hidden, w_down)


def own_body(states_ref, weights_ref, done_ref, hidden_ref, slope_ref, total_ref):
    states = states_ref[...]
    total_ref[...] = states.astype(f32) + half_forward(states, weights_ref, hidden_ref, slope_ref)


def forward_body(
    accept_ref, cols_ref, at_rank_ref, beams_ref, states_ref, partial_ref, weights_ref, gain_ref, head_ref,
    message_ref, hidden_ref, slope_ref, unit_ref, signal_ref, scale_ref,
):
    unit, scale = norm_parts(partial_ref[...] + half_forward(states_ref[...], weights_ref, hidden_ref, slope_ref))
    unit_ref[...] = unit
    scale_ref[...] = jnp.broadcast_to(scale, (ROWS, LANES))
    high, low = split(unit * gain_ref[...])
    logits = mm(high, head_ref[...]) + mm(low, head_ref[...])
    lane = iota((ROWS, LANES), 1)
    logits = jnp.where(lane < VOCAB, logits, -1e30)
    top = jnp.max(logits, -1, keepdims=True)
    grown = jnp.exp(logits - top)
    mass = jnp.sum(grown, -1, keepdims=True)
    is_label = cols_ref[:, 1:2] == lane
    taken = jnp.sum(jnp.where(is_label, logits, 0.0), -1, keepdims=True) - top - jnp.log(mass)
    beams = beams_ref[...]
    score = jnp.sum(beams * taken, 0, keepdims=True) / STEPS
    place = iota((1, LANES), 1)
    shares = jnp.zeros((1, LANES), f32)
    for s in range(2):
        inside = (place >= s * BEAM) & (place < (s + 1) * BEAM)
        e = jnp.where(inside, jnp.exp(score - jnp.max(jnp.where(inside, score, -1e30), -1, keepdims=True)), 0.0)
        share = e / jnp.sum(e, -1, keepdims=True) * accept_ref[s].astype(f32)
        shares = jnp.where(inside, share, shares)
    weight = jnp.sum(beams * shares, -1, keepdims=True)
    signal_ref[...] = weight * (grown / mass - is_label.astype(f32))
    hits = cols_ref[:, 2:3] == lane
    sums = jnp.sum(jnp.where(hits, weight, 0.0), 0, keepdims=True)
    high, low = split(at_rank_ref[...] * (-weight * taken))
    hits16 = hits.astype(bf16)
    message_ref[:, 0, :] = jnp.broadcast_to(sums, (N_DP, LANES))
    message_ref[:, 1, :] = mm_tall(hits16, high) + mm_tall(hits16, low)


def backward_body(
    cols_ref, states_ref, hidden_ref, slope_ref, weights_ref, hidden_2_ref, slope_2_ref, weights_2_ref, unit_ref, signal_ref,
    scale_ref, gain_ref, head_ref, keep_ref, send_ref,
):
    unit = unit_ref[...]
    high, low = split(signal_ref[...])
    d_unit = gain_ref[...] * (mm_flip(high, head_ref[...]) + mm_flip(low, head_ref[...]))
    along = jnp.mean(d_unit * unit, -1, keepdims=True)
    d_total = scale_ref[:, 0:1] * (d_unit - jnp.mean(d_unit, -1, keepdims=True) - unit * along)
    d_out = d_total.astype(bf16)
    states = states_ref[...]
    dest = jnp.broadcast_to(cols_ref[:, 2:3], (ROWS, LANES)).astype(f32).astype(bf16)
    for ref, hidden, slope, weights in (
        (send_ref, hidden_2_ref, slope_2_ref, weights_2_ref),
        (keep_ref, hidden_ref, slope_ref, weights_ref),
    ):
        w_down = jnp.concatenate([weights[m, 1] for m in range(N_X)], 0)
        ref[:, 0:WIDTH] = (mm_flip(d_out, w_down) * slope[...]).astype(bf16)
        ref[:, WIDTH : 2 * WIDTH] = hidden[...]
        ref[:, 2 * WIDTH : 3 * WIDTH] = states
        ref[:, 3 * WIDTH : 4 * WIDTH] = d_out
        ref[:, 4 * WIDTH :] = dest


def one_term(ref, got_ref, k):
    sums = jnp.sum(got_ref[:, 0, :], 0, keepdims=True)
    inverse = 1.0 / jnp.maximum(sums, 1.0)
    hits = ref[:, 4 * WIDTH :].astype(f32) == iota((ROWS, LANES), 1).astype(f32)
    factor = jnp.sum(jnp.where(hits, inverse, 0.0), -1, keepdims=True)
    scaled = (ref[:, (k + 2) * WIDTH : (k + 3) * WIDTH].astype(f32) * factor).astype(bf16)
    return mm_tall(ref[:, k * WIDTH : (k + 1) * WIDTH], scaled)


def first_body(keep_ref, got_ref, sum_ref, loss_ref):
    loss_ref[...] = got_ref[:, 1, :]
    for k in range(2):
        sum_ref[:, k * WIDTH : (k + 1) * WIDTH] = one_term(keep_ref, got_ref, k)


def term_body(sum_ref, other_ref, got_ref, term_ref):
    for k in range(2):
        lanes = slice(k * WIDTH, (k + 1) * WIDTH)
        grad = (sum_ref[:, lanes] + one_term(other_ref, got_ref, k)).astype(bf16)
        for m in range(N_X):
            for x in range(N_X):
                start = m * LANES + x * 32
                term_ref[x, m * 32 : (m + 1) * 32, lanes] = grad[start : start + 32]


def middle_body(got_ref, out_ref, held_ref):
    total = got_ref[0].astype(f32)
    for k in range(1, N_X):
        total = total + got_ref[k].astype(f32)
    for m in range(N_X):
        for r in range(2):
            for c in range(8):
                block = total[m * 32 + r * 16 : m * 32 + (r + 1) * 16, c * LANES : (c + 1) * LANES]
                held_ref[m * 16 : (m + 1) * 16, r * 8 + c, :] = block
    out_ref[...] = held_ref[...].astype(bf16)


def final_body(got_ref, momentum_ref, out_ref):
    total = jnp.sum(got_ref[...].astype(f32), 0)
    for r in range(2):
        for c in range(8):
            lanes = slice(c * LANES, (c + 1) * LANES)
            out_ref[r : r + 1, lanes] = 0.9 * momentum_ref[r : r + 1, lanes] + total[r * 8 + c : r * 8 + c + 1]


def constants():
    row = np.arange(ROWS)
    inside = row % PAD
    group = row // PAD * 6 + inside // (STEPS + 1)
    same = (group[:, None] == group[None, :]) & (row[:, None] <= row[None, :])
    valid = (inside < SEG) & (inside % (STEPS + 1) < STEPS)
    beam = np.where(valid, row // PAD * BEAM + inside // (STEPS + 1), -1)
    beams = beam[:, None] == np.arange(LANES)[None, :]
    return jnp.asarray(same, bf16), jnp.asarray(beams, f32)


def per_device(
    tokens, accept, dest, mem_keys, mem_values, embed, w_query, w_key, w_value, w_self, cross_query, cross_out,
    gain_self, gain_cross, w_in, w_down, gain_ff, head, momentum,
):
    same, beams = constants()
    core = lax.axis_index("core").astype(jnp.int32).reshape(1)
    swap = [(0, 1), (1, 0)]
    half = (ROWS, HALF)

    mine = call(
        prepare_body,
        [((N_X, 2, LANES, WIDTH), bf16)],
        scratch=[pltpu.VMEM((WIDTH, PART), bf16), pltpu.VMEM((PART, WIDTH), bf16), pltpu.SemaphoreType.DMA((2,))],
        n_smem=1, n_any=2, cost=1, name="prepare",
    )(core, w_in, w_down)
    own_w = lax.all_to_all(mine, "x", 0, 0)

    flat = jnp.pad(tokens.reshape(2, SEG), ((0, 0), (0, PAD - SEG))).reshape(ROWS)
    nexts = jnp.concatenate([flat[1:], flat[:1]])
    place = jnp.pad(dest.reshape(2, BEAM, STEPS), ((0, 0), (0, 0), (0, 1)), constant_values=-1).reshape(2, SEG)
    place = jnp.pad(place, ((0, 0), (0, PAD - SEG)), constant_values=-1).reshape(ROWS)
    rows = jnp.stack([flat, nexts, place, place, place, place, place, place])
    cols = rows.T
    states, at_rank, done = call(
        attend_body,
        [((ROWS, WIDTH), bf16), ((ROWS, LANES), f32), ((16, LANES), bf16)],
        scratch=[
            pltpu.VMEM((ROWS, WIDTH), bf16),
            pltpu.VMEM((6, WIDTH, WIDTH), bf16),
            pltpu.SemaphoreType.DMA((6,)),
        ],
        n_in=8, n_any=6, cost=8, name="attend",
    )(
        cols, rows, same, mem_keys, mem_values, embed, gain_self.reshape(1, WIDTH), gain_cross.reshape(1, WIDTH),
        w_query, w_key, w_value, w_self, cross_query, cross_out,
    )
    own_w, done = lax.optimization_barrier((own_w, done))
    other_w = lax.ppermute(own_w, "core", swap)
    hidden, slope, partial = call(
        own_body, [(half, bf16), (half, f32), ((ROWS, WIDTH), f32)], n_in=3, cost=2, name="own"
    )(states, own_w, done)
    gain = gain_ff.reshape(1, WIDTH)
    head = jnp.pad(head, ((0, 0), (0, LANES - VOCAB)))
    message, hidden_2, slope_2, unit, signal, scale = call(
        forward_body,
        [
            ((N_DP, 2, LANES), f32),
            (half, bf16),
            (half, f32),
            ((ROWS, WIDTH), f32),
            ((ROWS, LANES), f32),
            ((ROWS, LANES), f32),
        ],
        n_smem=1, n_in=8, cost=5, name="forward",
    )(accept, cols, at_rank, beams, states, partial, other_w, gain, head)
    got = lax.all_to_all(message, DP, 0, 0)
    keep, send = call(
        backward_body, [((ROWS, PAY), bf16), ((ROWS, PAY), bf16)], n_in=13, cost=4, name="backward"
    )(cols, states, hidden, slope, own_w, hidden_2, slope_2, other_w, unit, signal, scale, gain, head)
    other = lax.ppermute(send, "core", swap)
    first, loss = call(
        first_body, [((HALF, 2 * WIDTH), f32), ((N_DP, LANES), f32)], n_in=2, cost=20, name="first"
    )(keep, got)
    term = call(term_body, [((N_X, LANES, 2 * WIDTH), bf16)], n_in=3, cost=4, name="term")(first, other, got)
    got = lax.all_to_all(term, "x", 0, 0)
    middle = call(
        middle_body, [((64, 16, LANES), bf16)], scratch=[pltpu.VMEM((64, 16, LANES), f32)], n_in=1, cost=1, name="middle"
    )(got)
    got = lax.all_to_all(middle, ("z", "y"), 0, 0)
    out = call(final_body, [((2, 2 * WIDTH), f32)], n_in=2, cost=1, name="final")(got, momentum)
    return out, loss[:, :CAP].reshape(1, N_DP * CAP)


def solution(mesh):
    n_dp, n_mp = mesh.devices.shape
    side = int(np.sqrt(n_dp // 2))
    fine = Mesh(mesh.devices.reshape(side, side, 2, n_mp), EVERY)
    placed = (
        P(EVERY, None, None),
        P(EVERY),
        P(EVERY, None),
        P(EVERY, None, None),
        P(EVERY, None, None),
        P(),
        P(),
        P(),
        P(),
        P(),
        P(),
        P(),
        P(),
        P(),
        P(None, "x"),
        P("x", None),
        P(),
        P(),
        P(EVERY, None),
    )
    return jax.shard_map(
        per_device,
        mesh=fine,
        in_specs=placed,
        out_specs=(P(EVERY, None), P(EVERY, None)),
        check_vma=False,
    )
```

time: 114 us -> 106 us (0.930)
  blocking collectives: 62.5 us -> 45.4 us
  starting transfers between devices: 14.1 us -> 19 us
  Pallas kernels: 11.7 us -> 14.1 us
  local copies, waits for them, and re-layouts: 10.3 us -> 11.9 us
    all_to_all x1 -> x0, blocking collectives: 15.3 us -> none  [per_device(): got_w = lax.all_to_all(mine, 'x', 0, 0)]
    all_to_all x0 -> x1, starting transfers between devices: none -> 4.99 us  [per_device(): own_w = lax.all_to_all(mine, 'x', 0, 0)]
    pallas_call x5 -> x7, Pallas kernels: 9.8 us -> 12.2 us  [the longest x1 4.41 us: per_device(): call(attend_body, [((ROWS, WIDTH), bf16), ((ROWS, LANES), f32), ((16, LAN...]
    all_to_all x1, blocking collectives: 30 us -> 28.1 us  [per_device(): got = lax.all_to_all(message, DP, 0, 0)]
    unnamed x44 -> x46, local copies, waits for them, and re-layouts: 8.2 us -> 9.78 us
  transfers between devices with their start and end apart: 3 -> 4, of which waited for: 1 -> 1; matrix products, arithmetic and copies ran while one was open for 5% -> 6% of each run, Pallas kernels for 3% -> 6%
where the time goes in v3:
time: 106 us; the launch traced here: 104 us
  blocking collectives  45.4 us (43%)
  starting transfers between devices  19 us (18%)
  Pallas kernels  14.1 us (13%)
  local copies, waits for them, and re-layouts  11.9 us (11%)
  waiting for transfers between devices  11.7 us (11%)
    all_to_all x1, blocking collectives, per_device(): got = lax.all_to_all(message, DP, 0, 0)  28.1 us
    all_to_all x1, blocking collectives, per_device(): got = lax.all_to_all(term, 'x', 0, 0)  17.2 us
    all_to_all x1, waiting for transfers between devices, per_device(): got = lax.all_to_all(middle, ('z', 'y'), 0, 0)  11.7 us
    unnamed x46, local copies, waits for them, and re-layouts  9.78 us
    ppermute x1, starting transfers between devices, per_device(): other_w = lax.ppermute(own_w, 'core', swap)  7.47 us
    all_to_all x1, starting transfers between devices, per_device(): own_w = lax.all_to_all(mine, 'x', 0, 0)  4.99 us
    all_to_all x1, starting transfers between devices, per_device(): got = lax.all_to_all(middle, ('z', 'y'), 0, 0)  4.62 us
    pallas_call x1, Pallas kernels, per_device(): call(attend_body, [((ROWS, WIDTH), bf16), ((ROWS, LANES), f32), ((16, LAN...  4.41 us
  transfers between devices with their start and end apart: 4, of which 1 were waited for; matrix products, arithmetic and copies ran while one was open for 6% of the time, Pallas kernels for 6%

profile of v3, /device:TPU:1, one launch (start us, length us, event | category | flops | bytes accessed | tf_op | source)
XLA Modules:
  0.0 103.7 jit_solution(12807085357569639763)
XLA Ops:
  0.6 0.0 copy-start.6
  0.6 0.9 copy-done.6
  1.6 0.9 copy-done.7
  2.5 1.5 %prepare.1 = bf16[4,2,128,512]{3,2,1,0:T(8,128)(2,1)} custom-call(s32[1]{0:T(128)} %bitcast.3.core_ref, bf16[512,256]{1,0:T(8,128)(2,1)S(1)} %copy-done.6, bf16[256,512]{1,0:T(8,128)(2,1)S(1)} %copy-done.7), custom_call_target="tpu_custom_call" | custom-call | flops 500000000 | bytes 2000000 | tf_op jit(solution)/shard_map/prepare/pallas_call | solution.py:297
  4.0 0.0 copy-start.20
  4.0 0.0 copy-start
  4.1 0.0 copy-start.1
  4.1 0.0 copy-start.2
  4.1 0.0 copy-start.3
  4.1 0.0 copy-start.8
  4.1 0.0 copy-start.10
  4.1 0.0 copy-start.11
  4.1 5.0 %all-to-all-start = ((bf16[4,2,128,512]{3,2,1,0:T(8,128)(2,1)}), bf16[4,2,128,512]{3,2,1,0:T(8,128)(2,1)S(1)}, u32[]{:S(2)}, u32[]{:S(2)}) async-start(bf16[4,2,128,512]{3,2,1,0:T(8,128)(2,1)} %prepare.1), calls=%async_computation | async-start | bytes 2097152 | tf_op jit(solution)/shard_map/all_to_all | solution.py:303
  9.1 0.0 copy-done.19
  9.1 0.1 reshape.31
  9.2 0.1 stack_reshape.4
  9.3 0.1 reshape.32
  9.4 0.5 slice.10
  9.9 0.1 slice.9
  10.0 0.0 copy-done.20
  10.0 0.1 reshape.33
  10.1 0.1 reshape.34
  10.2 0.1 stack_reshape.5
  10.3 0.7 pad_add_fusion
  11.0 0.1 copy.41
  11.2 1.0 copy.42.keys_ref
  12.2 1.0 copy.43.values_ref
  13.2 0.0 copy-done
  13.2 0.0 copy-done.1
  13.2 0.0 copy-done.2
  13.2 0.0 copy-done.3
  13.2 0.0 copy-done.8
  13.2 0.0 copy-done.10
  13.2 0.0 copy-done.11
  13.2 0.0 copy-start.4
  13.3 1.0 copy-done.4
  14.3 1.0 %copy-done.5 = bf16[512,512]{1,0:T(8,128)(2,1)S(1)} copy-done((bf16[512,512]{1,0:T(8,128)(2,1)S(1)}, bf16[512,512]{1,0:T(8,128)(2,1)}, u32[]{:S(2)}) %copy-start.5) | copy-done | bytes 524312
  15.3 0.9 copy-done.14
  16.3 4.4 %attend.1 = (bf16[320,512]{1,0:T(8,128)(2,1)S(1)}, f32[320,128]{1,0:T(8,128)S(1)}, bf16[16,128]{1,0:T(8,128)(2,1)S(1)}) custom-call(s32[320,8]{1,0:T(8,128)S(1)} %bitcast.6, s32[8,320]{1,0:T(8,128)S(1)} %stack.7.rows_ref, bf16[320,320]{1,0:T(8,128)(2,1)S(1)} %copy-done.14, bf16[2,150,512]{2,1,0:T(8,128)(2,1)S(1)} %copy.42.keys_ref, ...), custom_call_target="tpu_custom_call" | custom-call | flops 4000000000 | bytes 16000000 | tf_op jit(solution)/shard_map/attend/pallas_call | solution.py:311
  20.7 0.0 copy-start.16
  20.7 0.7 copy-done.16
  21.4 0.0 all-to-all-done.weights_ref
  21.4 7.5 %collective-permute-start = (bf16[4,2,128,512]{3,2,1,0:T(8,128)(2,1)S(1)}, bf16[4,2,128,512]{3,2,1,0:T(8,128)(2,1)S(1)}, u32[]{:S(2)}, u32[]{:S(2)}) collective-permute-start(bf16[4,2,128,512]{3,2,1,0:T(8,128)(2,1)S(1)} %all-to-all-done.weights_ref), channel_id=1, source_target_pairs={{0,4},{4,0},{1,5},{5,1},{2,6},{6,2},{3,7},{7,3},{8,12},{12,8},{9,1... | collective-permute-start | bytes 3145736 | tf_op jit(solution)/shard_map/ppermute | solution.py:325
  28.9 0.9 copy.44
  29.8 1.0 copy-done.17
  30.8 0.8 own.1
  31.7 0.0 collective-permute-done.weights_ref.weights_2_ref
  31.7 0.0 copy-done.12
  31.7 0.0 copy-done.13
  31.7 0.1 copy-done.15
  31.8 0.1 copy-done.18
  31.9 2.7 %forward.1 = (f32[128,2,128]{2,1,0:T(2,128)S(1)}, bf16[320,512]{1,0:T(8,128)(2,1)S(1)}, f32[320,512]{1,0:T(8,128)S(1)}, f32[320,512]{1,0:T(8,128)S(1)}, f32[320,128]{1,0:T(8,128)S(1)}, /*index=5*/f32[320,128]{1,0:T(8,128)S(1)}) custom-call(s32[2]{0:T(128)S(1)} %copy-done.13, s32[320,8]{1,0:T(8,128)S(1)} %bitcast.7, ...), custom_call_target="tpu_custom_call" | custom-call | flops 2500000000 | bytes 10000000 | tf_op jit(solution)/shard_map/forward/pallas_call | solution.py:331
  34.6 1.0 %backward.1 = (bf16[320,2176]{1,0:T(8,128)(2,1)S(1)}, bf16[320,2176]{1,0:T(8,128)(2,1)S(1)}) custom-call(s32[320,8]{1,0:T(8,128)S(1)} %bitcast.8, bf16[320,512]{1,0:T(8,128)(2,1)S(1)} %copy-done.18, bf16[320,512]{1,0:T(8,128)(2,1)S(1)} %get-tuple-element.24.hidden_ref, f32[320,512]{1,0:T(8,128)S(1)} %get-tuple-element.25.slope_ref, ...), custom_call_target="tpu_custom_call" | custom-call | flops 2000000000 | bytes 8000000 | tf_op jit(solution)/shard_map/backward/pallas_call | solution.py:344
  35.7 1.9 %collective-permute-start.1 = (bf16[320,2176]{1,0:T(8,128)(2,1)S(1)}, bf16[320,2176]{1,0:T(8,128)(2,1)S(1)}, u32[]{:S(2)}, u32[]{:S(2)}) collective-permute-start(bf16[320,2176]{1,0:T(8,128)(2,1)S(1)} %get-tuple-element.36), channel_id=1, source_target_pairs={{0,4},{4,0},{1,5},{5,1},{2,6},{6,2},{3,7},{7,3},{8,12},{12,8},{9,1... | collective-permute-start | bytes 4177928 | tf_op jit(solution)/shard_map/ppermute | solution.py:347
  37.6 28.1 %all_to_all.20.got_ref = f32[128,2,128]{2,1,0:T(2,128)S(1)} all-to-all(f32[128,2,128]{2,1,0:T(2,128)S(1)} %get-tuple-element.34), channel_id=1, replica_groups=mesh['z'=8,'y'=8,'core'=2,'x'=4] {'z','y','core'}, dimensions={0} | all-to-all | bytes 262144 | tf_op jit(solution)/shard_map/all_to_all | solution.py:343
  65.7 0.9 first.1
  66.6 0.0 collective-permute-done.1.other_ref
  66.6 0.9 term.1
  67.5 17.2 %all_to_all.21.got_ref = bf16[4,128,1024]{2,1,0:T(8,128)(2,1)S(1)} all-to-all(bf16[4,128,1024]{2,1,0:T(8,128)(2,1)S(1)} %term.1), channel_id=1, replica_groups=mesh['z'=8,'y'=8,'core'=2,'x'=4] {'x'}, dimensions={0} | all-to-all | bytes 2097152 | tf_op jit(solution)/shard_map/all_to_all | solution.py:352
  84.7 1.2 %middle.1 = bf16[64,16,128]{2,1,0:T(8,128)(2,1)} custom-call(bf16[4,128,1024]{2,1,0:T(8,128)(2,1)S(1)} %all_to_all.21.got_ref), custom_call_target="tpu_custom_call" | custom-call | flops 500000000 | bytes 2000000 | tf_op jit(solution)/shard_map/middle/pallas_call | solution.py:353
  85.9 4.6 %all-to-all-start.3 = ((bf16[64,16,128]{2,1,0:T(8,128)(2,1)}), bf16[64,16,128]{2,1,0:T(8,128)(2,1)S(1)}, u32[]{:S(2)}, u32[]{:S(2)}) async-start(bf16[64,16,128]{2,1,0:T(8,128)(2,1)} %middle.1), calls=%async_computation.3 | async-start | bytes 524288 | tf_op jit(solution)/shard_map/all_to_all | solution.py:356
  90.5 0.8 reshape.39
  91.3 11.7 %all-to-all-done.3.got_ref = bf16[64,16,128]{2,1,0:T(8,128)(2,1)S(1)} async-done(((bf16[64,16,128]{2,1,0:T(8,128)(2,1)}), bf16[64,16,128]{2,1,0:T(8,128)(2,1)S(1)}, u32[]{:S(2)}, u32[]{:S(2)}) %all-to-all-start.3) | async-done | bytes 262176 | tf_op jit(solution)/shard_map/all_to_all | solution.py:356
  103.0 0.7 final.1
  (19 shorter events, 0.1 us)
Async XLA Ops:
  0.6 1.0 copy-start.6
  1.6 0.9 copy-start.7
  2.5 6.6 %copy-start.19 = (s32[2,5,31]{2,0,1:T(2,128)S(1)}, s32[2,5,31]{2,0,1:T(2,128)}, u32[]{:S(2)}) copy-start(s32[2,5,31]{2,0,1:T(2,128)} %param.21) | copy-start | bytes 3724
  4.0 5.9 %copy-start.20 = (s32[300,1]{0,1:T(1,128)S(1)}, s32[300,1]{0,1:T(1,128)}, u32[]{:S(2)}) copy-start(s32[300,1]{0,1:T(1,128)} %param.23) | copy-start | bytes 3604
  4.0 9.1 %copy-start = (bf16[512,512]{1,0:T(8,128)(2,1)S(1)}, bf16[512,512]{1,0:T(8,128)(2,1)}, u32[]{:S(2)}) copy-start(bf16[512,512]{1,0:T(8,128)(2,1)} %w_query_hbm.1) | copy-start | bytes 1572868
  4.1 9.1 %copy-start.1 = (bf16[512,512]{1,0:T(8,128)(2,1)S(1)}, bf16[512,512]{1,0:T(8,128)(2,1)}, u32[]{:S(2)}) copy-start(bf16[512,512]{1,0:T(8,128)(2,1)} %w_key_hbm.1) | copy-start | bytes 1572868
  4.1 9.1 %copy-start.2 = (bf16[512,512]{1,0:T(8,128)(2,1)S(1)}, bf16[512,512]{1,0:T(8,128)(2,1)}, u32[]{:S(2)}) copy-start(bf16[512,512]{1,0:T(8,128)(2,1)} %w_value_hbm.1) | copy-start | bytes 1572868
  4.1 9.1 %copy-start.3 = (bf16[512,512]{1,0:T(8,128)(2,1)S(1)}, bf16[512,512]{1,0:T(8,128)(2,1)}, u32[]{:S(2)}) copy-start(bf16[512,512]{1,0:T(8,128)(2,1)} %w_self_hbm.1) | copy-start | bytes 1572868
  4.1 9.1 %copy-start.8 = (bf16[28,512]{1,0:T(8,128)(2,1)S(1)}, bf16[28,512]{1,0:T(8,128)(2,1)}, u32[]{:S(2)}) copy-start(bf16[28,512]{1,0:T(8,128)(2,1)} %embed_ref.1) | copy-start | bytes 86020
  4.1 9.1 %copy-start.10 = (f32[512]{0:T(512)S(1)}, f32[512]{0:T(512)}, u32[]{:S(2)}) copy-start(f32[512]{0:T(512)} %param.33) | copy-start | bytes 6148
  4.1 9.1 %copy-start.11 = (f32[512]{0:T(512)S(1)}, f32[512]{0:T(512)}, u32[]{:S(2)}) copy-start(f32[512]{0:T(512)} %param.34) | copy-start | bytes 6148
  4.1 17.3 %all-to-all-start = ((bf16[4,2,128,512]{3,2,1,0:T(8,128)(2,1)}), bf16[4,2,128,512]{3,2,1,0:T(8,128)(2,1)S(1)}, u32[]{:S(2)}, u32[]{:S(2)}) async-start(bf16[4,2,128,512]{3,2,1,0:T(8,128)(2,1)} %prepare.1), calls=%async_computation | async-start | bytes 2097152 | tf_op jit(solution)/shard_map/all_to_all | solution.py:303
  13.2 1.0 %copy-start.4 = (bf16[512,512]{1,0:T(8,128)(2,1)S(1)}, bf16[512,512]{1,0:T(8,128)(2,1)}, u32[]{:S(2)}) copy-start(bf16[512,512]{1,0:T(8,128)(2,1)} %cross_query_hbm.1) | copy-start | bytes 1572868
  14.3 1.0 %copy-start.5 = (bf16[512,512]{1,0:T(8,128)(2,1)S(1)}, bf16[512,512]{1,0:T(8,128)(2,1)}, u32[]{:S(2)}) copy-start(bf16[512,512]{1,0:T(8,128)(2,1)} %cross_out_hbm.1) | copy-start | bytes 1572868
  15.3 0.9 copy-start.14
  20.7 0.7 copy-start.16
  21.4 10.2 %collective-permute-start = (bf16[4,2,128,512]{3,2,1,0:T(8,128)(2,1)S(1)}, bf16[4,2,128,512]{3,2,1,0:T(8,128)(2,1)S(1)}, u32[]{:S(2)}, u32[]{:S(2)}) collective-permute-start(bf16[4,2,128,512]{3,2,1,0:T(8,128)(2,1)S(1)} %all-to-all-done.weights_ref), channel_id=1, source_target_pairs={{0,4},{4,0},{1,5},{5,1},{2,6},{6,2},{3,7},{7,3},{8,12},{12,8},{9,1... | collective-permute-start | bytes 3145736 | tf_op jit(solution)/shard_map/ppermute | solution.py:325
  29.8 1.0 copy-start.17
  30.8 0.9 copy-start.12
  30.8 0.9 copy-start.13
  30.8 0.9 copy-start.15
  30.8 1.1 %copy-start.18 = (bf16[320,512]{1,0:T(8,128)(2,1)S(1)}, bf16[320,512]{1,0:T(8,128)(2,1)}, u32[]{:S(2)}) copy-start(bf16[320,512]{1,0:T(8,128)(2,1)} %copy-done.16) | copy-start | bytes 983044
  35.7 30.9 %collective-permute-start.1 = (bf16[320,2176]{1,0:T(8,128)(2,1)S(1)}, bf16[320,2176]{1,0:T(8,128)(2,1)S(1)}, u32[]{:S(2)}, u32[]{:S(2)}) collective-permute-start(bf16[320,2176]{1,0:T(8,128)(2,1)S(1)} %get-tuple-element.36), channel_id=1, source_target_pairs={{0,4},{4,0},{1,5},{5,1},{2,6},{6,2},{3,7},{7,3},{8,12},{12,8},{9,1... | collective-permute-start | bytes 4177928 | tf_op jit(solution)/shard_map/ppermute | solution.py:347
  84.7 18.3 %copy-start.9 = (f32[2,1024]{1,0:T(2,128)S(1)}, f32[2,1024]{1,0:T(2,128)}, u32[]{:S(2)}) copy-start(f32[2,1024]{1,0:T(2,128)} %momentum_ref.1) | copy-start | bytes 24580
  85.9 17.1 %all-to-all-start.3 = ((bf16[64,16,128]{2,1,0:T(8,128)(2,1)}), bf16[64,16,128]{2,1,0:T(8,128)(2,1)S(1)}, u32[]{:S(2)}, u32[]{:S(2)}) async-start(bf16[64,16,128]{2,1,0:T(8,128)(2,1)} %middle.1), calls=%async_computation.3 | async-start | bytes 524288 | tf_op jit(solution)/shard_map/all_to_all | solution.py:356

commit v4 on v3

--- a/solution.py
+++ b/solution.py
@@ -60,11 +60,11 @@
     return high, (v - high.astype(f32)).astype(bf16)
 
 
-def call(body, outs, scratch=(), cost=4.0, n_smem=0, n_in=0, n_any=0, name=None):
+def call(body, outs, scratch=(), cost=4.0, n_smem=0, n_in=0, n_any=0, out_hbm=False, limit=16 << 20, name=None):
     smem = [pl.BlockSpec(memory_space=pltpu.SMEM)] * n_smem
-    vmem = [pl.BlockSpec(memory_space=pltpu.VMEM)] * n_in + [pl.BlockSpec(memory_space=pl.ANY)] * n_any
+    vmem = [pl.BlockSpec(memory_space=pltpu.VMEM)] * n_in + [pl.BlockSpec(memory_space=pltpu.HBM)] * n_any
     shapes = [jax.ShapeDtypeStruct(s, d) for s, d in outs]
-    specs = [pl.BlockSpec(memory_space=pltpu.VMEM)] * len(outs)
+    specs = [pl.BlockSpec(memory_space=pltpu.HBM if out_hbm else pltpu.VMEM)] * len(outs)
     single = len(outs) == 1
     return pl.pallas_call(
         body,
@@ -72,16 +72,16 @@
         in_specs=smem + vmem,
         out_specs=specs[0] if single else specs,
         scratch_shapes=list(scratch),
-        compiler_params=pltpu.CompilerParams(vmem_limit_bytes=16 * 1024 * 1024),
+        compiler_params=pltpu.CompilerParams(vmem_limit_bytes=limit),
         cost_estimate=pl.CostEstimate(flops=int(cost * 5e8), bytes_accessed=int(cost * 2e6), transcendentals=0),
         name=name,
     )
 
 
-def prepare_body(core_ref, w_in_ref, w_down_ref, out_ref, w_in, w_down, sems):
+def prepare_body(core_ref, w_in_hbm, w_down_hbm, out_hbm, w_in, w_down, mine, sems):
     loads = [
-        pltpu.make_async_copy(w_in_ref, w_in, sems.at[0]),
-        pltpu.make_async_copy(w_down_ref, w_down, sems.at[1]),
+        pltpu.make_async_copy(w_in_hbm, w_in, sems.at[0]),
+        pltpu.make_async_copy(w_down_hbm, w_down, sems.at[1]),
     ]
     for load in loads:
         load.start()
@@ -89,16 +89,18 @@
     wanted = (place % 16) * 16 + core_ref[0] * 8 + place // 16
     chosen = (unit == wanted).astype(bf16)
     loads[0].wait()
-    mine_in = lax.dot_general(chosen, w_in[...], (((0,), (1,)), ((), ())), preferred_element_type=f32).astype(bf16)
+    mine[0] = lax.dot_general(chosen, w_in[...], (((0,), (1,)), ((), ())), preferred_element_type=f32).astype(bf16)
     loads[1].wait()
-    mine_down = mm_tall(chosen, w_down[...]).astype(bf16)
-    for k in range(N_X):
-        out_ref[k, 0] = mine_in
-        out_ref[k, 1] = mine_down
+    mine[1] = mm_tall(chosen, w_down[...]).astype(bf16)
+    stores = [pltpu.make_async_copy(mine, out_hbm.at[k], sems.at[2 + k]) for k in range(N_X)]
+    for store in stores:
+        store.start()
+    for store in stores:
+        store.wait()
 
 
 def attend_body(
-    cols_ref, rows_ref, same_ref, keys_ref, values_ref, embed_ref, gain_self_ref, gain_cross_ref, w_query_hbm, w_key_hbm,
+    cols_ref, rows_ref, keys_ref, values_ref, embed_ref, gain_self_ref, gain_cross_ref, w_query_hbm, w_key_hbm,
     w_value_hbm, w_self_hbm, cross_query_hbm, cross_out_hbm, states_ref, at_rank_ref, done_ref, ctx_ref, held, sems,
 ):
     sources = (w_query_hbm, w_key_hbm, w_value_hbm, w_self_hbm, cross_query_hbm, cross_out_hbm)
@@ -109,6 +111,8 @@
     hits = cols_ref[:, 2:3] == lane
     earlier = (iota((ROWS, ROWS), 0) > iota((ROWS, ROWS), 1)).astype(bf16)
     before = mm(earlier, hits.astype(bf16))
+    same = (beam_of(0) == beam_of(1)) & (iota((ROWS, ROWS), 0) <= iota((ROWS, ROWS), 1))
+    same = same.astype(bf16)
     rank = jnp.sum(jnp.where(hits, before, 0.0), -1, keepdims=True).astype(jnp.int32)
     at_rank_ref[...] = (rank == lane).astype(f32)
     embed = embed_ref[...]
@@ -126,7 +130,7 @@
     key_blocks = jnp.where(own, jnp.concatenate([keyed] * HEADS, 0), 0.0).astype(bf16)
     value_blocks = jnp.where(own, jnp.concatenate([valued] * HEADS, 0), 0.0).astype(bf16)
     scores = (mm_flip(key_blocks, query) * 0.125).reshape(HEADS, 32, ROWS)
-    counts = mm(picks_t, same_ref[...])[None]
+    counts = mm(picks_t, same)[None]
     scores = jnp.where(counts > 0.0, scores, -1e30)
     probs = jnp.exp(scores - jnp.max(scores, 1, keepdims=True)) * counts
     probs = probs / jnp.sum(probs, 1, keepdims=True)
@@ -154,6 +158,21 @@
     done_ref[...] = states[:16, :LANES]
 
 
+def beam_of(dim):
+    shape = (ROWS, 1) if dim == 0 else (1, ROWS)
+    row = iota(shape, dim)
+    second = (row >= PAD).astype(jnp.int32)
+    inside = row - second * PAD
+    beam = second * (BEAM + 1)
+    for k in range(1, BEAM + 1):
+        beam = beam + (inside >= k * (STEPS + 1)).astype(jnp.int32)
+    return beam
+
+
+def wide_head(head_ref):
+    return mm((iota((LANES, VOCAB), 0) == iota((LANES, VOCAB), 1)).astype(bf16), head_ref[...]).astype(bf16)
+
+
 def half_forward(states, weights_ref, hidden_ref, slope_ref):
     w_in = jnp.concatenate([weights_ref[m, 0] for m in range(N_X)], 0)
     w_down = jnp.concatenate([weights_ref[m, 1] for m in range(N_X)], 0)
@@ -171,14 +190,15 @@
 
 
 def forward_body(
-    accept_ref, cols_ref, at_rank_ref, beams_ref, states_ref, partial_ref, weights_ref, gain_ref, head_ref,
+    accept_ref, cols_ref, at_rank_ref, states_ref, partial_ref, weights_ref, gain_ref, head_ref,
     message_ref, hidden_ref, slope_ref, unit_ref, signal_ref, scale_ref,
 ):
     unit, scale = norm_parts(partial_ref[...] + half_forward(states_ref[...], weights_ref, hidden_ref, slope_ref))
     unit_ref[...] = unit
     scale_ref[...] = jnp.broadcast_to(scale, (ROWS, LANES))
     high, low = split(unit * gain_ref[...])
-    logits = mm(high, head_ref[...]) + mm(low, head_ref[...])
+    head = wide_head(head_ref)
+    logits = mm_flip(high, head) + mm_flip(low, head)
     lane = iota((ROWS, LANES), 1)
     logits = jnp.where(lane < VOCAB, logits, -1e30)
     top = jnp.max(logits, -1, keepdims=True)
@@ -186,7 +206,14 @@
     mass = jnp.sum(grown, -1, keepdims=True)
     is_label = cols_ref[:, 1:2] == lane
     taken = jnp.sum(jnp.where(is_label, logits, 0.0), -1, keepdims=True) - top - jnp.log(mass)
-    beams = beams_ref[...]
+    beam = beam_of(0)
+    row = iota((ROWS, 1), 0)
+    step = row - (row >= PAD).astype(jnp.int32) * PAD
+    beam = beam - (row >= PAD).astype(jnp.int32)
+    for k in range(1, BEAM + 1):
+        step = step - (step >= STEPS + 1).astype(jnp.int32) * (STEPS + 1)
+    inside = jnp.where(row >= PAD, row - PAD, row)
+    beams = jnp.where((beam == lane) & (step < STEPS) & (inside < SEG), 1.0, 0.0)
     score = jnp.sum(beams * taken, 0, keepdims=True) / STEPS
     place = iota((1, LANES), 1)
     shares = jnp.zeros((1, LANES), f32)
@@ -211,7 +238,8 @@
 ):
     unit = unit_ref[...]
     high, low = split(signal_ref[...])
-    d_unit = gain_ref[...] * (mm_flip(high, head_ref[...]) + mm_flip(low, head_ref[...]))
+    head = wide_head(head_ref)
+    d_unit = gain_ref[...] * (mm(high, head) + mm(low, head))
     along = jnp.mean(d_unit * unit, -1, keepdims=True)
     d_total = scale_ref[:, 0:1] * (d_unit - jnp.mean(d_unit, -1, keepdims=True) - unit * along)
     d_out = d_total.astype(bf16)
@@ -274,22 +302,10 @@
             out_ref[r : r + 1, lanes] = 0.9 * momentum_ref[r : r + 1, lanes] + total[r * 8 + c : r * 8 + c + 1]
 
 
-def constants():
-    row = np.arange(ROWS)
-    inside = row % PAD
-    group = row // PAD * 6 + inside // (STEPS + 1)
-    same = (group[:, None] == group[None, :]) & (row[:, None] <= row[None, :])
-    valid = (inside < SEG) & (inside % (STEPS + 1) < STEPS)
-    beam = np.where(valid, row // PAD * BEAM + inside // (STEPS + 1), -1)
-    beams = beam[:, None] == np.arange(LANES)[None, :]
-    return jnp.asarray(same, bf16), jnp.asarray(beams, f32)
-
-
 def per_device(
     tokens, accept, dest, mem_keys, mem_values, embed, w_query, w_key, w_value, w_self, cross_query, cross_out,
     gain_self, gain_cross, w_in, w_down, gain_ff, head, momentum,
 ):
-    same, beams = constants()
     core = lax.axis_index("core").astype(jnp.int32).reshape(1)
     swap = [(0, 1), (1, 0)]
     half = (ROWS, HALF)
@@ -297,13 +313,19 @@
     mine = call(
         prepare_body,
         [((N_X, 2, LANES, WIDTH), bf16)],
-        scratch=[pltpu.VMEM((WIDTH, PART), bf16), pltpu.VMEM((PART, WIDTH), bf16), pltpu.SemaphoreType.DMA((2,))],
-        n_smem=1, n_any=2, cost=1, name="prepare",
+        scratch=[
+            pltpu.VMEM((WIDTH, PART), bf16),
+            pltpu.VMEM((PART, WIDTH), bf16),
+            pltpu.VMEM((2, LANES, WIDTH), bf16),
+            pltpu.SemaphoreType.DMA((2 + N_X,)),
+        ],
+        n_smem=1, n_any=2, out_hbm=True, limit=63_300_000, cost=1, name="prepare",
     )(core, w_in, w_down)
     own_w = lax.all_to_all(mine, "x", 0, 0)
 
-    flat = jnp.pad(tokens.reshape(2, SEG), ((0, 0), (0, PAD - SEG))).reshape(ROWS)
-    nexts = jnp.concatenate([flat[1:], flat[:1]])
+    flat = tokens.reshape(2, SEG)
+    nexts = lax.pad(flat, jnp.int32(0), ((0, 0, 0), (-1, PAD - SEG + 1, 0))).reshape(ROWS)
+    flat = jnp.pad(flat, ((0, 0), (0, PAD - SEG))).reshape(ROWS)
     place = jnp.pad(dest.reshape(2, BEAM, STEPS), ((0, 0), (0, 0), (0, 1)), constant_values=-1).reshape(2, SEG)
     place = jnp.pad(place, ((0, 0), (0, PAD - SEG)), constant_values=-1).reshape(ROWS)
     rows = jnp.stack([flat, nexts, place, place, place, place, place, place])
@@ -316,9 +338,9 @@
             pltpu.VMEM((6, WIDTH, WIDTH), bf16),
             pltpu.SemaphoreType.DMA((6,)),
         ],
-        n_in=8, n_any=6, cost=8, name="attend",
+        n_in=7, n_any=6, limit=61_300_000, cost=8, name="attend",
     )(
-        cols, rows, same, mem_keys, mem_values, embed, gain_self.reshape(1, WIDTH), gain_cross.reshape(1, WIDTH),
+        cols, rows, mem_keys, mem_values, embed, gain_self.reshape(1, WIDTH), gain_cross.reshape(1, WIDTH),
         w_query, w_key, w_value, w_self, cross_query, cross_out,
     )
     own_w, done = lax.optimization_barrier((own_w, done))
@@ -327,7 +349,7 @@
         own_body, [(half, bf16), (half, f32), ((ROWS, WIDTH), f32)], n_in=3, cost=2, name="own"
     )(states, own_w, done)
     gain = gain_ff.reshape(1, WIDTH)
-    head = jnp.pad(head, ((0, 0), (0, LANES - VOCAB)))
+    head = head.T
     message, hidden_2, slope_2, unit, signal, scale = call(
         forward_body,
         [
@@ -338,8 +360,8 @@
             ((ROWS, LANES), f32),
             ((ROWS, LANES), f32),
         ],
-        n_smem=1, n_in=8, cost=5, name="forward",
-    )(accept, cols, at_rank, beams, states, partial, other_w, gain, head)
+        n_smem=1, n_in=7, cost=5, name="forward",
+    )(accept, cols, at_rank, states, partial, other_w, gain, head)
     got = lax.all_to_all(message, DP, 0, 0)
     keep, send = call(
         backward_body, [((ROWS, PAY), bf16), ((ROWS, PAY), bf16)], n_in=13, cost=4, name="backward"

time: 106 us -> 104 us (0.981)
  local copies, waits for them, and re-layouts: 11.9 us -> 5.74 us
  Pallas kernels: 14.1 us -> 18.2 us
  blocking collectives: 45.4 us -> 46.8 us
    unnamed x46 -> x31, local copies, waits for them, and re-layouts: 9.78 us -> 3.53 us
    pallas_call x1, Pallas kernels: 4.41 us -> 7.42 us  [per_device(): call(attend_body, [((ROWS, WIDTH), bf16), ((ROWS, LANES), f32), ((16, LAN...]
    all_to_all x1, blocking collectives: 28.1 us -> 29.6 us  [per_device(): got = lax.all_to_all(message, DP, 0, 0)]
  transfers between devices with their start and end apart: 4 -> 4, of which waited for: 1 -> 1; matrix products, arithmetic and copies ran while one was open for 6% -> 4% of each run, Pallas kernels for 6% -> 9%
where the time goes in v4:
time: 104 us; the launch traced here: 103 us
  blocking collectives  46.8 us (45%)
  starting transfers between devices  19.4 us (19%)
  Pallas kernels  18.2 us (18%)
  waiting for transfers between devices  11.7 us (11%)
  local copies, waits for them, and re-layouts  5.74 us (6%)
    all_to_all x1, blocking collectives, per_device(): got = lax.all_to_all(message, DP, 0, 0)  29.6 us
    all_to_all x1, blocking collectives, per_device(): got = lax.all_to_all(term, 'x', 0, 0)  17.2 us
    all_to_all x1, waiting for transfers between devices, per_device(): got = lax.all_to_all(middle, ('z', 'y'), 0, 0)  11.7 us
    ppermute x1, starting transfers between devices, per_device(): other_w = lax.ppermute(own_w, 'core', swap)  7.83 us
    pallas_call x1, Pallas kernels, per_device(): call(attend_body, [((ROWS, WIDTH), bf16), ((ROWS, LANES), f32), ((16, LAN...  7.42 us
    all_to_all x1, starting transfers between devices, per_device(): own_w = lax.all_to_all(mine, 'x', 0, 0)  4.99 us
    all_to_all x1, starting transfers between devices, per_device(): got = lax.all_to_all(middle, ('z', 'y'), 0, 0)  4.61 us
    unnamed x31, local copies, waits for them, and re-layouts  3.53 us
  transfers between devices with their start and end apart: 4, of which 1 were waited for; matrix products, arithmetic and copies ran while one was open for 4% of the time, Pallas kernels for 9%

profile of v4, /device:TPU:1, one launch (start us, length us, event | category | flops | bytes accessed | tf_op | source)
XLA Modules:
  0.0 102.6 jit_solution(10836240042125519400)
XLA Ops:
  0.6 2.4 %prepare.1 = bf16[4,2,128,512]{3,2,1,0:T(8,128)(2,1)} custom-call(s32[1]{0:T(128)} %bitcast.3.core_ref, bf16[512,256]{1,0:T(8,128)(2,1)} %w_in_hbm.1, bf16[256,512]{1,0:T(8,128)(2,1)} %w_down_hbm.1), custom_call_target="tpu_custom_call" | custom-call | flops 500000000 | bytes 2000000 | tf_op jit(solution)/shard_map/prepare/pallas_call | solution.py:313
  3.1 0.0 copy-start.13
  3.1 0.0 copy-start.12
  3.1 0.0 copy-start.9
  3.1 0.0 copy-start.10
  3.1 5.0 %all-to-all-start = ((bf16[4,2,128,512]{3,2,1,0:T(8,128)(2,1)}), bf16[4,2,128,512]{3,2,1,0:T(8,128)(2,1)S(1)}, u32[]{:S(2)}, u32[]{:S(2)}) async-start(bf16[4,2,128,512]{3,2,1,0:T(8,128)(2,1)} %prepare.1), calls=%async_computation | async-start | bytes 2097152 | tf_op jit(solution)/shard_map/all_to_all | solution.py:324
  8.1 0.0 copy-done.13
  8.1 0.1 reshape.29
  8.2 0.1 reshape.30
  8.3 0.1 stack_reshape.16
  8.4 0.0 copy-done.12
  8.4 0.1 reshape.28
  8.5 0.1 pad_slice_fusion
  8.5 0.1 stack_reshape.7
  8.6 0.1 stack_reshape.6
  8.8 0.0 copy-start.11
  8.8 0.8 copy.37
  9.6 0.0 copy-done.9
  9.6 0.8 copy.38.keys_ref
  10.3 0.0 copy-done.10
  10.3 0.8 copy.39.values_ref
  11.1 0.0 copy-done.11
  11.1 7.4 %attend.1 = (bf16[320,512]{1,0:T(8,128)(2,1)}, f32[320,128]{1,0:T(8,128)}, bf16[16,128]{1,0:T(8,128)(2,1)}) custom-call(s32[320,8]{1,0:T(8,128)} %bitcast.7, s32[8,320]{1,0:T(8,128)} %copy-done.11, bf16[2,150,512]{2,1,0:T(8,128)(2,1)} %copy.38.keys_ref, bf16[2,150,512]{2,1,0:T(8,128)(2,1)} %copy.39.values_ref, bf16[28,512]{1,0:T(8,128)(2,1)} %embed_ref.1, ...), custom_call_target="tpu_custom_call" | custom-call | flops 4000000000 | bytes 16000000 | tf_op jit(solution)/shard_map/attend/pallas_call | solution.py:333
  18.6 0.0 all-to-all-done.weights_ref
  18.6 7.8 %collective-permute-start = (bf16[4,2,128,512]{3,2,1,0:T(8,128)(2,1)S(1)}, bf16[4,2,128,512]{3,2,1,0:T(8,128)(2,1)S(1)}, u32[]{:S(2)}, u32[]{:S(2)}) collective-permute-start(bf16[4,2,128,512]{3,2,1,0:T(8,128)(2,1)S(1)} %all-to-all-done.weights_ref), channel_id=1, source_target_pairs={{0,4},{4,0},{1,5},{5,1},{2,6},{6,2},{3,7},{7,3},{8,12},{12,8},{9,1... | collective-permute-start | bytes 3145736 | tf_op jit(solution)/shard_map/ppermute | solution.py:347
  26.4 0.0 copy-start.5
  26.4 1.0 copy-done.5
  27.4 0.0 copy-start.8
  27.4 0.7 copy-done.8
  28.1 0.0 copy-start
  28.1 0.0 copy-start.1
  28.1 0.0 copy-start.3
  28.1 0.0 copy-start.4
  28.1 0.0 copy-start.6
  28.1 0.0 copy-start.7
  28.1 0.8 own.1
  28.9 0.0 collective-permute-done.weights_ref.weights_2_ref
  29.0 0.0 copy-done
  29.0 0.0 copy-done.1
  29.0 0.0 copy-done.3
  29.0 0.0 copy-done.4
  29.0 0.2 copy-done.6
  29.2 0.0 copy-done.7
  29.2 2.7 %forward.1 = (f32[128,2,128]{2,1,0:T(2,128)S(1)}, bf16[320,512]{1,0:T(8,128)(2,1)S(1)}, f32[320,512]{1,0:T(8,128)S(1)}, f32[320,512]{1,0:T(8,128)S(1)}, f32[320,128]{1,0:T(8,128)S(1)}, /*index=5*/f32[320,128]{1,0:T(8,128)S(1)}) custom-call(s32[2]{0:T(128)S(1)} %copy-done.4, s32[320,8]{1,0:T(8,128)S(1)} %bitcast.8, f32[320,128]{1,0:T(8,128)S(1)} %copy-done.7, ...), custom_call_target="tpu_custom_call" | custom-call | flops 2500000000 | bytes 10000000 | tf_op jit(solution)/shard_map/forward/pallas_call | solution.py:353
  32.0 1.2 %backward.1 = (bf16[320,2176]{1,0:T(8,128)(2,1)S(1)}, bf16[320,2176]{1,0:T(8,128)(2,1)S(1)}) custom-call(s32[320,8]{1,0:T(8,128)S(1)} %bitcast.9, bf16[320,512]{1,0:T(8,128)(2,1)S(1)} %copy-done.6, bf16[320,512]{1,0:T(8,128)(2,1)S(1)} %get-tuple-element.24.hidden_ref, f32[320,512]{1,0:T(8,128)S(1)} %get-tuple-element.25.slope_ref, ...), custom_call_target="tpu_custom_call" | custom-call | flops 2000000000 | bytes 8000000 | tf_op jit(solution)/shard_map/backward/pallas_call | solution.py:366
  33.2 1.9 %collective-permute-start.1 = (bf16[320,2176]{1,0:T(8,128)(2,1)S(1)}, bf16[320,2176]{1,0:T(8,128)(2,1)S(1)}, u32[]{:S(2)}, u32[]{:S(2)}) collective-permute-start(bf16[320,2176]{1,0:T(8,128)(2,1)S(1)} %get-tuple-element.36), channel_id=1, source_target_pairs={{0,4},{4,0},{1,5},{5,1},{2,6},{6,2},{3,7},{7,3},{8,12},{12,8},{9,1... | collective-permute-start | bytes 4177928 | tf_op jit(solution)/shard_map/ppermute | solution.py:369
  35.1 29.6 %all_to_all.20.got_ref = f32[128,2,128]{2,1,0:T(2,128)S(1)} all-to-all(f32[128,2,128]{2,1,0:T(2,128)S(1)} %get-tuple-element.34), channel_id=1, replica_groups=mesh['z'=8,'y'=8,'core'=2,'x'=4] {'z','y','core'}, dimensions={0} | all-to-all | bytes 262144 | tf_op jit(solution)/shard_map/all_to_all | solution.py:365
  64.7 0.9 first.1
  65.5 0.0 collective-permute-done.1.other_ref
  65.5 0.9 term.1
  66.4 17.2 %all_to_all.21.got_ref = bf16[4,128,1024]{2,1,0:T(8,128)(2,1)S(1)} all-to-all(bf16[4,128,1024]{2,1,0:T(8,128)(2,1)S(1)} %term.1), channel_id=1, replica_groups=mesh['z'=8,'y'=8,'core'=2,'x'=4] {'x'}, dimensions={0} | all-to-all | bytes 2097152 | tf_op jit(solution)/shard_map/all_to_all | solution.py:374
  83.6 0.0 copy-start.2
  83.6 1.2 %middle.1 = bf16[64,16,128]{2,1,0:T(8,128)(2,1)} custom-call(bf16[4,128,1024]{2,1,0:T(8,128)(2,1)S(1)} %all_to_all.21.got_ref), custom_call_target="tpu_custom_call" | custom-call | flops 500000000 | bytes 2000000 | tf_op jit(solution)/shard_map/middle/pallas_call | solution.py:375
  84.9 4.6 %all-to-all-start.3 = ((bf16[64,16,128]{2,1,0:T(8,128)(2,1)}), bf16[64,16,128]{2,1,0:T(8,128)(2,1)S(1)}, u32[]{:S(2)}, u32[]{:S(2)}) async-start(bf16[64,16,128]{2,1,0:T(8,128)(2,1)} %middle.1), calls=%async_computation.3 | async-start | bytes 524288 | tf_op jit(solution)/shard_map/all_to_all | solution.py:378
  89.5 0.8 reshape.35
  90.3 11.7 %all-to-all-done.3.got_ref = bf16[64,16,128]{2,1,0:T(8,128)(2,1)S(1)} async-done(((bf16[64,16,128]{2,1,0:T(8,128)(2,1)}), bf16[64,16,128]{2,1,0:T(8,128)(2,1)S(1)}, u32[]{:S(2)}, u32[]{:S(2)}) %all-to-all-start.3) | async-done | bytes 262176 | tf_op jit(solution)/shard_map/all_to_all | solution.py:378
  102.0 0.0 copy-done.2
  102.0 0.7 final.1
  (5 shorter events, 0.1 us)
Async XLA Ops:
  3.1 5.0 %copy-start.13 = (s32[300,1]{0,1:T(1,128)S(1)}, s32[300,1]{0,1:T(1,128)}, u32[]{:S(2)}) copy-start(s32[300,1]{0,1:T(1,128)} %param.21) | copy-start | bytes 3604
  3.1 5.3 %copy-start.12 = (s32[2,5,31]{2,0,1:T(2,128)S(1)}, s32[2,5,31]{2,0,1:T(2,128)}, u32[]{:S(2)}) copy-start(s32[2,5,31]{2,0,1:T(2,128)} %param.19) | copy-start | bytes 3724
  3.1 6.5 %copy-start.9 = (bf16[2,150,512]{2,0,1:T(2,128)(2,1)S(1)}, bf16[2,150,512]{2,0,1:T(2,128)(2,1)}, u32[]{:S(2)}) copy-start(bf16[2,150,512]{2,0,1:T(2,128)(2,1)} %param.22) | copy-start | bytes 921604
  3.1 7.2 %copy-start.10 = (bf16[2,150,512]{2,0,1:T(2,128)(2,1)S(1)}, bf16[2,150,512]{2,0,1:T(2,128)(2,1)}, u32[]{:S(2)}) copy-start(bf16[2,150,512]{2,0,1:T(2,128)(2,1)} %param.23) | copy-start | bytes 921604
  3.1 15.5 %all-to-all-start = ((bf16[4,2,128,512]{3,2,1,0:T(8,128)(2,1)}), bf16[4,2,128,512]{3,2,1,0:T(8,128)(2,1)S(1)}, u32[]{:S(2)}, u32[]{:S(2)}) async-start(bf16[4,2,128,512]{3,2,1,0:T(8,128)(2,1)} %prepare.1), calls=%async_computation | async-start | bytes 2097152 | tf_op jit(solution)/shard_map/all_to_all | solution.py:324
  8.8 2.4 %copy-start.11 = (s32[8,320]{1,0:T(8,128)}, s32[8,320]{1,0:T(8,128)S(1)}, u32[]{:S(2)}) copy-start(s32[8,320]{1,0:T(8,128)S(1)} %stack.3.rows_ref) | copy-start | bytes 30724
  18.6 10.4 %collective-permute-start = (bf16[4,2,128,512]{3,2,1,0:T(8,128)(2,1)S(1)}, bf16[4,2,128,512]{3,2,1,0:T(8,128)(2,1)S(1)}, u32[]{:S(2)}, u32[]{:S(2)}) collective-permute-start(bf16[4,2,128,512]{3,2,1,0:T(8,128)(2,1)S(1)} %all-to-all-done.weights_ref), channel_id=1, source_target_pairs={{0,4},{4,0},{1,5},{5,1},{2,6},{6,2},{3,7},{7,3},{8,12},{12,8},{9,1... | collective-permute-start | bytes 3145736 | tf_op jit(solution)/shard_map/ppermute | solution.py:347
  26.4 1.0 copy-start.5
  27.4 0.7 copy-start.8
  28.1 0.9 copy-start
  28.1 0.9 copy-start.1
  28.1 0.9 copy-start.3
  28.1 0.9 copy-start.4
  28.1 1.1 %copy-start.6 = (bf16[320,512]{1,0:T(8,128)(2,1)S(1)}, bf16[320,512]{1,0:T(8,128)(2,1)}, u32[]{:S(2)}) copy-start(bf16[320,512]{1,0:T(8,128)(2,1)} %get-tuple-element.20.states_ref) | copy-start | bytes 983044
  28.1 1.1 %copy-start.7 = (f32[320,128]{1,0:T(8,128)S(1)}, f32[320,128]{1,0:T(8,128)}, u32[]{:S(2)}) copy-start(f32[320,128]{1,0:T(8,128)} %get-tuple-element.26.at_rank_ref) | copy-start | bytes 491524
  33.2 32.4 %collective-permute-start.1 = (bf16[320,2176]{1,0:T(8,128)(2,1)S(1)}, bf16[320,2176]{1,0:T(8,128)(2,1)S(1)}, u32[]{:S(2)}, u32[]{:S(2)}) collective-permute-start(bf16[320,2176]{1,0:T(8,128)(2,1)S(1)} %get-tuple-element.36), channel_id=1, source_target_pairs={{0,4},{4,0},{1,5},{5,1},{2,6},{6,2},{3,7},{7,3},{8,12},{12,8},{9,1... | collective-permute-start | bytes 4177928 | tf_op jit(solution)/shard_map/ppermute | solution.py:369
  83.6 18.3 %copy-start.2 = (f32[2,1024]{1,0:T(2,128)S(1)}, f32[2,1024]{1,0:T(2,128)}, u32[]{:S(2)}) copy-start(f32[2,1024]{1,0:T(2,128)} %momentum_ref.1) | copy-start | bytes 24580
  84.9 17.1 %all-to-all-start.3 = ((bf16[64,16,128]{2,1,0:T(8,128)(2,1)}), bf16[64,16,128]{2,1,0:T(8,128)(2,1)S(1)}, u32[]{:S(2)}, u32[]{:S(2)}) async-start(bf16[64,16,128]{2,1,0:T(8,128)(2,1)} %middle.1), calls=%async_computation.3 | async-start | bytes 524288 | tf_op jit(solution)/shard_map/all_to_all | solution.py:378

commit v5 on v4

--- a/solution.py
+++ b/solution.py
@@ -60,16 +60,17 @@
     return high, (v - high.astype(f32)).astype(bf16)
 
 
-def call(body, outs, scratch=(), cost=4.0, n_smem=0, n_in=0, n_any=0, out_hbm=False, limit=16 << 20, name=None):
+def call(body, outs, scratch=(), cost=4.0, n_smem=0, n_in=0, n_hbm=0, limit=16 << 20, name=None):
     smem = [pl.BlockSpec(memory_space=pltpu.SMEM)] * n_smem
-    vmem = [pl.BlockSpec(memory_space=pltpu.VMEM)] * n_in + [pl.BlockSpec(memory_space=pltpu.HBM)] * n_any
-    shapes = [jax.ShapeDtypeStruct(s, d) for s, d in outs]
-    specs = [pl.BlockSpec(memory_space=pltpu.HBM if out_hbm else pltpu.VMEM)] * len(outs)
+    vmem = [pl.BlockSpec(memory_space=pltpu.VMEM)] * n_in
+    hbm = [pl.BlockSpec(memory_space=pltpu.HBM)] * n_hbm
+    shapes = [jax.ShapeDtypeStruct(out[0], out[1]) for out in outs]
+    specs = [pl.BlockSpec(memory_space=pltpu.HBM if len(out) > 2 else pltpu.VMEM) for out in outs]
     single = len(outs) == 1
     return pl.pallas_call(
         body,
         out_shape=shapes[0] if single else shapes,
-        in_specs=smem + vmem,
+        in_specs=smem + vmem + hbm,
         out_specs=specs[0] if single else specs,
         scratch_shapes=list(scratch),
         compiler_params=pltpu.CompilerParams(vmem_limit_bytes=limit),
@@ -78,25 +79,30 @@
     )
 
 
+def start(sems, first, *pairs):
+    copies = [pltpu.make_async_copy(src, dst, sems.at[first + k]) for k, (src, dst) in enumerate(pairs)]
+    for copy in copies:
+        copy.start()
+    return copies
+
+
+def finish(copies):
+    for copy in copies:
+        copy.wait()
+
+
 def prepare_body(core_ref, w_in_hbm, w_down_hbm, out_hbm, w_in, w_down, mine, sems):
-    loads = [
-        pltpu.make_async_copy(w_in_hbm, w_in, sems.at[0]),
-        pltpu.make_async_copy(w_down_hbm, w_down, sems.at[1]),
-    ]
-    for load in loads:
-        load.start()
+    loads = start(sems, 0, (w_in_hbm, w_in), (w_down_hbm, w_down))
     unit, place = iota((PART, LANES), 0), iota((PART, LANES), 1)
     wanted = (place % 16) * 16 + core_ref[0] * 8 + place // 16
     chosen = (unit == wanted).astype(bf16)
     loads[0].wait()
     mine[0] = lax.dot_general(chosen, w_in[...], (((0,), (1,)), ((), ())), preferred_element_type=f32).astype(bf16)
+    stores = start(sems, 2, *[(mine.at[0], out_hbm.at[k, 0]) for k in range(N_X)])
     loads[1].wait()
     mine[1] = mm_tall(chosen, w_down[...]).astype(bf16)
-    stores = [pltpu.make_async_copy(mine, out_hbm.at[k], sems.at[2 + k]) for k in range(N_X)]
-    for store in stores:
-        store.start()
-    for store in stores:
-        store.wait()
+    stores += start(sems, 2 + N_X, *[(mine.at[1], out_hbm.at[k, 1]) for k in range(N_X)])
+    finish(stores)
 
 
 def attend_body(
@@ -104,9 +110,7 @@
     w_value_hbm, w_self_hbm, cross_query_hbm, cross_out_hbm, states_ref, at_rank_ref, done_ref, ctx_ref, held, sems,
 ):
     sources = (w_query_hbm, w_key_hbm, w_value_hbm, w_self_hbm, cross_query_hbm, cross_out_hbm)
-    loads = [pltpu.make_async_copy(source, held.at[k], sems.at[k]) for k, source in enumerate(sources)]
-    for load in loads:
-        load.start()
+    loads = start(sems, 0, *[(source, held.at[k]) for k, source in enumerate(sources)])
     lane = iota((ROWS, LANES), 1)
     hits = cols_ref[:, 2:3] == lane
     earlier = (iota((ROWS, ROWS), 0) > iota((ROWS, ROWS), 1)).astype(bf16)
@@ -121,8 +125,7 @@
     picks = (cols_ref[:, 0:1] == iota((ROWS, 32), 1)).astype(bf16)
     picks_t = (rows_ref[0:1, :] == iota((32, ROWS), 0)).astype(bf16)
     embedded = mm(picks, table)
-    for load in loads:
-        load.wait()
+    finish(loads)
     query = mm(embedded.astype(bf16), held[0]).astype(bf16)
     keyed = mm(table, held[1])
     valued = mm(table, held[2])
@@ -173,38 +176,25 @@
     return mm((iota((LANES, VOCAB), 0) == iota((LANES, VOCAB), 1)).astype(bf16), head_ref[...]).astype(bf16)
 
 
-def half_forward(states, weights_ref, hidden_ref, slope_ref):
+def half_forward(states, weights_ref):
     w_in = jnp.concatenate([weights_ref[m, 0] for m in range(N_X)], 0)
     w_down = jnp.concatenate([weights_ref[m, 1] for m in range(N_X)], 0)
     pre = mm_flip(states, w_in)
     tanh = jnp.tanh(0.7978845608028654 * (pre + 0.044715 * pre * pre * pre))
     hidden = (0.5 * pre * (1.0 + tanh)).astype(bf16)
-    hidden_ref[...] = hidden
-    slope_ref[...] = 0.5 * (1.0 + tanh) + 0.5 * pre * (1.0 - tanh * tanh) * 0.7978845608028654 * (1.0 + 0.134145 * pre * pre)
-    return mm(hidden, w_down)
-
-
-def own_body(states_ref, weights_ref, done_ref, hidden_ref, slope_ref, total_ref):
-    states = states_ref[...]
-    total_ref[...] = states.astype(f32) + half_forward(states, weights_ref, hidden_ref, slope_ref)
-
-
-def forward_body(
-    accept_ref, cols_ref, at_rank_ref, states_ref, partial_ref, weights_ref, gain_ref, head_ref,
-    message_ref, hidden_ref, slope_ref, unit_ref, signal_ref, scale_ref,
-):
-    unit, scale = norm_parts(partial_ref[...] + half_forward(states_ref[...], weights_ref, hidden_ref, slope_ref))
-    unit_ref[...] = unit
-    scale_ref[...] = jnp.broadcast_to(scale, (ROWS, LANES))
-    high, low = split(unit * gain_ref[...])
-    head = wide_head(head_ref)
+    return pre, tanh, hidden, w_down, mm(hidden, w_down)
+
+
+def scores_of(total, gain, head, labels, accept_ref):
+    unit, scale = norm_parts(total)
+    high, low = split(unit * gain)
     logits = mm_flip(high, head) + mm_flip(low, head)
     lane = iota((ROWS, LANES), 1)
     logits = jnp.where(lane < VOCAB, logits, -1e30)
     top = jnp.max(logits, -1, keepdims=True)
     grown = jnp.exp(logits - top)
     mass = jnp.sum(grown, -1, keepdims=True)
-    is_label = cols_ref[:, 1:2] == lane
+    is_label = labels == lane
     taken = jnp.sum(jnp.where(is_label, logits, 0.0), -1, keepdims=True) - top - jnp.log(mass)
     beam = beam_of(0)
     row = iota((ROWS, 1), 0)
@@ -223,8 +213,21 @@
         share = e / jnp.sum(e, -1, keepdims=True) * accept_ref[s].astype(f32)
         shares = jnp.where(inside, share, shares)
     weight = jnp.sum(beams * shares, -1, keepdims=True)
-    signal_ref[...] = weight * (grown / mass - is_label.astype(f32))
-    hits = cols_ref[:, 2:3] == lane
+    return unit, scale, taken, weight, grown, mass, is_label
+
+
+def own_body(states_ref, weights_ref, done_ref, total_ref):
+    states = states_ref[...]
+    total_ref[...] = states.astype(f32) + half_forward(states, weights_ref)[4]
+
+
+def forward_body(
+    accept_ref, cols_ref, at_rank_ref, states_ref, partial_ref, weights_ref, gain_ref, head_ref, message_ref
+):
+    total = partial_ref[...] + half_forward(states_ref[...], weights_ref)[4]
+    out = scores_of(total, gain_ref[...], wide_head(head_ref), cols_ref[:, 1:2], accept_ref)
+    taken, weight = out[2], out[3]
+    hits = cols_ref[:, 2:3] == iota((ROWS, LANES), 1)
     sums = jnp.sum(jnp.where(hits, weight, 0.0), 0, keepdims=True)
     high, low = split(at_rank_ref[...] * (-weight * taken))
     hits16 = hits.astype(bf16)
@@ -233,25 +236,27 @@
 
 
 def backward_body(
-    cols_ref, states_ref, hidden_ref, slope_ref, weights_ref, hidden_2_ref, slope_2_ref, weights_2_ref, unit_ref, signal_ref,
-    scale_ref, gain_ref, head_ref, keep_ref, send_ref,
+    accept_ref, cols_ref, states_ref, own_ref, other_ref, gain_ref, head_ref, keep_ref, send_ref, slopes, downs,
 ):
-    unit = unit_ref[...]
-    high, low = split(signal_ref[...])
-    head = wide_head(head_ref)
-    d_unit = gain_ref[...] * (mm(high, head) + mm(low, head))
+    states = states_ref[...]
+    total = states.astype(f32)
+    hidden_at = slice(WIDTH, 2 * WIDTH)
+    for k, weights_ref, ref in ((0, own_ref, keep_ref), (1, other_ref, send_ref)):
+        pre, tanh, hidden, w_down, more = half_forward(states, weights_ref)
+        slope = 0.5 * (1.0 + tanh) + 0.5 * pre * (1.0 - tanh * tanh) * 0.7978845608028654 * (1.0 + 0.134145 * pre * pre)
+        slopes[k] = slope
+        downs[k] = w_down
+        ref[:, hidden_at] = hidden
+        total = total + more
+    head, gain = wide_head(head_ref), gain_ref[...]
+    unit, scale, _, weight, grown, mass, is_label = scores_of(total, gain, head, cols_ref[:, 1:2], accept_ref)
+    high, low = split(weight * (grown / mass - is_label.astype(f32)))
+    d_unit = gain * (mm(high, head) + mm(low, head))
     along = jnp.mean(d_unit * unit, -1, keepdims=True)
-    d_total = scale_ref[:, 0:1] * (d_unit - jnp.mean(d_unit, -1, keepdims=True) - unit * along)
-    d_out = d_total.astype(bf16)
-    states = states_ref[...]
+    d_out = (scale * (d_unit - jnp.mean(d_unit, -1, keepdims=True) - unit * along)).astype(bf16)
     dest = jnp.broadcast_to(cols_ref[:, 2:3], (ROWS, LANES)).astype(f32).astype(bf16)
-    for ref, hidden, slope, weights in (
-        (send_ref, hidden_2_ref, slope_2_ref, weights_2_ref),
-        (keep_ref, hidden_ref, slope_ref, weights_ref),
-    ):
-        w_down = jnp.concatenate([weights[m, 1] for m in range(N_X)], 0)
-        ref[:, 0:WIDTH] = (mm_flip(d_out, w_down) * slope[...]).astype(bf16)
-        ref[:, WIDTH : 2 * WIDTH] = hidden[...]
+    for k, ref in ((0, keep_ref), (1, send_ref)):
+        ref[:, 0:WIDTH] = (mm_flip(d_out, downs[k]) * slopes[k]).astype(bf16)
         ref[:, 2 * WIDTH : 3 * WIDTH] = states
         ref[:, 3 * WIDTH : 4 * WIDTH] = d_out
         ref[:, 4 * WIDTH :] = dest
@@ -312,14 +317,14 @@
 
     mine = call(
         prepare_body,
-        [((N_X, 2, LANES, WIDTH), bf16)],
+        [((N_X, 2, LANES, WIDTH), bf16, 1)],
         scratch=[
             pltpu.VMEM((WIDTH, PART), bf16),
             pltpu.VMEM((PART, WIDTH), bf16),
             pltpu.VMEM((2, LANES, WIDTH), bf16),
-            pltpu.SemaphoreType.DMA((2 + N_X,)),
+            pltpu.SemaphoreType.DMA((2 + 2 * N_X,)),
         ],
-        n_smem=1, n_any=2, out_hbm=True, limit=63_300_000, cost=1, name="prepare",
+        n_smem=1, n_hbm=2, limit=63_300_000, cost=1, name="prepare",
     )(core, w_in, w_down)
     own_w = lax.all_to_all(mine, "x", 0, 0)
 
@@ -338,37 +343,29 @@
             pltpu.VMEM((6, WIDTH, WIDTH), bf16),
             pltpu.SemaphoreType.DMA((6,)),
         ],
-        n_in=7, n_any=6, limit=61_300_000, cost=8, name="attend",
+        n_in=7, n_hbm=6, limit=61_300_000, cost=8, name="attend",
     )(
         cols, rows, mem_keys, mem_values, embed, gain_self.reshape(1, WIDTH), gain_cross.reshape(1, WIDTH),
         w_query, w_key, w_value, w_self, cross_query, cross_out,
     )
     own_w, done = lax.optimization_barrier((own_w, done))
     other_w = lax.ppermute(own_w, "core", swap)
-    hidden, slope, partial = call(
-        own_body, [(half, bf16), (half, f32), ((ROWS, WIDTH), f32)], n_in=3, cost=2, name="own"
-    )(states, own_w, done)
+    partial = call(own_body, [((ROWS, WIDTH), f32)], n_in=3, cost=2, name="own")(states, own_w, done)
     gain = gain_ff.reshape(1, WIDTH)
     head = head.T
-    message, hidden_2, slope_2, unit, signal, scale = call(
-        forward_body,
-        [
-            ((N_DP, 2, LANES), f32),
-            (half, bf16),
-            (half, f32),
-            ((ROWS, WIDTH), f32),
-            ((ROWS, LANES), f32),
-            ((ROWS, LANES), f32),
-        ],
-        n_smem=1, n_in=7, cost=5, name="forward",
-    )(accept, cols, at_rank, states, partial, other_w, gain, head)
+    message = call(forward_body, [((N_DP, 2, LANES), f32)], n_smem=1, n_in=7, cost=5, name="forward")(
+        accept, cols, at_rank, states, partial, other_w, gain, head
+    )
     got = lax.all_to_all(message, DP, 0, 0)
     keep, send = call(
-        backward_body, [((ROWS, PAY), bf16), ((ROWS, PAY), bf16)], n_in=13, cost=4, name="backward"
-    )(cols, states, hidden, slope, own_w, hidden_2, slope_2, other_w, unit, signal, scale, gain, head)
+        backward_body,
+        [((ROWS, PAY), bf16), ((ROWS, PAY), bf16)],
+        scratch=[pltpu.VMEM((2,) + half, f32), pltpu.VMEM((2, HALF, WIDTH), bf16)],
+        n_smem=1, n_in=6, limit=61_300_000, cost=4, name="backward",
+    )(accept, cols, states, own_w, other_w, gain, head)
     other = lax.ppermute(send, "core", swap)
     first, loss = call(
-        first_body, [((HALF, 2 * WIDTH), f32), ((N_DP, LANES), f32)], n_in=2, cost=20, name="first"
+        first_body, [((HALF, 2 * WIDTH), f32), ((N_DP, LANES), f32)], n_in=2, cost=40, name="first"
     )(keep, got)
     term = call(term_body, [((N_X, LANES, 2 * WIDTH), bf16)], n_in=3, cost=4, name="term")(first, other, got)
     got = lax.all_to_all(term, "x", 0, 0)

time: 104 us -> 108 us (1.038)
  blocking collectives: 46.8 us -> 17.2 us
  starting transfers between devices: 19.4 us -> 42 us
  Pallas kernels: 18.2 us -> 23.6 us
  waiting for transfers between devices: 11.7 us -> 15 us
  local copies, waits for them, and re-layouts: 5.74 us -> 7.1 us
    all_to_all x1 -> x0, blocking collectives: 29.6 us -> none  [per_device(): got = lax.all_to_all(message, DP, 0, 0)]
    all_to_all x0 -> x1, starting transfers between devices: none -> 16.7 us  [per_device(): got = lax.all_to_all(message, DP, 0, 0)]
    pallas_call x4, Pallas kernels: 7.16 us -> 12.6 us  [the longest x1 6.4 us: per_device(): call(backward_body, [((ROWS, PAY), bf16), ((ROWS, PAY), bf16)], scratch=[...]
    all_to_all x1, starting transfers between devices: 4.61 us -> 9.53 us  [per_device(): got = lax.all_to_all(middle, ('z', 'y'), 0, 0)]
    all_to_all x0 -> x1, waiting for transfers between devices: none -> 3.35 us  [per_device(): got = lax.all_to_all(message, DP, 0, 0)]
    unnamed x31 -> x35, local copies, waits for them, and re-layouts: 3.53 us -> 4.88 us
  transfers between devices with their start and end apart: 4 -> 5, of which waited for: 1 -> 2; matrix products, arithmetic and copies ran while one was open for 4% -> 4% of each run, Pallas kernels for 9% -> 14%
where the time goes in v5:
time: 108 us; the launch traced here: 106 us
  starting transfers between devices  42 us (39%)
  Pallas kernels  23.6 us (22%)
  blocking collectives  17.2 us (16%)
  waiting for transfers between devices  15 us (14%)
  local copies, waits for them, and re-layouts  7.1 us (7%)
    all_to_all x1, blocking collectives, per_device(): got = lax.all_to_all(term, 'x', 0, 0)  17.2 us
    all_to_all x1, starting transfers between devices, per_device(): got = lax.all_to_all(message, DP, 0, 0)  16.7 us
    all_to_all x1, waiting for transfers between devices, per_device(): got = lax.all_to_all(middle, ('z', 'y'), 0, 0)  11.7 us
    all_to_all x1, starting transfers between devices, per_device(): got = lax.all_to_all(middle, ('z', 'y'), 0, 0)  9.53 us
    ppermute x1, starting transfers between devices, per_device(): other_w = lax.ppermute(own_w, 'core', swap)  7.85 us
    pallas_call x1, Pallas kernels, per_device(): call(attend_body, [((ROWS, WIDTH), bf16), ((ROWS, LANES), f32), ((16, LAN...  7.42 us
    pallas_call x1, Pallas kernels, per_device(): call(backward_body, [((ROWS, PAY), bf16), ((ROWS, PAY), bf16)], scratch=[...  6.4 us
    all_to_all x1, starting transfers between devices, per_device(): own_w = lax.all_to_all(mine, 'x', 0, 0)  4.99 us
  transfers between devices with their start and end apart: 5, of which 2 were waited for; matrix products, arithmetic and copies ran while one was open for 4% of the time, Pallas kernels for 14%

profile of v5, /device:TPU:1, one launch (start us, length us, event | category | flops | bytes accessed | tf_op | source)
XLA Modules:
  0.0 105.9 jit_solution(14360479288427880263)
XLA Ops:
  0.6 2.3 %prepare.1 = bf16[4,2,128,512]{3,2,1,0:T(8,128)(2,1)} custom-call(s32[1]{0:T(128)} %bitcast.3.core_ref, bf16[512,256]{1,0:T(8,128)(2,1)} %w_in_hbm.1, bf16[256,512]{1,0:T(8,128)(2,1)} %w_down_hbm.1), custom_call_target="tpu_custom_call" | custom-call | flops 500000000 | bytes 2000000 | tf_op jit(solution)/shard_map/prepare/pallas_call | solution.py:318
  2.9 0.0 copy-start.15
  2.9 0.0 copy-start.14
  2.9 0.0 copy-start.11
  2.9 0.0 copy-start.12
  3.0 5.0 %all-to-all-start = ((bf16[4,2,128,512]{3,2,1,0:T(8,128)(2,1)}), bf16[4,2,128,512]{3,2,1,0:T(8,128)(2,1)S(1)}, u32[]{:S(2)}, u32[]{:S(2)}) async-start(bf16[4,2,128,512]{3,2,1,0:T(8,128)(2,1)} %prepare.1), calls=%async_computation | async-start | bytes 2097152 | tf_op jit(solution)/shard_map/all_to_all | solution.py:329
  7.9 0.0 copy-done.15
  8.0 0.1 reshape.29
  8.1 0.1 reshape.30
  8.1 0.1 stack_reshape.16
  8.2 0.0 copy-done.14
  8.2 0.1 reshape.28
  8.3 0.1 pad_slice_fusion
  8.4 0.1 stack_reshape.7
  8.5 0.1 stack_reshape.6
  8.6 0.0 copy-start.13
  8.6 0.8 copy.37
  9.4 0.0 copy-done.11
  9.4 0.8 copy.38.keys_ref
  10.2 0.0 copy-done.12
  10.2 0.8 copy.39.values_ref
  11.0 0.0 copy-done.13
  11.0 7.4 %attend.1 = (bf16[320,512]{1,0:T(8,128)(2,1)}, f32[320,128]{1,0:T(8,128)}, bf16[16,128]{1,0:T(8,128)(2,1)}) custom-call(s32[320,8]{1,0:T(8,128)} %bitcast.7, s32[8,320]{1,0:T(8,128)} %copy-done.13, bf16[2,150,512]{2,1,0:T(8,128)(2,1)} %copy.38.keys_ref, bf16[2,150,512]{2,1,0:T(8,128)(2,1)} %copy.39.values_ref, bf16[28,512]{1,0:T(8,128)(2,1)} %embed_ref.1, ...), custom_call_target="tpu_custom_call" | custom-call | flops 4000000000 | bytes 16000000 | tf_op jit(solution)/shard_map/attend/pallas_call | solution.py:338
  18.4 0.0 all-to-all-done.own_ref.weights_ref
  18.4 0.0 copy-start
  18.4 7.9 %collective-permute-start = (bf16[4,2,128,512]{3,2,1,0:T(8,128)(2,1)S(1)}, bf16[4,2,128,512]{3,2,1,0:T(8,128)(2,1)S(1)}, u32[]{:S(2)}, u32[]{:S(2)}) collective-permute-start(bf16[4,2,128,512]{3,2,1,0:T(8,128)(2,1)S(1)} %all-to-all-done.own_ref.weights_ref), channel_id=1, source_target_pairs={{0,4},{4,0},{1,5},{5,1},{2,6},{6,2},{3,7},{7,3},{8,12},{12,8},{9,1... | collective-permute-start | bytes 3145736 | tf_op jit(solution)/shard_map/ppermute | solution.py:352
  26.3 0.0 copy-start.7
  26.3 1.0 copy-done.7
  27.2 0.0 copy-start.10
  27.2 0.7 copy-done.10
  27.9 0.0 copy-start.1
  27.9 0.0 copy-start.3
  27.9 0.0 copy-start.5
  27.9 0.0 copy-start.6
  27.9 0.0 copy-start.9
  27.9 0.7 own.1.partial_ref
  28.6 0.0 copy-done
  28.6 0.0 collective-permute-done.other_ref.weights_ref
  28.7 0.0 copy-start.2
  28.7 0.2 copy-done.1
  28.8 0.0 copy-done.3
  28.8 0.0 copy-done.5
  28.8 0.0 copy-done.6
  28.9 0.1 copy-done.9
  29.0 3.3 %forward.1 = f32[128,2,128]{2,1,0:T(2,128)} custom-call(s32[2]{0:T(128)S(1)} %copy-done.6, s32[320,8]{1,0:T(8,128)S(1)} %bitcast.9, f32[320,128]{1,0:T(8,128)S(1)} %copy-done.9, bf16[320,512]{1,0:T(8,128)(2,1)S(1)} %copy-done.7, f32[320,512]{1,0:T(8,128)S(1)} %own.1.partial_ref, bf16[4,2,128,512]{3,2,1,0:T(8,128)(2,1)S(1)} %collective-permute-done.other_ref.weights_ref, ...), custom_call_target="tpu_custom_call" | custom-call | flops 2500000000 | bytes 10000000 | tf_op jit(solution)/shard_map/forward/pallas_call | solution.py:356
  32.2 0.0 copy-done.2
  32.2 16.7 %all-to-all-start.1 = ((f32[128,2,128]{2,1,0:T(2,128)}), f32[128,2,128]{2,1,0:T(2,128)S(1)}, u32[]{:S(2)}, u32[]{:S(2)}) async-start(f32[128,2,128]{2,1,0:T(2,128)} %forward.1), calls=%async_computation.1 | async-start | bytes 262144 | tf_op jit(solution)/shard_map/all_to_all | solution.py:359
  48.9 6.4 %backward.1 = (bf16[320,2176]{1,0:T(8,128)(2,1)}, bf16[320,2176]{1,0:T(8,128)(2,1)}) custom-call(s32[2]{0:T(128)} %accept_ref.3, s32[320,8]{1,0:T(8,128)} %bitcast.8, bf16[320,512]{1,0:T(8,128)(2,1)} %get-tuple-element.11.states_ref, bf16[4,2,128,512]{3,2,1,0:T(8,128)(2,1)} %copy-done, bf16[4,2,128,512]{3,2,1,0:T(8,128)(2,1)} %copy-done.2, ...), custom_call_target="tpu_custom_call" | custom-call | flops 2000000000 | bytes 8000000 | tf_op jit(solution)/shard_map/backward/pallas_call | solution.py:360
  55.3 3.0 %collective-permute-start.1 = (bf16[320,2176]{1,0:T(8,128)(2,1)}, bf16[320,2176]{1,0:T(8,128)(2,1)S(1)}, u32[]{:S(2)}, u32[]{:S(2)}) collective-permute-start(bf16[320,2176]{1,0:T(8,128)(2,1)} %get-tuple-element.18), channel_id=1, source_target_pairs={{0,4},{4,0},{1,5},{5,1},{2,6},{6,2},{3,7},{7,3},{8,12},{12,8},{9,1... | collective-permute-start | bytes 4177928 | tf_op jit(solution)/shard_map/ppermute | solution.py:366
  58.3 3.3 %all-to-all-done.1.got_ref = f32[128,2,128]{2,1,0:T(2,128)S(1)} async-done(((f32[128,2,128]{2,1,0:T(2,128)}), f32[128,2,128]{2,1,0:T(2,128)S(1)}, u32[]{:S(2)}, u32[]{:S(2)}) %all-to-all-start.1) | async-done | bytes 131104 | tf_op jit(solution)/shard_map/all_to_all | solution.py:359
  61.6 0.0 copy-start.8
  61.6 1.3 %copy-done.8 = bf16[320,2176]{1,0:T(8,128)(2,1)S(1)} copy-done((bf16[320,2176]{1,0:T(8,128)(2,1)S(1)}, bf16[320,2176]{1,0:T(8,128)(2,1)}, u32[]{:S(2)}) %copy-start.8) | copy-done | bytes 1392664
  63.0 0.9 first.1
  63.8 0.0 collective-permute-done.1.other_ref
  63.8 0.9 term.1
  64.7 17.2 %all_to_all.20.got_ref = bf16[4,128,1024]{2,1,0:T(8,128)(2,1)S(1)} all-to-all(bf16[4,128,1024]{2,1,0:T(8,128)(2,1)S(1)} %term.1), channel_id=1, replica_groups=mesh['z'=8,'y'=8,'core'=2,'x'=4] {'x'}, dimensions={0} | all-to-all | bytes 2097152 | tf_op jit(solution)/shard_map/all_to_all | solution.py:371
  81.9 0.0 copy-start.4
  81.9 1.2 %middle.1 = bf16[64,16,128]{2,1,0:T(8,128)(2,1)} custom-call(bf16[4,128,1024]{2,1,0:T(8,128)(2,1)S(1)} %all_to_all.20.got_ref), custom_call_target="tpu_custom_call" | custom-call | flops 500000000 | bytes 2000000 | tf_op jit(solution)/shard_map/middle/pallas_call | solution.py:372
  83.2 9.5 %all-to-all-start.3 = ((bf16[64,16,128]{2,1,0:T(8,128)(2,1)}), bf16[64,16,128]{2,1,0:T(8,128)(2,1)S(1)}, u32[]{:S(2)}, u32[]{:S(2)}) async-start(bf16[64,16,128]{2,1,0:T(8,128)(2,1)} %middle.1), calls=%async_computation.3 | async-start | bytes 524288 | tf_op jit(solution)/shard_map/all_to_all | solution.py:375
  92.7 0.8 reshape.35
  93.5 11.7 %all-to-all-done.3.got_ref = bf16[64,16,128]{2,1,0:T(8,128)(2,1)S(1)} async-done(((bf16[64,16,128]{2,1,0:T(8,128)(2,1)}), bf16[64,16,128]{2,1,0:T(8,128)(2,1)S(1)}, u32[]{:S(2)}, u32[]{:S(2)}) %all-to-all-start.3) | async-done | bytes 262176 | tf_op jit(solution)/shard_map/all_to_all | solution.py:375
  105.2 0.0 copy-done.4
  105.2 0.7 final.1
  (5 shorter events, 0.1 us)
Async XLA Ops:
  2.9 5.0 %copy-start.15 = (s32[300,1]{0,1:T(1,128)S(1)}, s32[300,1]{0,1:T(1,128)}, u32[]{:S(2)}) copy-start(s32[300,1]{0,1:T(1,128)} %param.21) | copy-start | bytes 3604
  2.9 5.3 %copy-start.14 = (s32[2,5,31]{2,0,1:T(2,128)S(1)}, s32[2,5,31]{2,0,1:T(2,128)}, u32[]{:S(2)}) copy-start(s32[2,5,31]{2,0,1:T(2,128)} %param.19) | copy-start | bytes 3724
  2.9 6.5 %copy-start.11 = (bf16[2,150,512]{2,0,1:T(2,128)(2,1)S(1)}, bf16[2,150,512]{2,0,1:T(2,128)(2,1)}, u32[]{:S(2)}) copy-start(bf16[2,150,512]{2,0,1:T(2,128)(2,1)} %param.22) | copy-start | bytes 921604
  2.9 7.2 %copy-start.12 = (bf16[2,150,512]{2,0,1:T(2,128)(2,1)S(1)}, bf16[2,150,512]{2,0,1:T(2,128)(2,1)}, u32[]{:S(2)}) copy-start(bf16[2,150,512]{2,0,1:T(2,128)(2,1)} %param.23) | copy-start | bytes 921604
  3.0 15.4 %all-to-all-start = ((bf16[4,2,128,512]{3,2,1,0:T(8,128)(2,1)}), bf16[4,2,128,512]{3,2,1,0:T(8,128)(2,1)S(1)}, u32[]{:S(2)}, u32[]{:S(2)}) async-start(bf16[4,2,128,512]{3,2,1,0:T(8,128)(2,1)} %prepare.1), calls=%async_computation | async-start | bytes 2097152 | tf_op jit(solution)/shard_map/all_to_all | solution.py:329
  8.6 2.3 %copy-start.13 = (s32[8,320]{1,0:T(8,128)}, s32[8,320]{1,0:T(8,128)S(1)}, u32[]{:S(2)}) copy-start(s32[8,320]{1,0:T(8,128)S(1)} %stack.3.rows_ref) | copy-start | bytes 30724
  18.4 10.2 %copy-start = (bf16[4,2,128,512]{3,2,1,0:T(8,128)(2,1)}, bf16[4,2,128,512]{3,2,1,0:T(8,128)(2,1)S(1)}, u32[]{:S(2)}) copy-start(bf16[4,2,128,512]{3,2,1,0:T(8,128)(2,1)S(1)} %all-to-all-done.own_ref.weights_ref) | copy-start | bytes 3145732
  18.4 10.2 %collective-permute-start = (bf16[4,2,128,512]{3,2,1,0:T(8,128)(2,1)S(1)}, bf16[4,2,128,512]{3,2,1,0:T(8,128)(2,1)S(1)}, u32[]{:S(2)}, u32[]{:S(2)}) collective-permute-start(bf16[4,2,128,512]{3,2,1,0:T(8,128)(2,1)S(1)} %all-to-all-done.own_ref.weights_ref), channel_id=1, source_target_pairs={{0,4},{4,0},{1,5},{5,1},{2,6},{6,2},{3,7},{7,3},{8,12},{12,8},{9,1... | collective-permute-start | bytes 3145736 | tf_op jit(solution)/shard_map/ppermute | solution.py:352
  26.3 1.0 copy-start.7
  27.2 0.7 copy-start.10
  27.9 0.9 copy-start.1
  27.9 0.9 copy-start.3
  27.9 0.9 copy-start.5
  27.9 0.9 copy-start.6
  27.9 1.0 copy-start.9
  28.7 3.6 %copy-start.2 = (bf16[4,2,128,512]{3,2,1,0:T(8,128)(2,1)}, bf16[4,2,128,512]{3,2,1,0:T(8,128)(2,1)S(1)}, u32[]{:S(2)}) copy-start(bf16[4,2,128,512]{3,2,1,0:T(8,128)(2,1)S(1)} %collective-permute-done.other_ref.weights_ref) | copy-start | bytes 3145732
  32.2 29.4 %all-to-all-start.1 = ((f32[128,2,128]{2,1,0:T(2,128)}), f32[128,2,128]{2,1,0:T(2,128)S(1)}, u32[]{:S(2)}, u32[]{:S(2)}) async-start(f32[128,2,128]{2,1,0:T(2,128)} %forward.1), calls=%async_computation.1 | async-start | bytes 262144 | tf_op jit(solution)/shard_map/all_to_all | solution.py:359
  55.3 8.5 %collective-permute-start.1 = (bf16[320,2176]{1,0:T(8,128)(2,1)}, bf16[320,2176]{1,0:T(8,128)(2,1)S(1)}, u32[]{:S(2)}, u32[]{:S(2)}) collective-permute-start(bf16[320,2176]{1,0:T(8,128)(2,1)} %get-tuple-element.18), channel_id=1, source_target_pairs={{0,4},{4,0},{1,5},{5,1},{2,6},{6,2},{3,7},{7,3},{8,12},{12,8},{9,1... | collective-permute-start | bytes 4177928 | tf_op jit(solution)/shard_map/ppermute | solution.py:366
  61.6 1.3 %copy-start.8 = (bf16[320,2176]{1,0:T(8,128)(2,1)S(1)}, bf16[320,2176]{1,0:T(8,128)(2,1)}, u32[]{:S(2)}) copy-start(bf16[320,2176]{1,0:T(8,128)(2,1)} %get-tuple-element.14.keep_ref) | copy-start | bytes 4177924
  81.9 23.2 %copy-start.4 = (f32[2,1024]{1,0:T(2,128)S(1)}, f32[2,1024]{1,0:T(2,128)}, u32[]{:S(2)}) copy-start(f32[2,1024]{1,0:T(2,128)} %momentum_ref.1) | copy-start | bytes 24580
  83.2 22.0 %all-to-all-start.3 = ((bf16[64,16,128]{2,1,0:T(8,128)(2,1)}), bf16[64,16,128]{2,1,0:T(8,128)(2,1)S(1)}, u32[]{:S(2)}, u32[]{:S(2)}) async-start(bf16[64,16,128]{2,1,0:T(8,128)(2,1)} %middle.1), calls=%async_computation.3 | async-start | bytes 524288 | tf_op jit(solution)/shard_map/all_to_all | solution.py:375

commit v6 on v4

--- a/solution.py
+++ b/solution.py
@@ -78,25 +78,30 @@
     )
 
 
+def start(sems, first, *pairs):
+    copies = [pltpu.make_async_copy(src, dst, sems.at[first + k]) for k, (src, dst) in enumerate(pairs)]
+    for copy in copies:
+        copy.start()
+    return copies
+
+
+def finish(copies):
+    for copy in copies:
+        copy.wait()
+
+
 def prepare_body(core_ref, w_in_hbm, w_down_hbm, out_hbm, w_in, w_down, mine, sems):
-    loads = [
-        pltpu.make_async_copy(w_in_hbm, w_in, sems.at[0]),
-        pltpu.make_async_copy(w_down_hbm, w_down, sems.at[1]),
-    ]
-    for load in loads:
-        load.start()
+    loads = start(sems, 0, (w_in_hbm, w_in), (w_down_hbm, w_down))
     unit, place = iota((PART, LANES), 0), iota((PART, LANES), 1)
     wanted = (place % 16) * 16 + core_ref[0] * 8 + place // 16
     chosen = (unit == wanted).astype(bf16)
     loads[0].wait()
     mine[0] = lax.dot_general(chosen, w_in[...], (((0,), (1,)), ((), ())), preferred_element_type=f32).astype(bf16)
+    stores = start(sems, 2, *[(mine.at[0], out_hbm.at[k, 0]) for k in range(N_X)])
     loads[1].wait()
     mine[1] = mm_tall(chosen, w_down[...]).astype(bf16)
-    stores = [pltpu.make_async_copy(mine, out_hbm.at[k], sems.at[2 + k]) for k in range(N_X)]
-    for store in stores:
-        store.start()
-    for store in stores:
-        store.wait()
+    stores += start(sems, 2 + N_X, *[(mine.at[1], out_hbm.at[k, 1]) for k in range(N_X)])
+    finish(stores)
 
 
 def attend_body(
@@ -189,14 +194,16 @@
     total_ref[...] = states.astype(f32) + half_forward(states, weights_ref, hidden_ref, slope_ref)
 
 
-def forward_body(
-    accept_ref, cols_ref, at_rank_ref, states_ref, partial_ref, weights_ref, gain_ref, head_ref,
-    message_ref, hidden_ref, slope_ref, unit_ref, signal_ref, scale_ref,
+def train_body(
+    accept_ref, cols_ref, at_rank_ref, states_ref, partial_ref, hidden_1_ref, slope_1_ref, own_ref, other_ref, gain_ref, head_ref,
+    message_ref, keep_ref, send_ref, hidden_ref, slope_ref, unit_ref,
 ):
-    unit, scale = norm_parts(partial_ref[...] + half_forward(states_ref[...], weights_ref, hidden_ref, slope_ref))
+    states = states_ref[...]
+    total = partial_ref[...] + half_forward(states, other_ref, hidden_ref, slope_ref)
+    unit, scale = norm_parts(total)
     unit_ref[...] = unit
-    scale_ref[...] = jnp.broadcast_to(scale, (ROWS, LANES))
-    high, low = split(unit * gain_ref[...])
+    gain = gain_ref[...]
+    high, low = split(unit * gain)
     head = wide_head(head_ref)
     logits = mm_flip(high, head) + mm_flip(low, head)
     lane = iota((ROWS, LANES), 1)
@@ -223,7 +230,6 @@
         share = e / jnp.sum(e, -1, keepdims=True) * accept_ref[s].astype(f32)
         shares = jnp.where(inside, share, shares)
     weight = jnp.sum(beams * shares, -1, keepdims=True)
-    signal_ref[...] = weight * (grown / mass - is_label.astype(f32))
     hits = cols_ref[:, 2:3] == lane
     sums = jnp.sum(jnp.where(hits, weight, 0.0), 0, keepdims=True)
     high, low = split(at_rank_ref[...] * (-weight * taken))
@@ -231,23 +237,16 @@
     message_ref[:, 0, :] = jnp.broadcast_to(sums, (N_DP, LANES))
     message_ref[:, 1, :] = mm_tall(hits16, high) + mm_tall(hits16, low)
 
-
-def backward_body(
-    cols_ref, states_ref, hidden_ref, slope_ref, weights_ref, hidden_2_ref, slope_2_ref, weights_2_ref, unit_ref, signal_ref,
-    scale_ref, gain_ref, head_ref, keep_ref, send_ref,
-):
+    high, low = split(weight * (grown / mass - is_label.astype(f32)))
     unit = unit_ref[...]
-    high, low = split(signal_ref[...])
-    head = wide_head(head_ref)
-    d_unit = gain_ref[...] * (mm(high, head) + mm(low, head))
+    d_unit = gain * (mm(high, head) + mm(low, head))
     along = jnp.mean(d_unit * unit, -1, keepdims=True)
-    d_total = scale_ref[:, 0:1] * (d_unit - jnp.mean(d_unit, -1, keepdims=True) - unit * along)
+    d_total = scale * (d_unit - jnp.mean(d_unit, -1, keepdims=True) - unit * along)
     d_out = d_total.astype(bf16)
-    states = states_ref[...]
     dest = jnp.broadcast_to(cols_ref[:, 2:3], (ROWS, LANES)).astype(f32).astype(bf16)
     for ref, hidden, slope, weights in (
-        (send_ref, hidden_2_ref, slope_2_ref, weights_2_ref),
-        (keep_ref, hidden_ref, slope_ref, weights_ref),
+        (send_ref, hidden_ref, slope_ref, other_ref),
+        (keep_ref, hidden_1_ref, slope_1_ref, own_ref),
     ):
         w_down = jnp.concatenate([weights[m, 1] for m in range(N_X)], 0)
         ref[:, 0:WIDTH] = (mm_flip(d_out, w_down) * slope[...]).astype(bf16)
@@ -257,29 +256,24 @@
         ref[:, 4 * WIDTH :] = dest
 
 
-def one_term(ref, got_ref, k):
+def term_body(keep_ref, other_ref, got_ref, term_ref, loss_ref, all_ref):
     sums = jnp.sum(got_ref[:, 0, :], 0, keepdims=True)
+    loss_ref[...] = got_ref[:, 1, :]
     inverse = 1.0 / jnp.maximum(sums, 1.0)
-    hits = ref[:, 4 * WIDTH :].astype(f32) == iota((ROWS, LANES), 1).astype(f32)
-    factor = jnp.sum(jnp.where(hits, inverse, 0.0), -1, keepdims=True)
-    scaled = (ref[:, (k + 2) * WIDTH : (k + 3) * WIDTH].astype(f32) * factor).astype(bf16)
-    return mm_tall(ref[:, k * WIDTH : (k + 1) * WIDTH], scaled)
-
-
-def first_body(keep_ref, got_ref, sum_ref, loss_ref):
-    loss_ref[...] = got_ref[:, 1, :]
+    lane = iota((ROWS, LANES), 1).astype(f32)
+    for place, ref in ((0, keep_ref), (1, other_ref)):
+        rows = slice(place * ROWS, (place + 1) * ROWS)
+        hits = ref[:, 4 * WIDTH :].astype(f32) == lane
+        factor = jnp.sum(jnp.where(hits, inverse, 0.0), -1, keepdims=True)
+        all_ref[rows, : 2 * WIDTH] = ref[:, : 2 * WIDTH]
+        all_ref[rows, 2 * WIDTH :] = (ref[:, 2 * WIDTH : 4 * WIDTH].astype(f32) * factor).astype(bf16)
     for k in range(2):
-        sum_ref[:, k * WIDTH : (k + 1) * WIDTH] = one_term(keep_ref, got_ref, k)
-
-
-def term_body(sum_ref, other_ref, got_ref, term_ref):
-    for k in range(2):
-        lanes = slice(k * WIDTH, (k + 1) * WIDTH)
-        grad = (sum_ref[:, lanes] + one_term(other_ref, got_ref, k)).astype(bf16)
+        grad = mm_tall(all_ref[:, k * WIDTH : (k + 1) * WIDTH], all_ref[:, (k + 2) * WIDTH : (k + 3) * WIDTH])
+        grad = grad.astype(bf16)
         for m in range(N_X):
             for x in range(N_X):
                 start = m * LANES + x * 32
-                term_ref[x, m * 32 : (m + 1) * 32, lanes] = grad[start : start + 32]
+                term_ref[x, m * 32 : (m + 1) * 32, k * WIDTH : (k + 1) * WIDTH] = grad[start : start + 32]
 
 
 def middle_body(got_ref, out_ref, held_ref):
@@ -317,7 +311,7 @@
             pltpu.VMEM((WIDTH, PART), bf16),
             pltpu.VMEM((PART, WIDTH), bf16),
             pltpu.VMEM((2, LANES, WIDTH), bf16),
-            pltpu.SemaphoreType.DMA((2 + N_X,)),
+            pltpu.SemaphoreType.DMA((2 + 2 * N_X,)),
         ],
         n_smem=1, n_any=2, out_hbm=True, limit=63_300_000, cost=1, name="prepare",
     )(core, w_in, w_down)
@@ -350,27 +344,20 @@
     )(states, own_w, done)
     gain = gain_ff.reshape(1, WIDTH)
     head = head.T
-    message, hidden_2, slope_2, unit, signal, scale = call(
-        forward_body,
-        [
-            ((N_DP, 2, LANES), f32),
-            (half, bf16),
-            (half, f32),
-            ((ROWS, WIDTH), f32),
-            ((ROWS, LANES), f32),
-            ((ROWS, LANES), f32),
-        ],
-        n_smem=1, n_in=7, cost=5, name="forward",
-    )(accept, cols, at_rank, states, partial, other_w, gain, head)
+    message, keep, send = call(
+        train_body,
+        [((N_DP, 2, LANES), f32), ((ROWS, PAY), bf16), ((ROWS, PAY), bf16)],
+        scratch=[pltpu.VMEM(half, bf16), pltpu.VMEM(half, f32), pltpu.VMEM((ROWS, WIDTH), f32)],
+        n_smem=1, n_in=10, cost=5, name="train",
+    )(accept, cols, at_rank, states, partial, hidden, slope, own_w, other_w, gain, head)
     got = lax.all_to_all(message, DP, 0, 0)
-    keep, send = call(
-        backward_body, [((ROWS, PAY), bf16), ((ROWS, PAY), bf16)], n_in=13, cost=4, name="backward"
-    )(cols, states, hidden, slope, own_w, hidden_2, slope_2, other_w, unit, signal, scale, gain, head)
     other = lax.ppermute(send, "core", swap)
-    first, loss = call(
-        first_body, [((HALF, 2 * WIDTH), f32), ((N_DP, LANES), f32)], n_in=2, cost=20, name="first"
-    )(keep, got)
-    term = call(term_body, [((N_X, LANES, 2 * WIDTH), bf16)], n_in=3, cost=4, name="term")(first, other, got)
+    term, loss = call(
+        term_body,
+        [((N_X, LANES, 2 * WIDTH), bf16), ((N_DP, LANES), f32)],
+        scratch=[pltpu.VMEM((2 * ROWS, 4 * WIDTH), bf16)],
+        n_in=3, cost=4, name="term",
+    )(keep, other, got)
     got = lax.all_to_all(term, "x", 0, 0)
     middle = call(
         middle_body, [((64, 16, LANES), bf16)], scratch=[pltpu.VMEM((64, 16, LANES), f32)], n_in=1, cost=1, name="middle"

time: 104 us -> 103 us (level)
  Pallas kernels: 18.2 us -> 17 us
    pallas_call x4 -> x2, Pallas kernels: 5.63 us -> 4.63 us  [the longest x1 3.45 us: per_device(): call(train_body, [((N_DP, 2, LANES), f32), ((ROWS, PAY), bf16), ((ROWS, P...]
    unnamed x31 -> x29, local copies, waits for them, and re-layouts: 3.53 us -> 3.41 us
  transfers between devices with their start and end apart: 4 -> 4, of which waited for: 1 -> 1; matrix products, arithmetic and copies ran while one was open for 4% -> 4% of each run, Pallas kernels for 9% -> 8%
where the time goes in v6:
time: 103 us; the launch traced here: 101 us
  blocking collectives  46.8 us (45%)
  starting transfers between devices  19.4 us (19%)
  Pallas kernels  17 us (17%)
  waiting for transfers between devices  11.7 us (11%)
  local copies, waits for them, and re-layouts  5.62 us (5%)
    all_to_all x1, blocking collectives, per_device(): got = lax.all_to_all(message, DP, 0, 0)  29.6 us
    all_to_all x1, blocking collectives, per_device(): got = lax.all_to_all(term, 'x', 0, 0)  17.2 us
    all_to_all x1, waiting for transfers between devices, per_device(): got = lax.all_to_all(middle, ('z', 'y'), 0, 0)  11.7 us
    ppermute x1, starting transfers between devices, per_device(): other_w = lax.ppermute(own_w, 'core', swap)  7.85 us
    pallas_call x1, Pallas kernels, per_device(): call(attend_body, [((ROWS, WIDTH), bf16), ((ROWS, LANES), f32), ((16, LAN...  7.42 us
    all_to_all x1, starting transfers between devices, per_device(): own_w = lax.all_to_all(mine, 'x', 0, 0)  4.99 us
    all_to_all x1, starting transfers between devices, per_device(): got = lax.all_to_all(middle, ('z', 'y'), 0, 0)  4.61 us
    pallas_call x1, Pallas kernels, per_device(): call(train_body, [((N_DP, 2, LANES), f32), ((ROWS, PAY), bf16), ((ROWS, P...  3.45 us
  transfers between devices with their start and end apart: 4, of which 1 were waited for; matrix products, arithmetic and copies ran while one was open for 4% of the time, Pallas kernels for 8%

profile of v6, /device:TPU:1, one launch (start us, length us, event | category | flops | bytes accessed | tf_op | source)
XLA Modules:
  0.0 101.4 jit_solution(13977097295407682472)
XLA Ops:
  0.6 2.2 %prepare.1 = bf16[4,2,128,512]{3,2,1,0:T(8,128)(2,1)} custom-call(s32[1]{0:T(128)} %bitcast.3.core_ref, bf16[512,256]{1,0:T(8,128)(2,1)} %w_in_hbm.1, bf16[256,512]{1,0:T(8,128)(2,1)} %w_down_hbm.1), custom_call_target="tpu_custom_call" | custom-call | flops 500000000 | bytes 2000000 | tf_op jit(solution)/shard_map/prepare/pallas_call | solution.py:307
  2.9 0.0 copy-start.12
  2.9 0.0 copy-start.11
  2.9 0.0 copy-start.8
  2.9 0.0 copy-start.9
  2.9 5.0 %all-to-all-start = ((bf16[4,2,128,512]{3,2,1,0:T(8,128)(2,1)}), bf16[4,2,128,512]{3,2,1,0:T(8,128)(2,1)S(1)}, u32[]{:S(2)}, u32[]{:S(2)}) async-start(bf16[4,2,128,512]{3,2,1,0:T(8,128)(2,1)} %prepare.1), calls=%async_computation | async-start | bytes 2097152 | tf_op jit(solution)/shard_map/all_to_all | solution.py:318
  7.9 0.0 copy-done.12
  7.9 0.1 reshape.29
  8.0 0.1 reshape.30
  8.1 0.1 stack_reshape.16
  8.2 0.0 copy-done.11
  8.2 0.1 reshape.28
  8.3 0.1 pad_slice_fusion
  8.4 0.1 stack_reshape.7
  8.5 0.1 stack_reshape.6
  8.6 0.0 copy-start.10
  8.6 0.8 copy.37
  9.4 0.0 copy-done.8
  9.4 0.8 copy.38.keys_ref
  10.2 0.0 copy-done.9
  10.2 0.8 copy.39.values_ref
  10.9 0.0 copy-done.10
  10.9 7.4 %attend.1 = (bf16[320,512]{1,0:T(8,128)(2,1)}, f32[320,128]{1,0:T(8,128)}, bf16[16,128]{1,0:T(8,128)(2,1)}) custom-call(s32[320,8]{1,0:T(8,128)} %bitcast.7, s32[8,320]{1,0:T(8,128)} %copy-done.10, bf16[2,150,512]{2,1,0:T(8,128)(2,1)} %copy.38.keys_ref, bf16[2,150,512]{2,1,0:T(8,128)(2,1)} %copy.39.values_ref, bf16[28,512]{1,0:T(8,128)(2,1)} %embed_ref.1, ...), custom_call_target="tpu_custom_call" | custom-call | flops 4000000000 | bytes 16000000 | tf_op jit(solution)/shard_map/attend/pallas_call | solution.py:327
  18.4 0.0 all-to-all-done.weights_ref.own_ref
  18.4 7.8 %collective-permute-start = (bf16[4,2,128,512]{3,2,1,0:T(8,128)(2,1)S(1)}, bf16[4,2,128,512]{3,2,1,0:T(8,128)(2,1)S(1)}, u32[]{:S(2)}, u32[]{:S(2)}) collective-permute-start(bf16[4,2,128,512]{3,2,1,0:T(8,128)(2,1)S(1)} %all-to-all-done.weights_ref.own_ref), channel_id=1, source_target_pairs={{0,4},{4,0},{1,5},{5,1},{2,6},{6,2},{3,7},{7,3},{8,12},{12,8},{9,1... | collective-permute-start | bytes 3145736 | tf_op jit(solution)/shard_map/ppermute | solution.py:341
  26.2 0.0 copy-start.5
  26.3 1.0 copy-done.5
  27.2 0.0 copy-start.7
  27.2 0.7 copy-done.7
  27.9 0.0 copy-start
  27.9 0.0 copy-start.1
  27.9 0.0 copy-start.3
  27.9 0.0 copy-start.4
  27.9 0.0 copy-start.6
  27.9 0.8 own.1
  28.8 0.0 collective-permute-done.other_ref
  28.8 0.0 copy-done
  28.8 0.0 copy-done.1
  28.8 0.0 copy-done.3
  28.8 0.0 copy-done.4
  28.8 0.1 copy-done.6
  29.0 3.5 %train.1 = (f32[128,2,128]{2,1,0:T(2,128)S(1)}, bf16[320,2176]{1,0:T(8,128)(2,1)S(1)}, bf16[320,2176]{1,0:T(8,128)(2,1)S(1)}) custom-call(s32[2]{0:T(128)S(1)} %copy-done.4, s32[320,8]{1,0:T(8,128)S(1)} %bitcast.8, f32[320,128]{1,0:T(8,128)S(1)} %copy-done.6, bf16[320,512]{1,0:T(8,128)(2,1)S(1)} %copy-done.5, f32[320,512]{1,0:T(8,128)S(1)} %get-tuple-element.20.partial_ref, ...), custom_call_target="tpu_custom_call" | custom-call | flops 2500000000 | bytes 10000000 | tf_op jit(solution)/shard_map/train/pallas_call | solution.py:347
  32.4 1.9 %collective-permute-start.1 = (bf16[320,2176]{1,0:T(8,128)(2,1)S(1)}, bf16[320,2176]{1,0:T(8,128)(2,1)S(1)}, u32[]{:S(2)}, u32[]{:S(2)}) collective-permute-start(bf16[320,2176]{1,0:T(8,128)(2,1)S(1)} %get-tuple-element.24), channel_id=1, source_target_pairs={{0,4},{4,0},{1,5},{5,1},{2,6},{6,2},{3,7},{7,3},{8,12},{12,8},{9,1... | collective-permute-start | bytes 4177928 | tf_op jit(solution)/shard_map/ppermute | solution.py:354
  34.3 29.6 %all_to_all.20.got_ref = f32[128,2,128]{2,1,0:T(2,128)S(1)} all-to-all(f32[128,2,128]{2,1,0:T(2,128)S(1)} %get-tuple-element.25), channel_id=1, replica_groups=mesh['z'=8,'y'=8,'core'=2,'x'=4] {'z','y','core'}, dimensions={0} | all-to-all | bytes 262144 | tf_op jit(solution)/shard_map/all_to_all | solution.py:353
  63.9 0.0 collective-permute-done.1.other_ref
  63.9 1.2 %term.1 = (bf16[4,128,1024]{2,1,0:T(8,128)(2,1)S(1)}, f32[128,128]{1,0:T(8,128)S(1)}) custom-call(bf16[320,2176]{1,0:T(8,128)(2,1)S(1)} %get-tuple-element.23.keep_ref, bf16[320,2176]{1,0:T(8,128)(2,1)S(1)} %collective-permute-done.1.other_ref, f32[128,2,128]{2,1,0:T(2,128)S(1)} %all_to_all.20.got_ref), custom_call_target="tpu_custom_call" | custom-call | flops 2000000000 | bytes 8000000 | tf_op jit(solution)/shard_map/term/pallas_call | solution.py:355
  65.1 17.2 %all_to_all.21.got_ref = bf16[4,128,1024]{2,1,0:T(8,128)(2,1)S(1)} all-to-all(bf16[4,128,1024]{2,1,0:T(8,128)(2,1)S(1)} %get-tuple-element.26), channel_id=1, replica_groups=mesh['z'=8,'y'=8,'core'=2,'x'=4] {'x'}, dimensions={0} | all-to-all | bytes 2097152 | tf_op jit(solution)/shard_map/all_to_all | solution.py:361
  82.4 0.0 copy-start.2
  82.4 1.2 %middle.1 = bf16[64,16,128]{2,1,0:T(8,128)(2,1)} custom-call(bf16[4,128,1024]{2,1,0:T(8,128)(2,1)S(1)} %all_to_all.21.got_ref), custom_call_target="tpu_custom_call" | custom-call | flops 500000000 | bytes 2000000 | tf_op jit(solution)/shard_map/middle/pallas_call | solution.py:362
  83.6 4.6 %all-to-all-start.3 = ((bf16[64,16,128]{2,1,0:T(8,128)(2,1)}), bf16[64,16,128]{2,1,0:T(8,128)(2,1)S(1)}, u32[]{:S(2)}, u32[]{:S(2)}) async-start(bf16[64,16,128]{2,1,0:T(8,128)(2,1)} %middle.1), calls=%async_computation.3 | async-start | bytes 524288 | tf_op jit(solution)/shard_map/all_to_all | solution.py:365
  88.2 0.8 reshape.35
  89.0 11.7 %all-to-all-done.3.got_ref = bf16[64,16,128]{2,1,0:T(8,128)(2,1)S(1)} async-done(((bf16[64,16,128]{2,1,0:T(8,128)(2,1)}), bf16[64,16,128]{2,1,0:T(8,128)(2,1)S(1)}, u32[]{:S(2)}, u32[]{:S(2)}) %all-to-all-start.3) | async-done | bytes 262176 | tf_op jit(solution)/shard_map/all_to_all | solution.py:365
  100.7 0.0 copy-done.2
  100.7 0.7 final.1
  (5 shorter events, 0.1 us)
Async XLA Ops:
  2.9 5.0 %copy-start.12 = (s32[300,1]{0,1:T(1,128)S(1)}, s32[300,1]{0,1:T(1,128)}, u32[]{:S(2)}) copy-start(s32[300,1]{0,1:T(1,128)} %param.21) | copy-start | bytes 3604
  2.9 5.3 %copy-start.11 = (s32[2,5,31]{2,0,1:T(2,128)S(1)}, s32[2,5,31]{2,0,1:T(2,128)}, u32[]{:S(2)}) copy-start(s32[2,5,31]{2,0,1:T(2,128)} %param.19) | copy-start | bytes 3724
  2.9 6.5 %copy-start.8 = (bf16[2,150,512]{2,0,1:T(2,128)(2,1)S(1)}, bf16[2,150,512]{2,0,1:T(2,128)(2,1)}, u32[]{:S(2)}) copy-start(bf16[2,150,512]{2,0,1:T(2,128)(2,1)} %param.22) | copy-start | bytes 921604
  2.9 7.2 %copy-start.9 = (bf16[2,150,512]{2,0,1:T(2,128)(2,1)S(1)}, bf16[2,150,512]{2,0,1:T(2,128)(2,1)}, u32[]{:S(2)}) copy-start(bf16[2,150,512]{2,0,1:T(2,128)(2,1)} %param.23) | copy-start | bytes 921604
  2.9 15.4 %all-to-all-start = ((bf16[4,2,128,512]{3,2,1,0:T(8,128)(2,1)}), bf16[4,2,128,512]{3,2,1,0:T(8,128)(2,1)S(1)}, u32[]{:S(2)}, u32[]{:S(2)}) async-start(bf16[4,2,128,512]{3,2,1,0:T(8,128)(2,1)} %prepare.1), calls=%async_computation | async-start | bytes 2097152 | tf_op jit(solution)/shard_map/all_to_all | solution.py:318
  8.6 2.4 %copy-start.10 = (s32[8,320]{1,0:T(8,128)}, s32[8,320]{1,0:T(8,128)S(1)}, u32[]{:S(2)}) copy-start(s32[8,320]{1,0:T(8,128)S(1)} %stack.3.rows_ref) | copy-start | bytes 30724
  18.4 10.4 %collective-permute-start = (bf16[4,2,128,512]{3,2,1,0:T(8,128)(2,1)S(1)}, bf16[4,2,128,512]{3,2,1,0:T(8,128)(2,1)S(1)}, u32[]{:S(2)}, u32[]{:S(2)}) collective-permute-start(bf16[4,2,128,512]{3,2,1,0:T(8,128)(2,1)S(1)} %all-to-all-done.weights_ref.own_ref), channel_id=1, source_target_pairs={{0,4},{4,0},{1,5},{5,1},{2,6},{6,2},{3,7},{7,3},{8,12},{12,8},{9,1... | collective-permute-start | bytes 3145736 | tf_op jit(solution)/shard_map/ppermute | solution.py:341
  26.2 1.0 copy-start.5
  27.2 0.7 copy-start.7
  27.9 0.9 copy-start
  27.9 0.9 copy-start.1
  27.9 0.9 copy-start.3
  27.9 0.9 copy-start.4
  27.9 1.0 %copy-start.6 = (f32[320,128]{1,0:T(8,128)S(1)}, f32[320,128]{1,0:T(8,128)}, u32[]{:S(2)}) copy-start(f32[320,128]{1,0:T(8,128)} %get-tuple-element.15.at_rank_ref) | copy-start | bytes 491524
  32.4 31.5 %collective-permute-start.1 = (bf16[320,2176]{1,0:T(8,128)(2,1)S(1)}, bf16[320,2176]{1,0:T(8,128)(2,1)S(1)}, u32[]{:S(2)}, u32[]{:S(2)}) collective-permute-start(bf16[320,2176]{1,0:T(8,128)(2,1)S(1)} %get-tuple-element.24), channel_id=1, source_target_pairs={{0,4},{4,0},{1,5},{5,1},{2,6},{6,2},{3,7},{7,3},{8,12},{12,8},{9,1... | collective-permute-start | bytes 4177928 | tf_op jit(solution)/shard_map/ppermute | solution.py:354
  82.4 18.3 %copy-start.2 = (f32[2,1024]{1,0:T(2,128)S(1)}, f32[2,1024]{1,0:T(2,128)}, u32[]{:S(2)}) copy-start(f32[2,1024]{1,0:T(2,128)} %momentum_ref.1) | copy-start | bytes 24580
  83.6 17.1 %all-to-all-start.3 = ((bf16[64,16,128]{2,1,0:T(8,128)(2,1)}), bf16[64,16,128]{2,1,0:T(8,128)(2,1)S(1)}, u32[]{:S(2)}, u32[]{:S(2)}) async-start(bf16[64,16,128]{2,1,0:T(8,128)(2,1)} %middle.1), calls=%async_computation.3 | async-start | bytes 524288 | tf_op jit(solution)/shard_map/all_to_all | solution.py:365

commit v7 on v6

--- a/solution.py
+++ b/solution.py
@@ -30,6 +30,28 @@
 TALL = (((0,), (0,)), ((), ()))
 DP = ("z", "y", "core")
 EVERY = ("z", "y", "core", "x")
+SIDE = 8
+
+
+def index(z, y, core, x):
+    return ((z * SIDE + y) * 2 + core) * N_X + x
+
+
+def stages():
+    side, half, pair, ring = range(SIDE), range(SIDE // 2), range(2), range(N_X)
+    one = [[index(z, y, 0, x) for x in ring] for z in side for y in side]
+    two = [[index(z, y, 0, x) for z in side for y in side] for x in ring]
+    for a in half:
+        for b in half:
+            for x in ring:
+                one.append([index(2 * a + z, 2 * b + y, 1, x) for z in pair for y in pair])
+    for z in pair:
+        for y in pair:
+            two.append([index(2 * a + z, 2 * b + y, 1, x) for a in half for b in half for x in ring])
+    return one, two
+
+
+STAGE_1, STAGE_2 = stages()
 
 
 def mm(a, b):
@@ -93,7 +115,10 @@
 def prepare_body(core_ref, w_in_hbm, w_down_hbm, out_hbm, w_in, w_down, mine, sems):
     loads = start(sems, 0, (w_in_hbm, w_in), (w_down_hbm, w_down))
     unit, place = iota((PART, LANES), 0), iota((PART, LANES), 1)
-    wanted = (place % 16) * 16 + core_ref[0] * 8 + place // 16
+    block, row, rest = place // 32, place // 16 % 2, place % 16
+    first = rest * 16 + block * 2 + row
+    second = (block // 2 * 8 + rest // 4 * 2 + block % 2) * 16 + 8 + rest % 4 * 2 + row
+    wanted = jnp.where(core_ref[0] == 0, first, second)
     chosen = (unit == wanted).astype(bf16)
     loads[0].wait()
     mine[0] = lax.dot_general(chosen, w_in[...], (((0,), (1,)), ((), ())), preferred_element_type=f32).astype(bf16)
@@ -358,11 +383,11 @@
         scratch=[pltpu.VMEM((2 * ROWS, 4 * WIDTH), bf16)],
         n_in=3, cost=4, name="term",
     )(keep, other, got)
-    got = lax.all_to_all(term, "x", 0, 0)
+    got = lax.all_to_all(term, EVERY, 0, 0, axis_index_groups=STAGE_1)
     middle = call(
         middle_body, [((64, 16, LANES), bf16)], scratch=[pltpu.VMEM((64, 16, LANES), f32)], n_in=1, cost=1, name="middle"
     )(got)
-    got = lax.all_to_all(middle, ("z", "y"), 0, 0)
+    got = lax.all_to_all(middle, EVERY, 0, 0, axis_index_groups=STAGE_2)
     out = call(final_body, [((2, 2 * WIDTH), f32)], n_in=2, cost=1, name="final")(got, momentum)
     return out, loss[:, :CAP].reshape(1, N_DP * CAP)
 

time: 103 us -> 99.8 us (0.969); the launches traced: 101 us -> 99.3 us
  blocking collectives: 46.8 us -> 41.1 us
  waiting for transfers between devices: 11.7 us -> 15.1 us
    all_to_all x1, blocking collectives: 17.2 us -> 11.5 us  [per_device(): got = lax.all_to_all(term, EVERY, 0, 0, axis_index_groups=STAGE_1)]
    all_to_all x1, waiting for transfers between devices: 11.7 us -> 15.1 us  [per_device(): got = lax.all_to_all(middle, EVERY, 0, 0, axis_index_groups=STAGE_2)]
where the time goes in v7:
time: 99.8 us; the launch traced here: 99.3 us
  blocking collectives  41.1 us (41%)
  starting transfers between devices  19.6 us (20%)
  Pallas kernels  17 us (17%)
  waiting for transfers between devices  15.1 us (15%)
  local copies, waits for them, and re-layouts  5.62 us (6%)
    all_to_all x1, blocking collectives, per_device(): got = lax.all_to_all(message, DP, 0, 0)  29.6 us
    all_to_all x1, waiting for transfers between devices, per_device(): got = lax.all_to_all(middle, EVERY, 0, 0, axis_index_groups=STAGE_2)  15.1 us
    all_to_all x1, blocking collectives, per_device(): got = lax.all_to_all(term, EVERY, 0, 0, axis_index_groups=STAGE_1)  11.5 us
    ppermute x1, starting transfers between devices, per_device(): other_w = lax.ppermute(own_w, 'core', swap)  7.85 us
    pallas_call x1, Pallas kernels, per_device(): call(attend_body, [((ROWS, WIDTH), bf16), ((ROWS, LANES), f32), ((16, LAN...  7.42 us
    all_to_all x1, starting transfers between devices, per_device(): own_w = lax.all_to_all(mine, 'x', 0, 0)  4.99 us
    all_to_all x1, starting transfers between devices, per_device(): got = lax.all_to_all(middle, EVERY, 0, 0, axis_index_groups=STAGE_2)  4.89 us
    pallas_call x1, Pallas kernels, per_device(): call(train_body, [((N_DP, 2, LANES), f32), ((ROWS, PAY), bf16), ((ROWS, P...  3.45 us
  transfers between devices with their start and end apart: 4, of which 1 were waited for; matrix products, arithmetic and copies ran while one was open for 4% of the time, Pallas kernels for 8%

profile of v7, /device:TPU:1, one launch (start us, length us, event | category | flops | bytes accessed | tf_op | source)
XLA Modules:
  0.0 99.3 jit_solution(17938378719859091324)
XLA Ops:
  0.6 2.2 %prepare.1 = bf16[4,2,128,512]{3,2,1,0:T(8,128)(2,1)} custom-call(s32[1]{0:T(128)} %bitcast.3.core_ref, bf16[512,256]{1,0:T(8,128)(2,1)} %w_in_hbm.1, bf16[256,512]{1,0:T(8,128)(2,1)} %w_down_hbm.1), custom_call_target="tpu_custom_call" | custom-call | flops 500000000 | bytes 2000000 | tf_op jit(solution)/shard_map/prepare/pallas_call | solution.py:332
  2.9 0.0 copy-start.12
  2.9 0.0 copy-start.11
  2.9 0.0 copy-start.8
  2.9 0.0 copy-start.9
  2.9 5.0 %all-to-all-start = ((bf16[4,2,128,512]{3,2,1,0:T(8,128)(2,1)}), bf16[4,2,128,512]{3,2,1,0:T(8,128)(2,1)S(1)}, u32[]{:S(2)}, u32[]{:S(2)}) async-start(bf16[4,2,128,512]{3,2,1,0:T(8,128)(2,1)} %prepare.1), calls=%async_computation | async-start | bytes 2097152 | tf_op jit(solution)/shard_map/all_to_all | solution.py:343
  7.9 0.0 copy-done.12
  7.9 0.1 reshape.29
  8.0 0.1 reshape.30
  8.1 0.1 stack_reshape.16
  8.2 0.0 copy-done.11
  8.2 0.1 reshape.28
  8.3 0.1 pad_slice_fusion
  8.4 0.1 stack_reshape.7
  8.5 0.1 stack_reshape.6
  8.6 0.0 copy-start.10
  8.6 0.8 copy.37
  9.4 0.0 copy-done.8
  9.4 0.8 copy.38.keys_ref
  10.2 0.0 copy-done.9
  10.2 0.8 copy.39.values_ref
  10.9 0.0 copy-done.10
  10.9 7.4 %attend.1 = (bf16[320,512]{1,0:T(8,128)(2,1)}, f32[320,128]{1,0:T(8,128)}, bf16[16,128]{1,0:T(8,128)(2,1)}) custom-call(s32[320,8]{1,0:T(8,128)} %bitcast.7, s32[8,320]{1,0:T(8,128)} %copy-done.10, bf16[2,150,512]{2,1,0:T(8,128)(2,1)} %copy.38.keys_ref, bf16[2,150,512]{2,1,0:T(8,128)(2,1)} %copy.39.values_ref, bf16[28,512]{1,0:T(8,128)(2,1)} %embed_ref.1, ...), custom_call_target="tpu_custom_call" | custom-call | flops 4000000000 | bytes 16000000 | tf_op jit(solution)/shard_map/attend/pallas_call | solution.py:352
  18.4 0.0 all-to-all-done.weights_ref.own_ref
  18.4 7.8 %collective-permute-start = (bf16[4,2,128,512]{3,2,1,0:T(8,128)(2,1)S(1)}, bf16[4,2,128,512]{3,2,1,0:T(8,128)(2,1)S(1)}, u32[]{:S(2)}, u32[]{:S(2)}) collective-permute-start(bf16[4,2,128,512]{3,2,1,0:T(8,128)(2,1)S(1)} %all-to-all-done.weights_ref.own_ref), channel_id=1, source_target_pairs={{0,4},{4,0},{1,5},{5,1},{2,6},{6,2},{3,7},{7,3},{8,12},{12,8},{9,1... | collective-permute-start | bytes 3145736 | tf_op jit(solution)/shard_map/ppermute | solution.py:366
  26.2 0.0 copy-start.5
  26.3 1.0 copy-done.5
  27.2 0.0 copy-start.7
  27.2 0.7 copy-done.7
  27.9 0.0 copy-start
  27.9 0.0 copy-start.1
  27.9 0.0 copy-start.3
  27.9 0.0 copy-start.4
  27.9 0.0 copy-start.6
  27.9 0.8 own.1
  28.8 0.0 collective-permute-done.other_ref
  28.8 0.0 copy-done
  28.8 0.0 copy-done.1
  28.8 0.0 copy-done.3
  28.8 0.0 copy-done.4
  28.8 0.1 copy-done.6
  29.0 3.5 %train.1 = (f32[128,2,128]{2,1,0:T(2,128)S(1)}, bf16[320,2176]{1,0:T(8,128)(2,1)S(1)}, bf16[320,2176]{1,0:T(8,128)(2,1)S(1)}) custom-call(s32[2]{0:T(128)S(1)} %copy-done.4, s32[320,8]{1,0:T(8,128)S(1)} %bitcast.8, f32[320,128]{1,0:T(8,128)S(1)} %copy-done.6, bf16[320,512]{1,0:T(8,128)(2,1)S(1)} %copy-done.5, f32[320,512]{1,0:T(8,128)S(1)} %get-tuple-element.20.partial_ref, ...), custom_call_target="tpu_custom_call" | custom-call | flops 2500000000 | bytes 10000000 | tf_op jit(solution)/shard_map/train/pallas_call | solution.py:372
  32.4 1.9 %collective-permute-start.1 = (bf16[320,2176]{1,0:T(8,128)(2,1)S(1)}, bf16[320,2176]{1,0:T(8,128)(2,1)S(1)}, u32[]{:S(2)}, u32[]{:S(2)}) collective-permute-start(bf16[320,2176]{1,0:T(8,128)(2,1)S(1)} %get-tuple-element.24), channel_id=1, source_target_pairs={{0,4},{4,0},{1,5},{5,1},{2,6},{6,2},{3,7},{7,3},{8,12},{12,8},{9,1... | collective-permute-start | bytes 4177928 | tf_op jit(solution)/shard_map/ppermute | solution.py:379
  34.3 29.6 %all_to_all.20.got_ref = f32[128,2,128]{2,1,0:T(2,128)S(1)} all-to-all(f32[128,2,128]{2,1,0:T(2,128)S(1)} %get-tuple-element.25), channel_id=1, replica_groups=mesh['z'=8,'y'=8,'core'=2,'x'=4] {'z','y','core'}, dimensions={0} | all-to-all | bytes 262144 | tf_op jit(solution)/shard_map/all_to_all | solution.py:378
  63.9 0.0 collective-permute-done.1.other_ref
  63.9 1.2 %term.1 = (bf16[4,128,1024]{2,1,0:T(8,128)(2,1)S(1)}, f32[128,128]{1,0:T(8,128)S(1)}) custom-call(bf16[320,2176]{1,0:T(8,128)(2,1)S(1)} %get-tuple-element.23.keep_ref, bf16[320,2176]{1,0:T(8,128)(2,1)S(1)} %collective-permute-done.1.other_ref, f32[128,2,128]{2,1,0:T(2,128)S(1)} %all_to_all.20.got_ref), custom_call_target="tpu_custom_call" | custom-call | flops 2000000000 | bytes 8000000 | tf_op jit(solution)/shard_map/term/pallas_call | solution.py:380
  65.1 11.5 %all_to_all.21.got_ref = bf16[4,128,1024]{2,1,0:T(8,128)(2,1)S(1)} all-to-all(bf16[4,128,1024]{2,1,0:T(8,128)(2,1)S(1)} %get-tuple-element.26), channel_id=1, replica_groups={{0,1,2,3},{8,9,10,11},{16,17,18,19},{24,25,26,27},{32,33,34,35},{40,41,..., dimensions={0} | all-to-all | bytes 2097152 | tf_op jit(solution)/shard_map/all_to_all | solution.py:386
  76.6 0.0 copy-start.2
  76.6 1.2 %middle.1 = bf16[64,16,128]{2,1,0:T(8,128)(2,1)} custom-call(bf16[4,128,1024]{2,1,0:T(8,128)(2,1)S(1)} %all_to_all.21.got_ref), custom_call_target="tpu_custom_call" | custom-call | flops 500000000 | bytes 2000000 | tf_op jit(solution)/shard_map/middle/pallas_call | solution.py:387
  77.8 4.9 %all-to-all-start.3 = ((bf16[64,16,128]{2,1,0:T(8,128)(2,1)}), bf16[64,16,128]{2,1,0:T(8,128)(2,1)S(1)}, u32[]{:S(2)}, u32[]{:S(2)}) async-start(bf16[64,16,128]{2,1,0:T(8,128)(2,1)} %middle.1), calls=%async_computation.3 | async-start | bytes 524288 | tf_op jit(solution)/shard_map/all_to_all | solution.py:390
  82.7 0.8 reshape.35
  83.5 15.1 %all-to-all-done.3.got_ref = bf16[64,16,128]{2,1,0:T(8,128)(2,1)S(1)} async-done(((bf16[64,16,128]{2,1,0:T(8,128)(2,1)}), bf16[64,16,128]{2,1,0:T(8,128)(2,1)S(1)}, u32[]{:S(2)}, u32[]{:S(2)}) %all-to-all-start.3) | async-done | bytes 262176 | tf_op jit(solution)/shard_map/all_to_all | solution.py:390
  98.6 0.0 copy-done.2
  98.6 0.7 final.1
  (5 shorter events, 0.1 us)
Async XLA Ops:
  2.9 5.0 %copy-start.12 = (s32[300,1]{0,1:T(1,128)S(1)}, s32[300,1]{0,1:T(1,128)}, u32[]{:S(2)}) copy-start(s32[300,1]{0,1:T(1,128)} %param.21) | copy-start | bytes 3604
  2.9 5.3 %copy-start.11 = (s32[2,5,31]{2,0,1:T(2,128)S(1)}, s32[2,5,31]{2,0,1:T(2,128)}, u32[]{:S(2)}) copy-start(s32[2,5,31]{2,0,1:T(2,128)} %param.19) | copy-start | bytes 3724
  2.9 6.5 %copy-start.8 = (bf16[2,150,512]{2,0,1:T(2,128)(2,1)S(1)}, bf16[2,150,512]{2,0,1:T(2,128)(2,1)}, u32[]{:S(2)}) copy-start(bf16[2,150,512]{2,0,1:T(2,128)(2,1)} %param.22) | copy-start | bytes 921604
  2.9 7.2 %copy-start.9 = (bf16[2,150,512]{2,0,1:T(2,128)(2,1)S(1)}, bf16[2,150,512]{2,0,1:T(2,128)(2,1)}, u32[]{:S(2)}) copy-start(bf16[2,150,512]{2,0,1:T(2,128)(2,1)} %param.23) | copy-start | bytes 921604
  2.9 15.4 %all-to-all-start = ((bf16[4,2,128,512]{3,2,1,0:T(8,128)(2,1)}), bf16[4,2,128,512]{3,2,1,0:T(8,128)(2,1)S(1)}, u32[]{:S(2)}, u32[]{:S(2)}) async-start(bf16[4,2,128,512]{3,2,1,0:T(8,128)(2,1)} %prepare.1), calls=%async_computation | async-start | bytes 2097152 | tf_op jit(solution)/shard_map/all_to_all | solution.py:343
  8.6 2.4 %copy-start.10 = (s32[8,320]{1,0:T(8,128)}, s32[8,320]{1,0:T(8,128)S(1)}, u32[]{:S(2)}) copy-start(s32[8,320]{1,0:T(8,128)S(1)} %stack.3.rows_ref) | copy-start | bytes 30724
  18.4 10.4 %collective-permute-start = (bf16[4,2,128,512]{3,2,1,0:T(8,128)(2,1)S(1)}, bf16[4,2,128,512]{3,2,1,0:T(8,128)(2,1)S(1)}, u32[]{:S(2)}, u32[]{:S(2)}) collective-permute-start(bf16[4,2,128,512]{3,2,1,0:T(8,128)(2,1)S(1)} %all-to-all-done.weights_ref.own_ref), channel_id=1, source_target_pairs={{0,4},{4,0},{1,5},{5,1},{2,6},{6,2},{3,7},{7,3},{8,12},{12,8},{9,1... | collective-permute-start | bytes 3145736 | tf_op jit(solution)/shard_map/ppermute | solution.py:366
  26.2 1.0 copy-start.5
  27.2 0.7 copy-start.7
  27.9 0.9 copy-start
  27.9 0.9 copy-start.1
  27.9 0.9 copy-start.3
  27.9 0.9 copy-start.4
  27.9 1.0 %copy-start.6 = (f32[320,128]{1,0:T(8,128)S(1)}, f32[320,128]{1,0:T(8,128)}, u32[]{:S(2)}) copy-start(f32[320,128]{1,0:T(8,128)} %get-tuple-element.15.at_rank_ref) | copy-start | bytes 491524
  32.4 31.5 %collective-permute-start.1 = (bf16[320,2176]{1,0:T(8,128)(2,1)S(1)}, bf16[320,2176]{1,0:T(8,128)(2,1)S(1)}, u32[]{:S(2)}, u32[]{:S(2)}) collective-permute-start(bf16[320,2176]{1,0:T(8,128)(2,1)S(1)} %get-tuple-element.24), channel_id=1, source_target_pairs={{0,4},{4,0},{1,5},{5,1},{2,6},{6,2},{3,7},{7,3},{8,12},{12,8},{9,1... | collective-permute-start | bytes 4177928 | tf_op jit(solution)/shard_map/ppermute | solution.py:379
  76.6 22.0 %copy-start.2 = (f32[2,1024]{1,0:T(2,128)S(1)}, f32[2,1024]{1,0:T(2,128)}, u32[]{:S(2)}) copy-start(f32[2,1024]{1,0:T(2,128)} %momentum_ref.1) | copy-start | bytes 24580
  77.8 20.8 %all-to-all-start.3 = ((bf16[64,16,128]{2,1,0:T(8,128)(2,1)}), bf16[64,16,128]{2,1,0:T(8,128)(2,1)S(1)}, u32[]{:S(2)}, u32[]{:S(2)}) async-start(bf16[64,16,128]{2,1,0:T(8,128)(2,1)} %middle.1), calls=%async_computation.3 | async-start | bytes 524288 | tf_op jit(solution)/shard_map/all_to_all | solution.py:390

commit v8 on v7

--- a/solution.py
+++ b/solution.py
@@ -114,17 +114,17 @@
 
 def prepare_body(core_ref, w_in_hbm, w_down_hbm, out_hbm, w_in, w_down, mine, sems):
     loads = start(sems, 0, (w_in_hbm, w_in), (w_down_hbm, w_down))
-    unit, place = iota((PART, LANES), 0), iota((PART, LANES), 1)
+    place, unit = iota((LANES, PART), 0), iota((LANES, PART), 1)
     block, row, rest = place // 32, place // 16 % 2, place % 16
     first = rest * 16 + block * 2 + row
     second = (block // 2 * 8 + rest // 4 * 2 + block % 2) * 16 + 8 + rest % 4 * 2 + row
     wanted = jnp.where(core_ref[0] == 0, first, second)
     chosen = (unit == wanted).astype(bf16)
     loads[0].wait()
-    mine[0] = lax.dot_general(chosen, w_in[...], (((0,), (1,)), ((), ())), preferred_element_type=f32).astype(bf16)
+    mine[0] = mm_flip(chosen, w_in[...]).astype(bf16)
     stores = start(sems, 2, *[(mine.at[0], out_hbm.at[k, 0]) for k in range(N_X)])
     loads[1].wait()
-    mine[1] = mm_tall(chosen, w_down[...]).astype(bf16)
+    mine[1] = mm(chosen, w_down[...]).astype(bf16)
     stores += start(sems, 2 + N_X, *[(mine.at[1], out_hbm.at[k, 1]) for k in range(N_X)])
     finish(stores)
 
@@ -144,7 +144,7 @@
     same = (beam_of(0) == beam_of(1)) & (iota((ROWS, ROWS), 0) <= iota((ROWS, ROWS), 1))
     same = same.astype(bf16)
     rank = jnp.sum(jnp.where(hits, before, 0.0), -1, keepdims=True).astype(jnp.int32)
-    at_rank_ref[...] = (rank == lane).astype(f32)
+    at_rank_ref[...] = (rank == lane).astype(bf16)
     embed = embed_ref[...]
     names = (iota((32, VOCAB), 0) == iota((32, VOCAB), 1)).astype(bf16)
     table = mm(names, embed).astype(bf16)
@@ -199,18 +199,16 @@
     return beam
 
 
-def wide_head(head_ref):
-    return mm((iota((LANES, VOCAB), 0) == iota((LANES, VOCAB), 1)).astype(bf16), head_ref[...]).astype(bf16)
-
-
 def half_forward(states, weights_ref, hidden_ref, slope_ref):
     w_in = jnp.concatenate([weights_ref[m, 0] for m in range(N_X)], 0)
     w_down = jnp.concatenate([weights_ref[m, 1] for m in range(N_X)], 0)
     pre = mm_flip(states, w_in)
-    tanh = jnp.tanh(0.7978845608028654 * (pre + 0.044715 * pre * pre * pre))
-    hidden = (0.5 * pre * (1.0 + tanh)).astype(bf16)
+    square = pre * pre
+    tanh = jnp.tanh(pre * (0.7978845608028654 + 0.035677408136300125 * square))
+    gate = 0.5 * (1.0 + tanh)
+    hidden = (pre * gate).astype(bf16)
     hidden_ref[...] = hidden
-    slope_ref[...] = 0.5 * (1.0 + tanh) + 0.5 * pre * (1.0 - tanh * tanh) * 0.7978845608028654 * (1.0 + 0.134145 * pre * pre)
+    slope_ref[...] = gate * (1.0 + pre * (1.0 - tanh) * (0.7978845608028654 + 0.10703222440890037 * square))
     return mm(hidden, w_down)
 
 
@@ -220,8 +218,8 @@
 
 
 def train_body(
-    accept_ref, cols_ref, at_rank_ref, states_ref, partial_ref, hidden_1_ref, slope_1_ref, own_ref, other_ref, gain_ref, head_ref,
-    message_ref, keep_ref, send_ref, hidden_ref, slope_ref, unit_ref,
+    accept_ref, cols_ref, rows_ref, at_rank_ref, states_ref, partial_ref, hidden_1_ref, slope_1_ref, own_ref, other_ref, gain_ref,
+    head_ref, message_ref, keep_ref, send_ref, hidden_ref, slope_ref, unit_ref,
 ):
     states = states_ref[...]
     total = partial_ref[...] + half_forward(states, other_ref, hidden_ref, slope_ref)
@@ -229,42 +227,47 @@
     unit_ref[...] = unit
     gain = gain_ref[...]
     high, low = split(unit * gain)
-    head = wide_head(head_ref)
-    logits = mm_flip(high, head) + mm_flip(low, head)
-    lane = iota((ROWS, LANES), 1)
-    logits = jnp.where(lane < VOCAB, logits, -1e30)
-    top = jnp.max(logits, -1, keepdims=True)
+    names = (iota((32, VOCAB), 0) == iota((32, VOCAB), 1)).astype(bf16)
+    head = mm(names, head_ref[...]).astype(bf16)
+    logits = mm_flip(head, high) + mm_flip(head, low)
+    word = iota((32, ROWS), 0)
+    logits = jnp.where(word < VOCAB, logits, -1e30)
+    top = jnp.max(logits, 0, keepdims=True)
     grown = jnp.exp(logits - top)
-    mass = jnp.sum(grown, -1, keepdims=True)
-    is_label = cols_ref[:, 1:2] == lane
-    taken = jnp.sum(jnp.where(is_label, logits, 0.0), -1, keepdims=True) - top - jnp.log(mass)
-    beam = beam_of(0)
-    row = iota((ROWS, 1), 0)
-    step = row - (row >= PAD).astype(jnp.int32) * PAD
-    beam = beam - (row >= PAD).astype(jnp.int32)
+    mass = jnp.sum(grown, 0, keepdims=True)
+    is_label = rows_ref[1:2, :] == word
+    taken = jnp.sum(jnp.where(is_label, logits, 0.0), 0, keepdims=True) - top - jnp.log(mass)
+    row = iota((1, ROWS), 1)
+    second = (row >= PAD).astype(jnp.int32)
+    beam = beam_of(1) - second
+    inside = row - second * PAD
+    step = inside
     for k in range(1, BEAM + 1):
         step = step - (step >= STEPS + 1).astype(jnp.int32) * (STEPS + 1)
-    inside = jnp.where(row >= PAD, row - PAD, row)
-    beams = jnp.where((beam == lane) & (step < STEPS) & (inside < SEG), 1.0, 0.0)
-    score = jnp.sum(beams * taken, 0, keepdims=True) / STEPS
-    place = iota((1, LANES), 1)
-    shares = jnp.zeros((1, LANES), f32)
+    beams = jnp.where((beam == iota((16, ROWS), 0)) & (step < STEPS) & (inside < SEG), 1.0, 0.0)
+    score = jnp.sum(beams * taken, 1, keepdims=True) / STEPS
+    place = iota((16, 1), 0)
+    shares = jnp.zeros((16, 1), f32)
     for s in range(2):
-        inside = (place >= s * BEAM) & (place < (s + 1) * BEAM)
-        e = jnp.where(inside, jnp.exp(score - jnp.max(jnp.where(inside, score, -1e30), -1, keepdims=True)), 0.0)
-        share = e / jnp.sum(e, -1, keepdims=True) * accept_ref[s].astype(f32)
-        shares = jnp.where(inside, share, shares)
-    weight = jnp.sum(beams * shares, -1, keepdims=True)
-    hits = cols_ref[:, 2:3] == lane
-    sums = jnp.sum(jnp.where(hits, weight, 0.0), 0, keepdims=True)
-    high, low = split(at_rank_ref[...] * (-weight * taken))
-    hits16 = hits.astype(bf16)
-    message_ref[:, 0, :] = jnp.broadcast_to(sums, (N_DP, LANES))
-    message_ref[:, 1, :] = mm_tall(hits16, high) + mm_tall(hits16, low)
+        mine = (place >= s * BEAM) & (place < (s + 1) * BEAM)
+        e = jnp.where(mine, jnp.exp(score - jnp.max(jnp.where(mine, score, -1e30), 0, keepdims=True)), 0.0)
+        share = e / jnp.sum(e, 0, keepdims=True) * accept_ref[s].astype(f32)
+        shares = jnp.where(mine, share, shares)
+    weight = jnp.sum(beams * shares, 0, keepdims=True)
+    to = rows_ref[2:3, :] == iota((LANES, ROWS), 0)
+    high, low = split(-weight * taken)
+    zero = jnp.zeros((1, ROWS), bf16)
+    at_rank = at_rank_ref[...]
+    slots = mm(jnp.where(to, high, zero), at_rank) + mm(jnp.where(to, low, zero), at_rank)
+    high, low = split(jnp.broadcast_to(weight, (8, ROWS)))
+    hits = (cols_ref[:, 2:3] == iota((ROWS, LANES), 1)).astype(bf16)
+    sums = mm(high, hits) + mm(low, hits)
+    message_ref[:, 0, :] = jnp.broadcast_to(sums[0:1], (N_DP, LANES))
+    message_ref[:, 1, :] = slots
 
     high, low = split(weight * (grown / mass - is_label.astype(f32)))
     unit = unit_ref[...]
-    d_unit = gain * (mm(high, head) + mm(low, head))
+    d_unit = gain * mm_tall(jnp.concatenate([high, low], 0), jnp.concatenate([head, head], 0))
     along = jnp.mean(d_unit * unit, -1, keepdims=True)
     d_total = scale * (d_unit - jnp.mean(d_unit, -1, keepdims=True) - unit * along)
     d_out = d_total.astype(bf16)
@@ -302,23 +305,29 @@
 
 
 def middle_body(got_ref, out_ref, held_ref):
-    total = got_ref[0].astype(f32)
-    for k in range(1, N_X):
-        total = total + got_ref[k].astype(f32)
     for m in range(N_X):
+        rows = slice(m * 32, (m + 1) * 32)
+        total = got_ref[0, rows].astype(f32) + got_ref[1, rows].astype(f32)
+        total = total + (got_ref[2, rows].astype(f32) + got_ref[3, rows].astype(f32))
+        here = slice(m * 16, (m + 1) * 16)
         for r in range(2):
             for c in range(8):
-                block = total[m * 32 + r * 16 : m * 32 + (r + 1) * 16, c * LANES : (c + 1) * LANES]
-                held_ref[m * 16 : (m + 1) * 16, r * 8 + c, :] = block
-    out_ref[...] = held_ref[...].astype(bf16)
-
-
-def final_body(got_ref, momentum_ref, out_ref):
+                held_ref[here, r * 8 + c, :] = total[r * 16 : (r + 1) * 16, c * LANES : (c + 1) * LANES]
+        out_ref[here] = held_ref[here].astype(bf16)
+
+
+def final_body(got_ref, momentum_ref, loss_ref, out_ref, slots_ref):
     total = jnp.sum(got_ref[...].astype(f32), 0)
     for r in range(2):
         for c in range(8):
             lanes = slice(c * LANES, (c + 1) * LANES)
             out_ref[r : r + 1, lanes] = 0.9 * momentum_ref[r : r + 1, lanes] + total[r * 8 + c : r * 8 + c + 1]
+    slot, source = iota((N_DP, N_DP * CAP), 1), iota((N_DP, N_DP * CAP), 0)
+    offset = slot - source * CAP
+    spread = jnp.zeros((N_DP, N_DP * CAP), f32)
+    for k in range(CAP):
+        spread = jnp.where(offset == k, loss_ref[:, k : k + 1], spread)
+    slots_ref[...] = jnp.sum(spread, 0, keepdims=True)
 
 
 def per_device(
@@ -351,7 +360,7 @@
     cols = rows.T
     states, at_rank, done = call(
         attend_body,
-        [((ROWS, WIDTH), bf16), ((ROWS, LANES), f32), ((16, LANES), bf16)],
+        [((ROWS, WIDTH), bf16), ((ROWS, LANES), bf16), ((16, LANES), bf16)],
         scratch=[
             pltpu.VMEM((ROWS, WIDTH), bf16),
             pltpu.VMEM((6, WIDTH, WIDTH), bf16),
@@ -373,8 +382,8 @@
         train_body,
         [((N_DP, 2, LANES), f32), ((ROWS, PAY), bf16), ((ROWS, PAY), bf16)],
         scratch=[pltpu.VMEM(half, bf16), pltpu.VMEM(half, f32), pltpu.VMEM((ROWS, WIDTH), f32)],
-        n_smem=1, n_in=10, cost=5, name="train",
-    )(accept, cols, at_rank, states, partial, hidden, slope, own_w, other_w, gain, head)
+        n_smem=1, n_in=11, cost=5, name="train",
+    )(accept, cols, rows, at_rank, states, partial, hidden, slope, own_w, other_w, gain, head)
     got = lax.all_to_all(message, DP, 0, 0)
     other = lax.ppermute(send, "core", swap)
     term, loss = call(
@@ -388,8 +397,9 @@
         middle_body, [((64, 16, LANES), bf16)], scratch=[pltpu.VMEM((64, 16, LANES), f32)], n_in=1, cost=1, name="middle"
     )(got)
     got = lax.all_to_all(middle, EVERY, 0, 0, axis_index_groups=STAGE_2)
-    out = call(final_body, [((2, 2 * WIDTH), f32)], n_in=2, cost=1, name="final")(got, momentum)
-    return out, loss[:, :CAP].reshape(1, N_DP * CAP)
+    return tuple(
+        call(final_body, [((2, 2 * WIDTH), f32), ((1, N_DP * CAP), f32)], n_in=3, cost=1, name="final")(got, momentum, loss)
+    )
 
 
 def solution(mesh):

time: 99.8 us -> 99 us (level)
  blocking collectives: 41.1 us -> 62.1 us
  waiting for transfers between devices: 15.1 us -> 0.01 us
  starting transfers between devices: 19.6 us -> 14.8 us
  Pallas kernels: 17 us -> 16 us
    all_to_all x0 -> x1, blocking collectives: none -> 21 us  [per_device(): got = lax.all_to_all(middle, EVERY, 0, 0, axis_index_groups=STAGE_2)]
    all_to_all x1 -> x0, waiting for transfers between devices: 15.1 us -> none  [per_device(): got = lax.all_to_all(middle, EVERY, 0, 0, axis_index_groups=STAGE_2)]
    all_to_all x1 -> x0, starting transfers between devices: 4.89 us -> none  [per_device(): got = lax.all_to_all(middle, EVERY, 0, 0, axis_index_groups=STAGE_2)]
    unnamed x29 -> x31, local copies, waits for them, and re-layouts: 3.41 us -> 3.33 us
  transfers between devices with their start and end apart: 4 -> 3, of which waited for: 1 -> 0; matrix products, arithmetic and copies ran while one was open for 4% -> 3% of each run, Pallas kernels for 8% -> 8%
where the time goes in v8:
time: 99 us; the launch traced here: 98.5 us
  blocking collectives  62.1 us (63%)
  Pallas kernels  16 us (16%)
  starting transfers between devices  14.8 us (15%)
  local copies, waits for them, and re-layouts  4.76 us (5%)
    all_to_all x1, blocking collectives, per_device(): got = lax.all_to_all(message, DP, 0, 0)  29.6 us
    all_to_all x1, blocking collectives, per_device(): got = lax.all_to_all(middle, EVERY, 0, 0, axis_index_groups=STAGE_2)  21 us
    all_to_all x1, blocking collectives, per_device(): got = lax.all_to_all(term, EVERY, 0, 0, axis_index_groups=STAGE_1)  11.5 us
    ppermute x1, starting transfers between devices, per_device(): other_w = lax.ppermute(own_w, 'core', swap)  7.86 us
    pallas_call x1, Pallas kernels, per_device(): call(attend_body, [((ROWS, WIDTH), bf16), ((ROWS, LANES), bf16), ((16, LA...  7.43 us
    all_to_all x1, starting transfers between devices, per_device(): own_w = lax.all_to_all(mine, 'x', 0, 0)  4.99 us
    unnamed x31, local copies, waits for them, and re-layouts  3.33 us
    pallas_call x1, Pallas kernels, per_device(): call(train_body, [((N_DP, 2, LANES), f32), ((ROWS, PAY), bf16), ((ROWS, P...  2.92 us
  transfers between devices with their start and end apart: 3, of which 0 were waited for; matrix products, arithmetic and copies ran while one was open for 3% of the time, Pallas kernels for 8%

profile of v8, /device:TPU:1, one launch (start us, length us, event | category | flops | bytes accessed | tf_op | source)
XLA Modules:
  0.0 98.5 jit_solution(4271616845032554056)
XLA Ops:
  0.6 2.3 %prepare.1 = bf16[4,2,128,512]{3,2,1,0:T(8,128)(2,1)} custom-call(s32[1]{0:T(128)} %bitcast.3.core_ref, bf16[512,256]{1,0:T(8,128)(2,1)} %w_in_hbm.1, bf16[256,512]{1,0:T(8,128)(2,1)} %w_down_hbm.1), custom_call_target="tpu_custom_call" | custom-call | flops 500000000 | bytes 2000000 | tf_op jit(solution)/shard_map/prepare/pallas_call | solution.py:341
  2.9 0.0 copy-start.13
  2.9 0.0 copy-start.12
  3.0 0.0 copy-start.10
  3.0 0.0 copy-start.11
  3.0 5.0 %all-to-all-start = ((bf16[4,2,128,512]{3,2,1,0:T(8,128)(2,1)}), bf16[4,2,128,512]{3,2,1,0:T(8,128)(2,1)S(1)}, u32[]{:S(2)}, u32[]{:S(2)}) async-start(bf16[4,2,128,512]{3,2,1,0:T(8,128)(2,1)} %prepare.1), calls=%async_computation | async-start | bytes 2097152 | tf_op jit(solution)/shard_map/all_to_all | solution.py:352
  8.0 0.0 copy-done.13
  8.0 0.1 reshape.26
  8.1 0.1 reshape.27
  8.2 0.1 stack_reshape.16
  8.3 0.0 copy-done.12
  8.3 0.1 reshape.25
  8.3 0.1 pad_slice_fusion
  8.4 0.1 stack_reshape.7
  8.5 0.1 stack_reshape.6
  8.6 0.0 copy-start.1
  8.6 0.8 copy.29.cols_ref
  9.4 0.0 copy-done.10
  9.4 0.7 copy.27.keys_ref
  10.2 0.0 copy-done.11
  10.2 0.8 copy.28.values_ref
  11.0 0.0 copy-done.1
  11.0 7.4 %attend.1 = (bf16[320,512]{1,0:T(8,128)(2,1)}, bf16[320,128]{1,0:T(8,128)(2,1)}, bf16[16,128]{1,0:T(8,128)(2,1)}) custom-call(s32[320,8]{1,0:T(8,128)} %copy.29.cols_ref, s32[8,320]{1,0:T(8,128)} %copy-done.1, bf16[2,150,512]{2,1,0:T(8,128)(2,1)} %copy.27.keys_ref, bf16[2,150,512]{2,1,0:T(8,128)(2,1)} %copy.28.values_ref, bf16[28,512]{1,0:T(8,128)(2,1)} %embed_ref.1, ...), custom_call_target="tpu_custom_call" | custom-call | flops 4000000000 | bytes 16000000 | tf_op jit(solution)/shard_map/attend/pallas_call | solution.py:361
  18.4 0.0 all-to-all-done.weights_ref.own_ref
  18.4 7.9 %collective-permute-start = (bf16[4,2,128,512]{3,2,1,0:T(8,128)(2,1)S(1)}, bf16[4,2,128,512]{3,2,1,0:T(8,128)(2,1)S(1)}, u32[]{:S(2)}, u32[]{:S(2)}) collective-permute-start(bf16[4,2,128,512]{3,2,1,0:T(8,128)(2,1)S(1)} %all-to-all-done.weights_ref.own_ref), channel_id=1, source_target_pairs={{0,4},{4,0},{1,5},{5,1},{2,6},{6,2},{3,7},{7,3},{8,12},{12,8},{9,1... | collective-permute-start | bytes 3145736 | tf_op jit(solution)/shard_map/ppermute | solution.py:375
  26.3 0.0 copy-start.7
  26.3 1.0 copy-done.7
  27.3 0.0 copy-start.9
  27.3 0.7 copy-done.9
  27.9 0.0 copy-start
  27.9 0.0 copy-start.2
  27.9 0.0 copy-start.3
  28.0 0.0 copy-start.5
  28.0 0.0 copy-start.6
  28.0 0.0 copy-start.8
  28.0 0.8 own.1
  28.8 0.0 collective-permute-done.other_ref
  28.8 0.0 copy-done
  28.9 0.0 copy-done.2
  28.9 0.0 copy-done.3
  28.9 0.0 copy-done.5
  28.9 0.0 copy-done.6
  28.9 0.1 copy-done.8
  29.0 2.9 %train.1 = (f32[128,2,128]{2,1,0:T(2,128)S(1)}, bf16[320,2176]{1,0:T(8,128)(2,1)S(1)}, bf16[320,2176]{1,0:T(8,128)(2,1)S(1)}) custom-call(s32[2]{0:T(128)S(1)} %copy-done.6, s32[320,8]{1,0:T(8,128)S(1)} %copy-done, s32[8,320]{1,0:T(8,128)S(1)} %copy-done.2, bf16[320,128]{1,0:T(8,128)(2,1)S(1)} %copy-done.8, bf16[320,512]{1,0:T(8,128)(2,1)S(1)} %copy-done.7, ...), custom_call_target="tpu_custom_call" | custom-call | flops 2500000000 | bytes 10000000 | tf_op jit(solution)/shard_map/train/pallas_call | solution.py:381
  31.9 1.9 %collective-permute-start.1 = (bf16[320,2176]{1,0:T(8,128)(2,1)S(1)}, bf16[320,2176]{1,0:T(8,128)(2,1)S(1)}, u32[]{:S(2)}, u32[]{:S(2)}) collective-permute-start(bf16[320,2176]{1,0:T(8,128)(2,1)S(1)} %get-tuple-element.24), channel_id=1, source_target_pairs={{0,4},{4,0},{1,5},{5,1},{2,6},{6,2},{3,7},{7,3},{8,12},{12,8},{9,1... | collective-permute-start | bytes 4177928 | tf_op jit(solution)/shard_map/ppermute | solution.py:388
  33.8 29.6 %all_to_all.20.got_ref = f32[128,2,128]{2,1,0:T(2,128)S(1)} all-to-all(f32[128,2,128]{2,1,0:T(2,128)S(1)} %get-tuple-element.25), channel_id=1, replica_groups=mesh['z'=8,'y'=8,'core'=2,'x'=4] {'z','y','core'}, dimensions={0} | all-to-all | bytes 262144 | tf_op jit(solution)/shard_map/all_to_all | solution.py:387
  63.4 0.0 collective-permute-done.1.other_ref
  63.4 1.2 %term.1 = (bf16[4,128,1024]{2,1,0:T(8,128)(2,1)S(1)}, f32[128,128]{1,0:T(8,128)S(1)}) custom-call(bf16[320,2176]{1,0:T(8,128)(2,1)S(1)} %get-tuple-element.23.keep_ref, bf16[320,2176]{1,0:T(8,128)(2,1)S(1)} %collective-permute-done.1.other_ref, f32[128,2,128]{2,1,0:T(2,128)S(1)} %all_to_all.20.got_ref), custom_call_target="tpu_custom_call" | custom-call | flops 2000000000 | bytes 8000000 | tf_op jit(solution)/shard_map/term/pallas_call | solution.py:389
  64.6 11.5 %all_to_all.21.got_ref = bf16[4,128,1024]{2,1,0:T(8,128)(2,1)S(1)} all-to-all(bf16[4,128,1024]{2,1,0:T(8,128)(2,1)S(1)} %get-tuple-element.26), channel_id=1, replica_groups={{0,1,2,3},{8,9,10,11},{16,17,18,19},{24,25,26,27},{32,33,34,35},{40,41,..., dimensions={0} | all-to-all | bytes 2097152 | tf_op jit(solution)/shard_map/all_to_all | solution.py:395
  76.1 0.0 copy-start.4
  76.1 0.5 middle.1
  76.6 21.0 %all_to_all.22.got_ref = bf16[64,16,128]{2,1,0:T(8,128)(2,1)S(1)} all-to-all(bf16[64,16,128]{2,1,0:T(8,128)(2,1)S(1)} %middle.1), channel_id=1, replica_groups={{0,8,16,24,32,40,48,56,64,72,80,88,96,104,112,120,128,136,144,152,160,1..., dimensions={0} | all-to-all | bytes 524288 | tf_op jit(solution)/shard_map/all_to_all | solution.py:399
  97.6 0.0 copy-done.4
  97.6 0.9 final.1
  (5 shorter events, 0.1 us)
Async XLA Ops:
  2.9 5.0 %copy-start.13 = (s32[300,1]{0,1:T(1,128)S(1)}, s32[300,1]{0,1:T(1,128)}, u32[]{:S(2)}) copy-start(s32[300,1]{0,1:T(1,128)} %param.21) | copy-start | bytes 3604
  2.9 5.3 %copy-start.12 = (s32[2,5,31]{2,0,1:T(2,128)S(1)}, s32[2,5,31]{2,0,1:T(2,128)}, u32[]{:S(2)}) copy-start(s32[2,5,31]{2,0,1:T(2,128)} %param.19) | copy-start | bytes 3724
  3.0 6.5 %copy-start.10 = (bf16[2,150,512]{2,0,1:T(2,128)(2,1)S(1)}, bf16[2,150,512]{2,0,1:T(2,128)(2,1)}, u32[]{:S(2)}) copy-start(bf16[2,150,512]{2,0,1:T(2,128)(2,1)} %param.22) | copy-start | bytes 921604
  3.0 7.2 %copy-start.11 = (bf16[2,150,512]{2,0,1:T(2,128)(2,1)S(1)}, bf16[2,150,512]{2,0,1:T(2,128)(2,1)}, u32[]{:S(2)}) copy-start(bf16[2,150,512]{2,0,1:T(2,128)(2,1)} %param.23) | copy-start | bytes 921604
  3.0 15.4 %all-to-all-start = ((bf16[4,2,128,512]{3,2,1,0:T(8,128)(2,1)}), bf16[4,2,128,512]{3,2,1,0:T(8,128)(2,1)S(1)}, u32[]{:S(2)}, u32[]{:S(2)}) async-start(bf16[4,2,128,512]{3,2,1,0:T(8,128)(2,1)} %prepare.1), calls=%async_computation | async-start | bytes 2097152 | tf_op jit(solution)/shard_map/all_to_all | solution.py:352
  8.6 2.3 %copy-start.1 = (s32[8,320]{1,0:T(8,128)}, s32[8,320]{1,0:T(8,128)S(1)}, u32[]{:S(2)}) copy-start(s32[8,320]{1,0:T(8,128)S(1)} %stack.3.rows_ref) | copy-start | bytes 30724
  18.4 10.4 %collective-permute-start = (bf16[4,2,128,512]{3,2,1,0:T(8,128)(2,1)S(1)}, bf16[4,2,128,512]{3,2,1,0:T(8,128)(2,1)S(1)}, u32[]{:S(2)}, u32[]{:S(2)}) collective-permute-start(bf16[4,2,128,512]{3,2,1,0:T(8,128)(2,1)S(1)} %all-to-all-done.weights_ref.own_ref), channel_id=1, source_target_pairs={{0,4},{4,0},{1,5},{5,1},{2,6},{6,2},{3,7},{7,3},{8,12},{12,8},{9,1... | collective-permute-start | bytes 3145736 | tf_op jit(solution)/shard_map/ppermute | solution.py:375
  26.3 1.0 copy-start.7
  27.3 0.7 copy-start.9
  27.9 0.9 copy-start
  27.9 0.9 copy-start.2
  27.9 0.9 copy-start.3
  28.0 0.9 copy-start.5
  28.0 0.9 copy-start.6
  28.0 1.0 %copy-start.8 = (bf16[320,128]{1,0:T(8,128)(2,1)S(1)}, bf16[320,128]{1,0:T(8,128)(2,1)}, u32[]{:S(2)}) copy-start(bf16[320,128]{1,0:T(8,128)(2,1)} %get-tuple-element.15.at_rank_ref) | copy-start | bytes 245764
  31.9 31.5 %collective-permute-start.1 = (bf16[320,2176]{1,0:T(8,128)(2,1)S(1)}, bf16[320,2176]{1,0:T(8,128)(2,1)S(1)}, u32[]{:S(2)}, u32[]{:S(2)}) collective-permute-start(bf16[320,2176]{1,0:T(8,128)(2,1)S(1)} %get-tuple-element.24), channel_id=1, source_target_pairs={{0,4},{4,0},{1,5},{5,1},{2,6},{6,2},{3,7},{7,3},{8,12},{12,8},{9,1... | collective-permute-start | bytes 4177928 | tf_op jit(solution)/shard_map/ppermute | solution.py:388
  76.1 21.5 %copy-start.4 = (f32[2,1024]{1,0:T(2,128)S(1)}, f32[2,1024]{1,0:T(2,128)}, u32[]{:S(2)}) copy-start(f32[2,1024]{1,0:T(2,128)} %momentum_ref.1) | copy-start | bytes 24580

commit v9 on v8

--- a/solution.py
+++ b/solution.py
@@ -112,31 +112,31 @@
         copy.wait()
 
 
-def prepare_body(core_ref, w_in_hbm, w_down_hbm, out_hbm, w_in, w_down, mine, sems):
+def prepare_body(ids_ref, w_in_hbm, w_down_hbm, out_hbm, w_in, w_down, mine, sems):
     loads = start(sems, 0, (w_in_hbm, w_in), (w_down_hbm, w_down))
     place, unit = iota((LANES, PART), 0), iota((LANES, PART), 1)
     block, row, rest = place // 32, place // 16 % 2, place % 16
     first = rest * 16 + block * 2 + row
     second = (block // 2 * 8 + rest // 4 * 2 + block % 2) * 16 + 8 + rest % 4 * 2 + row
-    wanted = jnp.where(core_ref[0] == 0, first, second)
-    chosen = (unit == wanted).astype(bf16)
+    own = ids_ref[0] == 0
+    chosen = [(unit == jnp.where(own, first, second)).astype(bf16), (unit == jnp.where(own, second, first)).astype(bf16)]
     loads[0].wait()
-    mine[0] = mm_flip(chosen, w_in[...]).astype(bf16)
-    stores = start(sems, 2, *[(mine.at[0], out_hbm.at[k, 0]) for k in range(N_X)])
+    for k in range(2):
+        mine[k, 0] = mm_flip(chosen[k], w_in[...]).astype(bf16)
+    stores = start(sems, 2, *[(mine.at[k, 0], out_hbm.at[k, 0]) for k in range(2)])
     loads[1].wait()
-    mine[1] = mm(chosen, w_down[...]).astype(bf16)
-    stores += start(sems, 2 + N_X, *[(mine.at[1], out_hbm.at[k, 1]) for k in range(N_X)])
+    for k in range(2):
+        mine[k, 1] = mm(chosen[k], w_down[...]).astype(bf16)
+    stores += start(sems, 4, *[(mine.at[k, 1], out_hbm.at[k, 1]) for k in range(2)])
     finish(stores)
 
 
-def attend_body(
-    cols_ref, rows_ref, keys_ref, values_ref, embed_ref, gain_self_ref, gain_cross_ref, w_query_hbm, w_key_hbm,
-    w_value_hbm, w_self_hbm, cross_query_hbm, cross_out_hbm, states_ref, at_rank_ref, done_ref, ctx_ref, held, sems,
+def self_body(
+    cols_ref, rows_ref, embed_ref, gain_self_ref, w_query_hbm, w_key_hbm, w_value_hbm, w_self_hbm,
+    attended_ref, at_rank_ref, done_ref, held, sems,
 ):
-    sources = (w_query_hbm, w_key_hbm, w_value_hbm, w_self_hbm, cross_query_hbm, cross_out_hbm)
-    loads = [pltpu.make_async_copy(source, held.at[k], sems.at[k]) for k, source in enumerate(sources)]
-    for load in loads:
-        load.start()
+    sources = (w_query_hbm, w_key_hbm, w_value_hbm, w_self_hbm)
+    loads = start(sems, 0, *[(source, held.at[k]) for k, source in enumerate(sources)])
     lane = iota((ROWS, LANES), 1)
     hits = cols_ref[:, 2:3] == lane
     earlier = (iota((ROWS, ROWS), 0) > iota((ROWS, ROWS), 1)).astype(bf16)
@@ -151,8 +151,7 @@
     picks = (cols_ref[:, 0:1] == iota((ROWS, 32), 1)).astype(bf16)
     picks_t = (rows_ref[0:1, :] == iota((32, ROWS), 0)).astype(bf16)
     embedded = mm(picks, table)
-    for load in loads:
-        load.wait()
+    finish(loads)
     query = mm(embedded.astype(bf16), held[0]).astype(bf16)
     keyed = mm(table, held[1])
     valued = mm(table, held[2])
@@ -167,7 +166,21 @@
     context = mm_tall(probs.reshape(HEADS * 32, ROWS).astype(bf16), value_blocks).astype(bf16)
     unit, _ = norm_parts(embedded + mm(context, held[3]))
     attended = (unit * gain_self_ref[...]).astype(bf16)
-    cross_q = mm(attended, held[4]).astype(bf16)
+    attended_ref[...] = attended
+    done_ref[...] = attended[:16, :LANES]
+
+
+def cross_body(
+    attended_ref, gain_cross_ref, cross_query_hbm, keys_hbm, values_hbm, cross_out_hbm, states_ref, done_ref,
+    ctx_ref, held, keys_ref, values_ref, sems,
+):
+    loads = start(
+        sems, 0, (cross_query_hbm, held.at[0]), (keys_hbm, keys_ref), (values_hbm, values_ref), (cross_out_hbm, held.at[1])
+    )
+    attended = attended_ref[...]
+    loads[0].wait()
+    cross_q = mm(attended, held[0]).astype(bf16)
+    finish(loads[1:3])
     left = iota((PAD, LANES), 1) < 64
     for s in range(2):
         for pair in range(HEADS // 2):
@@ -182,7 +195,8 @@
                 p = (e / jnp.sum(e, -1, keepdims=True)).astype(bf16)
                 both.append(mm(p, v))
             ctx_ref[s * PAD : (s + 1) * PAD, lanes] = jnp.where(left, both[0], both[1]).astype(bf16)
-    unit, _ = norm_parts(attended.astype(f32) + mm(ctx_ref[...], held[5]))
+    loads[3].wait()
+    unit, _ = norm_parts(attended.astype(f32) + mm(ctx_ref[...], held[1]))
     states = (unit * gain_cross_ref[...]).astype(bf16)
     states_ref[...] = states
     done_ref[...] = states[:16, :LANES]
@@ -199,9 +213,9 @@
     return beam
 
 
-def half_forward(states, weights_ref, hidden_ref, slope_ref):
-    w_in = jnp.concatenate([weights_ref[m, 0] for m in range(N_X)], 0)
-    w_down = jnp.concatenate([weights_ref[m, 1] for m in range(N_X)], 0)
+def part_forward(states, blocks, hidden_ref, slope_ref):
+    w_in = jnp.concatenate([ref[at + (0,)] for ref, at in blocks], 0)
+    w_down = jnp.concatenate([ref[at + (1,)] for ref, at in blocks], 0)
     pre = mm_flip(states, w_in)
     square = pre * pre
     tanh = jnp.tanh(pre * (0.7978845608028654 + 0.035677408136300125 * square))
@@ -212,17 +226,18 @@
     return mm(hidden, w_down)
 
 
-def own_body(states_ref, weights_ref, done_ref, hidden_ref, slope_ref, total_ref):
+def own_body(states_ref, mine_ref, next_ref, last_ref, hidden_ref, slope_ref, total_ref):
     states = states_ref[...]
-    total_ref[...] = states.astype(f32) + half_forward(states, weights_ref, hidden_ref, slope_ref)
+    blocks = [(ref, (k,)) for ref in (mine_ref, next_ref, last_ref) for k in range(2)]
+    total_ref[...] = states.astype(f32) + part_forward(states, blocks, hidden_ref, slope_ref)
 
 
 def train_body(
-    accept_ref, cols_ref, rows_ref, at_rank_ref, states_ref, partial_ref, hidden_1_ref, slope_1_ref, own_ref, other_ref, gain_ref,
-    head_ref, message_ref, keep_ref, send_ref, hidden_ref, slope_ref, unit_ref,
+    accept_ref, ids_ref, cols_ref, rows_ref, at_rank_ref, states_ref, partial_ref, hidden_1_ref, slope_1_ref, mine_ref, next_ref,
+    last_ref, far_ref, far_2_ref, gain_ref, head_ref, message_ref, keep_ref, send_ref, hidden_ref, slope_ref, unit_ref,
 ):
     states = states_ref[...]
-    total = partial_ref[...] + half_forward(states, other_ref, hidden_ref, slope_ref)
+    total = partial_ref[...] + part_forward(states, [(far_ref, ()), (far_2_ref, ())], hidden_ref, slope_ref)
     unit, scale = norm_parts(total)
     unit_ref[...] = unit
     gain = gain_ref[...]
@@ -272,13 +287,23 @@
     d_total = scale * (d_unit - jnp.mean(d_unit, -1, keepdims=True) - unit * along)
     d_out = d_total.astype(bf16)
     dest = jnp.broadcast_to(cols_ref[:, 2:3], (ROWS, LANES)).astype(f32).astype(bf16)
-    for ref, hidden, slope, weights in (
-        (send_ref, hidden_ref, slope_ref, other_ref),
-        (keep_ref, hidden_1_ref, slope_1_ref, own_ref),
-    ):
-        w_down = jnp.concatenate([weights[m, 1] for m in range(N_X)], 0)
-        ref[:, 0:WIDTH] = (mm_flip(d_out, w_down) * slope[...]).astype(bf16)
-        ref[:, WIDTH : 2 * WIDTH] = hidden[...]
+    core, x = ids_ref[0], ids_ref[1]
+    one, three = lax.bitwise_xor(x, 1), lax.bitwise_xor(x, 3)
+    places = (x, jnp.where(core == 0, one, three), jnp.where(core == 0, three, one), lax.bitwise_xor(x, 2))
+    for k, ref, far in ((1, send_ref, far_2_ref), (0, keep_ref, far_ref)):
+        w_down = jnp.concatenate([mine_ref[k, 1], next_ref[k, 1], last_ref[1 - k, 1], far[1]], 0)
+        d_hidden = mm_flip(d_out, w_down)
+        blocks = (
+            (hidden_1_ref, slope_1_ref, k),
+            (hidden_1_ref, slope_1_ref, 2 + k),
+            (hidden_1_ref, slope_1_ref, 5 - k),
+            (hidden_ref, slope_ref, k),
+        )
+        for q, (hidden, slope, at) in enumerate(blocks):
+            lanes = slice(at * LANES, (at + 1) * LANES)
+            d_pre = (d_hidden[:, q * LANES : (q + 1) * LANES] * slope[:, lanes]).astype(bf16)
+            ref[:, pl.ds(pl.multiple_of(places[q] * LANES, LANES), LANES)] = d_pre
+            ref[:, pl.ds(pl.multiple_of(WIDTH + places[q] * LANES, LANES), LANES)] = hidden[:, lanes]
         ref[:, 2 * WIDTH : 3 * WIDTH] = states
         ref[:, 3 * WIDTH : 4 * WIDTH] = d_out
         ref[:, 4 * WIDTH :] = dest
@@ -316,7 +341,7 @@
         out_ref[here] = held_ref[here].astype(bf16)
 
 
-def final_body(got_ref, momentum_ref, loss_ref, out_ref, slots_ref):
+def final_body(got_ref, momentum_ref, loss_ref, done_ref, done_2_ref, out_ref, slots_ref):
     total = jnp.sum(got_ref[...].astype(f32), 0)
     for r in range(2):
         for c in range(8):
@@ -334,22 +359,26 @@
     tokens, accept, dest, mem_keys, mem_values, embed, w_query, w_key, w_value, w_self, cross_query, cross_out,
     gain_self, gain_cross, w_in, w_down, gain_ff, head, momentum,
 ):
-    core = lax.axis_index("core").astype(jnp.int32).reshape(1)
+    ids = jnp.stack([lax.axis_index("core"), lax.axis_index("x")]).astype(jnp.int32)
+    chip = ("core", "x")
     swap = [(0, 1), (1, 0)]
-    half = (ROWS, HALF)
+    ring = range(N_X)
+    near = [(x, x ^ 1) for x in ring] + [(N_X + x, N_X + (x ^ 3)) for x in ring]
+    far = [(x, N_X + (x ^ 3)) for x in ring] + [(N_X + x, x ^ 1) for x in ring]
+    shard = (2, 2, LANES, WIDTH)
 
     mine = call(
         prepare_body,
-        [((N_X, 2, LANES, WIDTH), bf16)],
+        [(shard, bf16)],
         scratch=[
             pltpu.VMEM((WIDTH, PART), bf16),
             pltpu.VMEM((PART, WIDTH), bf16),
-            pltpu.VMEM((2, LANES, WIDTH), bf16),
-            pltpu.SemaphoreType.DMA((2 + 2 * N_X,)),
+            pltpu.VMEM(shard, bf16),
+            pltpu.SemaphoreType.DMA((6,)),
         ],
         n_smem=1, n_any=2, out_hbm=True, limit=63_300_000, cost=1, name="prepare",
-    )(core, w_in, w_down)
-    own_w = lax.all_to_all(mine, "x", 0, 0)
+    )(ids, w_in, w_down)
+    next_w = lax.ppermute(mine, chip, near)
 
     flat = tokens.reshape(2, SEG)
     nexts = lax.pad(flat, jnp.int32(0), ((0, 0, 0), (-1, PAD - SEG + 1, 0))).reshape(ROWS)
@@ -358,32 +387,44 @@
     place = jnp.pad(place, ((0, 0), (0, PAD - SEG)), constant_values=-1).reshape(ROWS)
     rows = jnp.stack([flat, nexts, place, place, place, place, place, place])
     cols = rows.T
-    states, at_rank, done = call(
-        attend_body,
+    attended, at_rank, done = call(
+        self_body,
         [((ROWS, WIDTH), bf16), ((ROWS, LANES), bf16), ((16, LANES), bf16)],
+        scratch=[pltpu.VMEM((4, WIDTH, WIDTH), bf16), pltpu.SemaphoreType.DMA((4,))],
+        n_in=4, n_any=4, limit=61_300_000, cost=5, name="self",
+    )(cols, rows, embed, gain_self.reshape(1, WIDTH), w_query, w_key, w_value, w_self)
+    next_w, done = lax.optimization_barrier((next_w, done))
+    far_w = lax.ppermute(next_w[1], chip, far)
+    last_w = lax.ppermute(next_w, "core", swap)
+    states, done_2 = call(
+        cross_body,
+        [((ROWS, WIDTH), bf16), ((16, LANES), bf16)],
         scratch=[
             pltpu.VMEM((ROWS, WIDTH), bf16),
-            pltpu.VMEM((6, WIDTH, WIDTH), bf16),
-            pltpu.SemaphoreType.DMA((6,)),
+            pltpu.VMEM((2, WIDTH, WIDTH), bf16),
+            pltpu.VMEM((2, PEAKS, WIDTH), bf16),
+            pltpu.VMEM((2, PEAKS, WIDTH), bf16),
+            pltpu.SemaphoreType.DMA((4,)),
         ],
-        n_in=7, n_any=6, limit=61_300_000, cost=8, name="attend",
-    )(
-        cols, rows, mem_keys, mem_values, embed, gain_self.reshape(1, WIDTH), gain_cross.reshape(1, WIDTH),
-        w_query, w_key, w_value, w_self, cross_query, cross_out,
-    )
-    own_w, done = lax.optimization_barrier((own_w, done))
-    other_w = lax.ppermute(own_w, "core", swap)
+        n_in=2, n_any=4, limit=61_300_000, cost=5, name="cross",
+    )(attended, gain_cross.reshape(1, WIDTH), cross_query, mem_keys, mem_values, cross_out)
+    far_w, done_2 = lax.optimization_barrier((far_w, done_2))
+    far_2_w = lax.ppermute(far_w, "core", swap)
+    most = (ROWS, 6 * LANES)
+    rest = (ROWS, 2 * LANES)
     hidden, slope, partial = call(
-        own_body, [(half, bf16), (half, f32), ((ROWS, WIDTH), f32)], n_in=3, cost=2, name="own"
-    )(states, own_w, done)
+        own_body, [(most, bf16), (most, f32), ((ROWS, WIDTH), f32)], n_in=4, cost=2, name="own"
+    )(states, mine, next_w, last_w)
     gain = gain_ff.reshape(1, WIDTH)
     head = head.T
     message, keep, send = call(
         train_body,
         [((N_DP, 2, LANES), f32), ((ROWS, PAY), bf16), ((ROWS, PAY), bf16)],
-        scratch=[pltpu.VMEM(half, bf16), pltpu.VMEM(half, f32), pltpu.VMEM((ROWS, WIDTH), f32)],
-        n_smem=1, n_in=11, cost=5, name="train",
-    )(accept, cols, rows, at_rank, states, partial, hidden, slope, own_w, other_w, gain, head)
+        scratch=[pltpu.VMEM(rest, bf16), pltpu.VMEM(rest, f32), pltpu.VMEM((ROWS, WIDTH), f32)],
+        n_smem=2, n_in=14, cost=5, name="train",
+    )(
+        accept, ids, cols, rows, at_rank, states, partial, hidden, slope, mine, next_w, last_w, far_w, far_2_w, gain, head
+    )
     got = lax.all_to_all(message, DP, 0, 0)
     other = lax.ppermute(send, "core", swap)
     term, loss = call(
@@ -398,7 +439,9 @@
     )(got)
     got = lax.all_to_all(middle, EVERY, 0, 0, axis_index_groups=STAGE_2)
     return tuple(
-        call(final_body, [((2, 2 * WIDTH), f32), ((1, N_DP * CAP), f32)], n_in=3, cost=1, name="final")(got, momentum, loss)
+        call(final_body, [((2, 2 * WIDTH), f32), ((1, N_DP * CAP), f32)], n_in=5, cost=1, name="final")(
+            got, momentum, loss, done, done_2
+        )
     )
 
 

time: 99 us -> 105 us (1.061)
  starting transfers between devices: 14.8 us -> 19.5 us
  Pallas kernels: 16 us -> 19.7 us
  blocking collectives: 62.1 us -> 58.9 us
    ppermute x1 -> x4, starting transfers between devices: 7.86 us -> 17.1 us  [the longest x1 8.07 us: per_device(): last_w = lax.ppermute(next_w, 'core', swap)]
    all_to_all x1 -> x0, starting transfers between devices: 4.99 us -> none  [per_device(): own_w = lax.all_to_all(mine, 'x', 0, 0)]
    pallas_call x4 -> x5, Pallas kernels: 11.5 us -> 14.9 us  [the longest x1 5.38 us: per_device(): call(cross_body, [((ROWS, WIDTH), bf16), ((16, LANES), bf16)], scratch=[p...]
    all_to_all x1, blocking collectives: 29.6 us -> 26.9 us  [per_device(): got = lax.all_to_all(message, DP, 0, 0)]
    unnamed x31 -> x39, local copies, waits for them, and re-layouts: 3.33 us -> 2.54 us
  transfers between devices with their start and end apart: 3 -> 5, of which waited for: 0 -> 2; matrix products, arithmetic and copies ran while one was open for 3% -> 3% of each run, Pallas kernels for 8% -> 11%
where the time goes in v9:
time: 105 us; the launch traced here: 104 us
  blocking collectives  58.9 us (56%)
  Pallas kernels  19.7 us (19%)
  starting transfers between devices  19.5 us (19%)
  local copies, waits for them, and re-layouts  3.98 us (4%)
    all_to_all x1, blocking collectives, per_device(): got = lax.all_to_all(message, DP, 0, 0)  26.9 us
    all_to_all x1, blocking collectives, per_device(): got = lax.all_to_all(middle, EVERY, 0, 0, axis_index_groups=STAGE_2)  20.5 us
    all_to_all x1, blocking collectives, per_device(): got = lax.all_to_all(term, EVERY, 0, 0, axis_index_groups=STAGE_1)  11.5 us
    ppermute x1, starting transfers between devices, per_device(): last_w = lax.ppermute(next_w, 'core', swap)  8.07 us
    pallas_call x1, Pallas kernels, per_device(): call(cross_body, [((ROWS, WIDTH), bf16), ((16, LANES), bf16)], scratch=[p...  5.38 us
    ppermute x1, starting transfers between devices, per_device(): next_w = lax.ppermute(mine, chip, near)  5.22 us
    pallas_call x1, Pallas kernels, per_device(): call(self_body, [((ROWS, WIDTH), bf16), ((ROWS, LANES), bf16), ((16, LANE...  4.73 us
    pallas_call x1, Pallas kernels, per_device(): call(train_body, [((N_DP, 2, LANES), f32), ((ROWS, PAY), bf16), ((ROWS, P...  3.11 us
  transfers between devices with their start and end apart: 5, of which 2 were waited for; matrix products, arithmetic and copies ran while one was open for 3% of the time, Pallas kernels for 11%

profile of v9, /device:TPU:1, one launch (start us, length us, event | category | flops | bytes accessed | tf_op | source)
XLA Modules:
  0.0 104.3 jit_solution(5110356173921595735)
XLA Ops:
  0.6 0.0 copy-start.17
  0.6 0.0 copy-start.16
  0.7 0.6 pad_add_fusion.ids_ref
  1.3 2.9 %prepare.1.mine_ref = bf16[2,2,128,512]{3,2,1,0:T(8,128)(2,1)} custom-call(s32[2]{0:T(128)} %pad_add_fusion.ids_ref, bf16[512,256]{1,0:T(8,128)(2,1)} %w_in_hbm.1, bf16[256,512]{1,0:T(8,128)(2,1)} %w_down_hbm.1), custom_call_target="tpu_custom_call" | custom-call | flops 500000000 | bytes 2000000 | tf_op jit(solution)/shard_map/prepare/pallas_call | solution.py:370
  4.2 5.2 %collective-permute-start = (bf16[2,2,128,512]{3,2,1,0:T(8,128)(2,1)}, bf16[2,2,128,512]{3,2,1,0:T(8,128)(2,1)S(1)}, u32[]{:S(2)}, u32[]{:S(2)}) collective-permute-start(bf16[2,2,128,512]{3,2,1,0:T(8,128)(2,1)} %prepare.1.mine_ref), channel_id=1, source_target_pairs={{0,1},{1,0},{2,3},{3,2},{4,7},{5,6},{6,5},{7,4},{8,9},{9,8},{10,11... | collective-permute-start | bytes 1572872 | tf_op jit(solution)/shard_map/ppermute | solution.py:381
  9.4 0.0 copy-done.17
  9.4 0.1 reshape.23
  9.5 0.1 reshape.24
  9.6 0.1 stack_reshape.16
  9.7 0.0 copy-done.16
  9.7 0.1 reshape.22
  9.8 0.1 pad_slice_fusion
  9.9 0.1 stack_reshape.7
  10.0 0.1 stack_reshape.6
  10.1 0.0 copy-start.1
  10.1 0.8 copy.29.cols_ref
  10.9 0.0 copy-done.1
  10.9 0.0 copy-start.15
  10.9 4.7 %self.1 = (bf16[320,512]{1,0:T(8,128)(2,1)}, bf16[320,128]{1,0:T(8,128)(2,1)}, bf16[16,128]{1,0:T(8,128)(2,1)}) custom-call(s32[320,8]{1,0:T(8,128)} %copy.29.cols_ref, s32[8,320]{1,0:T(8,128)} %copy-done.1, bf16[28,512]{1,0:T(8,128)(2,1)} %embed_ref.1, f32[1,512]{1,0:T(1,128)} %bitcast.12, bf16[512,512]{1,0:T(8,128)(2,1)} %w_query_hbm.1, ...), custom_call_target="tpu_custom_call" | custom-call | flops 2500000000 | bytes 10000000 | tf_op jit(solution)/shard_map/self/pallas_call | solution.py:390
  15.6 0.5 collective-permute-done.next_ref
  16.2 8.1 %collective-permute-start.1 = (bf16[2,2,128,512]{3,2,1,0:T(8,128)(2,1)S(1)}, bf16[2,2,128,512]{3,2,1,0:T(8,128)(2,1)S(1)}, u32[]{:S(2)}, u32[]{:S(2)}) collective-permute-start(bf16[2,2,128,512]{3,2,1,0:T(8,128)(2,1)S(1)} %collective-permute-done.next_ref), channel_id=1, source_target_pairs={{0,4},{4,0},{1,5},{5,1},{2,6},{6,2},{3,7},{7,3},{8,12},{12,8},{9,1... | collective-permute-start | bytes 1572872 | tf_op jit(solution)/shard_map/ppermute | solution.py:398
  24.3 1.9 %collective-permute-start.2 = (bf16[2,128,512]{2,1,0:T(8,128)(2,1)S(1)}, bf16[2,128,512]{2,1,0:T(8,128)(2,1)S(1)}, u32[]{:S(2)}, u32[]{:S(2)}) collective-permute-start(bf16[2,128,512]{2,1,0:T(8,128)(2,1)S(1)} %slice_bitcast_fusion), channel_id=1, source_target_pairs={{0,7},{1,6},{2,5},{3,4},{4,1},{5,0},{6,3},{7,2},{8,15},{9,14},{10,... | collective-permute-start | bytes 786440 | tf_op jit(solution)/shard_map/ppermute | solution.py:397
  26.2 0.0 copy-done.14
  26.2 0.7 copy.27.keys_hbm
  27.0 0.0 copy-done.15
  27.0 0.8 copy.28.values_hbm
  27.7 0.0 copy-start.3
  27.7 5.4 %cross.1 = (bf16[320,512]{1,0:T(8,128)(2,1)}, bf16[16,128]{1,0:T(8,128)(2,1)}) custom-call(bf16[320,512]{1,0:T(8,128)(2,1)} %get-tuple-element.20.attended_ref, f32[1,512]{1,0:T(1,128)} %bitcast.13, bf16[512,512]{1,0:T(8,128)(2,1)} %cross_query_hbm.1, bf16[2,150,512]{2,1,0:T(8,128)(2,1)} %copy.27.keys_hbm, bf16[2,150,512]{2,1,0:T(8,128)(2,1)} %copy.28.values_hbm, ...), custom_call_target="tpu_custom_call" | custom-call | flops 2500000000 | bytes 10000000 | tf_op jit(solution)/shard_map/cross/pallas_call | solution.py:399
  33.1 0.1 collective-permute-done.2.far_ref
  33.2 1.9 %collective-permute-start.3 = (bf16[2,128,512]{2,1,0:T(8,128)(2,1)S(1)}, bf16[2,128,512]{2,1,0:T(8,128)(2,1)S(1)}, u32[]{:S(2)}, u32[]{:S(2)}) collective-permute-start(bf16[2,128,512]{2,1,0:T(8,128)(2,1)S(1)} %collective-permute-done.2.far_ref), channel_id=1, source_target_pairs={{0,4},{4,0},{1,5},{5,1},{2,6},{6,2},{3,7},{7,3},{8,12},{12,8},{9,1... | collective-permute-start | bytes 786440 | tf_op jit(solution)/shard_map/ppermute | solution.py:412
  35.1 0.0 collective-permute-done.1.last_ref
  35.1 0.0 copy-done.3
  35.1 0.0 copy-start.9
  35.1 1.0 copy-done.9
  36.1 0.0 copy-start
  36.1 0.0 copy-start.2
  36.1 0.0 copy-start.4
  36.1 0.0 copy-start.6
  36.1 0.0 copy-start.7
  36.1 0.0 copy-start.8
  36.1 0.0 copy-start.10
  36.1 0.0 copy-start.11
  36.2 1.0 own.1
  37.2 0.0 collective-permute-done.3.far_2_ref
  37.2 0.0 copy-done
  37.2 0.0 copy-done.2
  37.2 0.0 copy-done.4
  37.2 0.0 copy-done.6
  37.2 0.0 copy-done.7
  37.2 0.0 copy-done.8
  37.2 0.0 copy-done.10
  37.2 0.0 copy-done.11
  37.3 3.1 %train.1 = (f32[128,2,128]{2,1,0:T(2,128)S(1)}, bf16[320,2176]{1,0:T(8,128)(2,1)S(1)}, bf16[320,2176]{1,0:T(8,128)(2,1)S(1)}) custom-call(s32[2]{0:T(128)S(1)} %copy-done.7, s32[2]{0:T(128)S(1)} %copy-done.8, s32[320,8]{1,0:T(8,128)S(1)} %copy-done, s32[8,320]{1,0:T(8,128)S(1)} %copy-done.2, bf16[320,128]{1,0:T(8,128)(2,1)S(1)} %copy-done.11, ...), custom_call_target="tpu_custom_call" | custom-call | flops 2500000000 | bytes 10000000 | tf_op jit(solution)/shard_map/train/pallas_call | solution.py:420
  40.4 2.4 %collective-permute-start.4 = (bf16[320,2176]{1,0:T(8,128)(2,1)S(1)}, bf16[320,2176]{1,0:T(8,128)(2,1)S(1)}, u32[]{:S(2)}, u32[]{:S(2)}) collective-permute-start(bf16[320,2176]{1,0:T(8,128)(2,1)S(1)} %get-tuple-element.30), channel_id=1, source_target_pairs={{0,4},{4,0},{1,5},{5,1},{2,6},{6,2},{3,7},{7,3},{8,12},{12,8},{9,1... | collective-permute-start | bytes 4177928 | tf_op jit(solution)/shard_map/ppermute | solution.py:429
  42.8 26.9 %all_to_all.15.got_ref = f32[128,2,128]{2,1,0:T(2,128)S(1)} all-to-all(f32[128,2,128]{2,1,0:T(2,128)S(1)} %get-tuple-element.31), channel_id=1, replica_groups=mesh['z'=8,'y'=8,'core'=2,'x'=4] {'z','y','core'}, dimensions={0} | all-to-all | bytes 262144 | tf_op jit(solution)/shard_map/all_to_all | solution.py:428
  69.7 0.0 collective-permute-done.4.other_ref
  69.7 1.2 %term.1 = (bf16[4,128,1024]{2,1,0:T(8,128)(2,1)S(1)}, f32[128,128]{1,0:T(8,128)S(1)}) custom-call(bf16[320,2176]{1,0:T(8,128)(2,1)S(1)} %get-tuple-element.29.keep_ref, bf16[320,2176]{1,0:T(8,128)(2,1)S(1)} %collective-permute-done.4.other_ref, f32[128,2,128]{2,1,0:T(2,128)S(1)} %all_to_all.15.got_ref), custom_call_target="tpu_custom_call" | custom-call | flops 2000000000 | bytes 8000000 | tf_op jit(solution)/shard_map/term/pallas_call | solution.py:430
  70.9 11.5 %all_to_all.16.got_ref = bf16[4,128,1024]{2,1,0:T(8,128)(2,1)S(1)} all-to-all(bf16[4,128,1024]{2,1,0:T(8,128)(2,1)S(1)} %get-tuple-element.32), channel_id=1, replica_groups={{0,1,2,3},{8,9,10,11},{16,17,18,19},{24,25,26,27},{32,33,34,35},{40,41,..., dimensions={0} | all-to-all | bytes 2097152 | tf_op jit(solution)/shard_map/all_to_all | solution.py:436
  82.4 0.4 middle.1
  82.9 20.5 %all_to_all.17.got_ref = bf16[64,16,128]{2,1,0:T(8,128)(2,1)S(1)} all-to-all(bf16[64,16,128]{2,1,0:T(8,128)(2,1)S(1)} %middle.1), channel_id=1, replica_groups={{0,8,16,24,32,40,48,56,64,72,80,88,96,104,112,120,128,136,144,152,160,1..., dimensions={0} | all-to-all | bytes 524288 | tf_op jit(solution)/shard_map/all_to_all | solution.py:440
  103.4 0.0 copy-done.5
  103.4 0.0 copy-done.12
  103.4 0.0 copy-done.13
  103.4 0.9 final.1
  (10 shorter events, 0.1 us)
Async XLA Ops:
  0.6 8.8 %copy-start.17 = (s32[300,1]{0,1:T(1,128)S(1)}, s32[300,1]{0,1:T(1,128)}, u32[]{:S(2)}) copy-start(s32[300,1]{0,1:T(1,128)} %param.21) | copy-start | bytes 3604
  0.6 9.1 %copy-start.16 = (s32[2,5,31]{2,0,1:T(2,128)S(1)}, s32[2,5,31]{2,0,1:T(2,128)}, u32[]{:S(2)}) copy-start(s32[2,5,31]{2,0,1:T(2,128)} %param.19) | copy-start | bytes 3724
  4.2 12.0 %collective-permute-start = (bf16[2,2,128,512]{3,2,1,0:T(8,128)(2,1)}, bf16[2,2,128,512]{3,2,1,0:T(8,128)(2,1)S(1)}, u32[]{:S(2)}, u32[]{:S(2)}) collective-permute-start(bf16[2,2,128,512]{3,2,1,0:T(8,128)(2,1)} %prepare.1.mine_ref), channel_id=1, source_target_pairs={{0,1},{1,0},{2,3},{3,2},{4,7},{5,6},{6,5},{7,4},{8,9},{9,8},{10,11... | collective-permute-start | bytes 1572872 | tf_op jit(solution)/shard_map/ppermute | solution.py:381
  10.1 0.8 copy-start.1
  10.9 15.3 %copy-start.14 = (bf16[2,150,512]{2,0,1:T(2,128)(2,1)S(1)}, bf16[2,150,512]{2,0,1:T(2,128)(2,1)}, u32[]{:S(2)}) copy-start(bf16[2,150,512]{2,0,1:T(2,128)(2,1)} %param.22) | copy-start | bytes 921604
  10.9 16.1 %copy-start.15 = (bf16[2,150,512]{2,0,1:T(2,128)(2,1)S(1)}, bf16[2,150,512]{2,0,1:T(2,128)(2,1)}, u32[]{:S(2)}) copy-start(bf16[2,150,512]{2,0,1:T(2,128)(2,1)} %param.23) | copy-start | bytes 921604
  16.2 18.9 %collective-permute-start.1 = (bf16[2,2,128,512]{3,2,1,0:T(8,128)(2,1)S(1)}, bf16[2,2,128,512]{3,2,1,0:T(8,128)(2,1)S(1)}, u32[]{:S(2)}, u32[]{:S(2)}) collective-permute-start(bf16[2,2,128,512]{3,2,1,0:T(8,128)(2,1)S(1)} %collective-permute-done.next_ref), channel_id=1, source_target_pairs={{0,4},{4,0},{1,5},{5,1},{2,6},{6,2},{3,7},{7,3},{8,12},{12,8},{9,1... | collective-permute-start | bytes 1572872 | tf_op jit(solution)/shard_map/ppermute | solution.py:398
  24.3 8.9 %collective-permute-start.2 = (bf16[2,128,512]{2,1,0:T(8,128)(2,1)S(1)}, bf16[2,128,512]{2,1,0:T(8,128)(2,1)S(1)}, u32[]{:S(2)}, u32[]{:S(2)}) collective-permute-start(bf16[2,128,512]{2,1,0:T(8,128)(2,1)S(1)} %slice_bitcast_fusion), channel_id=1, source_target_pairs={{0,7},{1,6},{2,5},{3,4},{4,1},{5,0},{6,3},{7,2},{8,15},{9,14},{10,... | collective-permute-start | bytes 786440 | tf_op jit(solution)/shard_map/ppermute | solution.py:397
  27.7 7.4 %copy-start.3 = (bf16[2,2,128,512]{3,2,1,0:T(8,128)(2,1)S(1)}, bf16[2,2,128,512]{3,2,1,0:T(8,128)(2,1)}, u32[]{:S(2)}) copy-start(bf16[2,2,128,512]{3,2,1,0:T(8,128)(2,1)} %prepare.1.mine_ref) | copy-start | bytes 1572868
  33.2 4.0 %collective-permute-start.3 = (bf16[2,128,512]{2,1,0:T(8,128)(2,1)S(1)}, bf16[2,128,512]{2,1,0:T(8,128)(2,1)S(1)}, u32[]{:S(2)}, u32[]{:S(2)}) collective-permute-start(bf16[2,128,512]{2,1,0:T(8,128)(2,1)S(1)} %collective-permute-done.2.far_ref), channel_id=1, source_target_pairs={{0,4},{4,0},{1,5},{5,1},{2,6},{6,2},{3,7},{7,3},{8,12},{12,8},{9,1... | collective-permute-start | bytes 786440 | tf_op jit(solution)/shard_map/ppermute | solution.py:412
  35.1 1.0 copy-start.9
  36.1 1.1 %copy-start = (s32[320,8]{1,0:T(8,128)S(1)}, s32[320,8]{1,0:T(8,128)}, u32[]{:S(2)}) copy-start(s32[320,8]{1,0:T(8,128)} %copy.29.cols_ref) | copy-start | bytes 30724
  36.1 1.1 %copy-start.2 = (s32[8,320]{1,0:T(8,128)S(1)}, s32[8,320]{1,0:T(8,128)}, u32[]{:S(2)}) copy-start(s32[8,320]{1,0:T(8,128)} %copy-done.1) | copy-start | bytes 30724
  36.1 1.1 %copy-start.4 = (bf16[512,28]{0,1:T(8,128)(2,1)S(1)}, bf16[512,28]{0,1:T(8,128)(2,1)}, u32[]{:S(2)}) copy-start(bf16[512,28]{0,1:T(8,128)(2,1)} %param.36) | copy-start | bytes 86020
  36.1 1.1 %copy-start.6 = (f32[512]{0:T(512)S(1)}, f32[512]{0:T(512)}, u32[]{:S(2)}) copy-start(f32[512]{0:T(512)} %param.35) | copy-start | bytes 6148
  36.1 1.1 %copy-start.7 = (s32[2]{0:T(128)S(1)}, s32[2]{0:T(128)}, u32[]{:S(2)}) copy-start(s32[2]{0:T(128)} %accept_ref.1) | copy-start | bytes 28
  36.1 1.1 %copy-start.8 = (s32[2]{0:T(128)S(1)}, s32[2]{0:T(128)}, u32[]{:S(2)}) copy-start(s32[2]{0:T(128)} %pad_add_fusion.ids_ref) | copy-start | bytes 28
  36.1 1.1 %copy-start.10 = (bf16[320,512]{1,0:T(8,128)(2,1)S(1)}, bf16[320,512]{1,0:T(8,128)(2,1)}, u32[]{:S(2)}) copy-start(bf16[320,512]{1,0:T(8,128)(2,1)} %get-tuple-element.21.states_ref) | copy-start | bytes 983044
  36.1 1.1 %copy-start.11 = (bf16[320,128]{1,0:T(8,128)(2,1)S(1)}, bf16[320,128]{1,0:T(8,128)(2,1)}, u32[]{:S(2)}) copy-start(bf16[320,128]{1,0:T(8,128)(2,1)} %get-tuple-element.19.at_rank_ref) | copy-start | bytes 245764
  40.4 29.3 %collective-permute-start.4 = (bf16[320,2176]{1,0:T(8,128)(2,1)S(1)}, bf16[320,2176]{1,0:T(8,128)(2,1)S(1)}, u32[]{:S(2)}, u32[]{:S(2)}) collective-permute-start(bf16[320,2176]{1,0:T(8,128)(2,1)S(1)} %get-tuple-element.30), channel_id=1, source_target_pairs={{0,4},{4,0},{1,5},{5,1},{2,6},{6,2},{3,7},{7,3},{8,12},{12,8},{9,1... | collective-permute-start | bytes 4177928 | tf_op jit(solution)/shard_map/ppermute | solution.py:429
  82.4 21.0 %copy-start.5 = (f32[2,1024]{1,0:T(2,128)S(1)}, f32[2,1024]{1,0:T(2,128)}, u32[]{:S(2)}) copy-start(f32[2,1024]{1,0:T(2,128)} %momentum_ref.1) | copy-start | bytes 24580
  82.4 21.0 %copy-start.12 = (bf16[16,128]{1,0:T(8,128)(2,1)S(1)}, bf16[16,128]{1,0:T(8,128)(2,1)}, u32[]{:S(2)}) copy-start(bf16[16,128]{1,0:T(8,128)(2,1)} %get-tuple-element.34.done_ref) | copy-start | bytes 12292
  82.4 21.0 %copy-start.13 = (bf16[16,128]{1,0:T(8,128)(2,1)S(1)}, bf16[16,128]{1,0:T(8,128)(2,1)}, u32[]{:S(2)}) copy-start(bf16[16,128]{1,0:T(8,128)(2,1)} %get-tuple-element.35.done_2_ref) | copy-start | bytes 12292

commit v10 on v8

--- a/solution.py
+++ b/solution.py
@@ -39,15 +39,16 @@
 
 def stages():
     side, half, pair, ring = range(SIDE), range(SIDE // 2), range(2), range(N_X)
-    one = [[index(z, y, 0, x) for x in ring] for z in side for y in side]
-    two = [[index(z, y, 0, x) for z in side for y in side] for x in ring]
+    one, two = [], []
     for a in half:
         for b in half:
             for x in ring:
-                one.append([index(2 * a + z, 2 * b + y, 1, x) for z in pair for y in pair])
+                one.append([index(2 * a + z, 2 * b + y, 0, x) for z in pair for y in pair])
     for z in pair:
         for y in pair:
-            two.append([index(2 * a + z, 2 * b + y, 1, x) for a in half for b in half for x in ring])
+            two.append([index(2 * a + z, 2 * b + y, 0, x) for a in half for b in half for x in ring])
+    one += [[index(z, y, 1, x) for x in ring] for z in side for y in side]
+    two += [[index(z, y, 1, x) for z in side for y in side] for x in ring]
     return one, two
 
 
@@ -116,8 +117,8 @@
     loads = start(sems, 0, (w_in_hbm, w_in), (w_down_hbm, w_down))
     place, unit = iota((LANES, PART), 0), iota((LANES, PART), 1)
     block, row, rest = place // 32, place // 16 % 2, place % 16
-    first = rest * 16 + block * 2 + row
-    second = (block // 2 * 8 + rest // 4 * 2 + block % 2) * 16 + 8 + rest % 4 * 2 + row
+    first = (block // 2 * 8 + rest // 4 * 2 + block % 2) * 16 + rest % 4 * 2 + row
+    second = rest * 16 + 8 + block * 2 + row
     wanted = jnp.where(core_ref[0] == 0, first, second)
     chosen = (unit == wanted).astype(bf16)
     loads[0].wait()

time: 99 us -> 97.2 us (0.982)
  the two profiles are of different devices: /device:TPU:1 before, /device:TPU:8 now
where the time goes in v10:
time: 97.2 us; the launch traced here: 96.7 us
  blocking collectives  61.7 us (63%)
  Pallas kernels  16 us (16%)
  starting transfers between devices  8.74 us (9%)
  waiting for transfers between devices  4.73 us (5%)
  local copies, waits for them, and re-layouts  4.7 us (5%)
    all_to_all x1, blocking collectives, per_device(): got = lax.all_to_all(message, DP, 0, 0)  29.1 us
    all_to_all x1, blocking collectives, per_device(): got = lax.all_to_all(middle, EVERY, 0, 0, axis_index_groups=STAGE_2)  20.1 us
    all_to_all x1, blocking collectives, per_device(): got = lax.all_to_all(term, EVERY, 0, 0, axis_index_groups=STAGE_1)  12.4 us
    pallas_call x1, Pallas kernels, per_device(): call(attend_body, [((ROWS, WIDTH), bf16), ((ROWS, LANES), bf16), ((16, LA...  7.43 us
    all_to_all x1, waiting for transfers between devices, per_device(): own_w = lax.all_to_all(mine, 'x', 0, 0)  4.65 us
    all_to_all x1, starting transfers between devices, per_device(): own_w = lax.all_to_all(mine, 'x', 0, 0)  4.43 us
    unnamed x31, local copies, waits for them, and re-layouts  3.27 us
    pallas_call x1, Pallas kernels, per_device(): call(train_body, [((N_DP, 2, LANES), f32), ((ROWS, PAY), bf16), ((ROWS, P...  2.92 us
  transfers between devices with their start and end apart: 3, of which 2 were waited for; matrix products, arithmetic and copies ran while one was open for 3% of the time, Pallas kernels for 9%

profile of v10, /device:TPU:8, one launch (start us, length us, event | category | flops | bytes accessed | tf_op | source)
XLA Modules:
  0.0 96.7 jit_solution(976708538171800975)
XLA Ops:
  0.6 2.3 %prepare.1 = bf16[4,2,128,512]{3,2,1,0:T(8,128)(2,1)} custom-call(s32[1]{0:T(128)} %bitcast.3.core_ref, bf16[512,256]{1,0:T(8,128)(2,1)} %w_in_hbm.1, bf16[256,512]{1,0:T(8,128)(2,1)} %w_down_hbm.1), custom_call_target="tpu_custom_call" | custom-call | flops 500000000 | bytes 2000000 | tf_op jit(solution)/shard_map/prepare/pallas_call | solution.py:342
  2.9 0.0 copy-start.13
  2.9 0.0 copy-start.12
  3.0 0.0 copy-start.10
  3.0 0.0 copy-start.11
  3.0 4.4 %all-to-all-start = ((bf16[4,2,128,512]{3,2,1,0:T(8,128)(2,1)}), bf16[4,2,128,512]{3,2,1,0:T(8,128)(2,1)S(1)}, u32[]{:S(2)}, u32[]{:S(2)}) async-start(bf16[4,2,128,512]{3,2,1,0:T(8,128)(2,1)} %prepare.1), calls=%async_computation | async-start | bytes 2097152 | tf_op jit(solution)/shard_map/all_to_all | solution.py:353
  7.4 0.0 copy-done.13
  7.4 0.1 reshape.26
  7.5 0.1 reshape.27
  7.6 0.1 stack_reshape.16
  7.7 0.0 copy-done.12
  7.7 0.1 reshape.25
  7.8 0.1 pad_slice_fusion
  7.9 0.1 stack_reshape.7
  8.0 0.1 stack_reshape.6
  8.1 0.0 copy-start.1
  8.1 0.8 copy.29.cols_ref
  8.9 0.0 copy-done.10
  8.9 0.7 copy.27.keys_ref
  9.6 0.0 copy-done.11
  9.6 0.8 copy.28.values_ref
  10.4 0.0 copy-done.1
  10.4 7.4 %attend.1 = (bf16[320,512]{1,0:T(8,128)(2,1)}, bf16[320,128]{1,0:T(8,128)(2,1)}, bf16[16,128]{1,0:T(8,128)(2,1)}) custom-call(s32[320,8]{1,0:T(8,128)} %copy.29.cols_ref, s32[8,320]{1,0:T(8,128)} %copy-done.1, bf16[2,150,512]{2,1,0:T(8,128)(2,1)} %copy.27.keys_ref, bf16[2,150,512]{2,1,0:T(8,128)(2,1)} %copy.28.values_ref, bf16[28,512]{1,0:T(8,128)(2,1)} %embed_ref.1, ...), custom_call_target="tpu_custom_call" | custom-call | flops 4000000000 | bytes 16000000 | tf_op jit(solution)/shard_map/attend/pallas_call | solution.py:362
  17.9 4.7 %all-to-all-done.weights_ref.own_ref = bf16[4,2,128,512]{3,2,1,0:T(8,128)(2,1)S(1)} async-done(((bf16[4,2,128,512]{3,2,1,0:T(8,128)(2,1)}), bf16[4,2,128,512]{3,2,1,0:T(8,128)(2,1)S(1)}, u32[]{:S(2)}, u32[]{:S(2)}) %all-to-all-start) | async-done | bytes 1048608 | tf_op jit(solution)/shard_map/all_to_all | solution.py:353
  22.5 1.9 %collective-permute-start = (bf16[4,2,128,512]{3,2,1,0:T(8,128)(2,1)S(1)}, bf16[4,2,128,512]{3,2,1,0:T(8,128)(2,1)S(1)}, u32[]{:S(2)}, u32[]{:S(2)}) collective-permute-start(bf16[4,2,128,512]{3,2,1,0:T(8,128)(2,1)S(1)} %all-to-all-done.weights_ref.own_ref), channel_id=1, source_target_pairs={{0,4},{4,0},{1,5},{5,1},{2,6},{6,2},{3,7},{7,3},{8,12},{12,8},{9,1... | collective-permute-start | bytes 3145736 | tf_op jit(solution)/shard_map/ppermute | solution.py:376
  24.4 0.0 copy-start.7
  24.4 1.0 copy-done.7
  25.4 0.0 copy-start.9
  25.4 0.7 copy-done.9
  26.1 0.0 copy-start
  26.1 0.0 copy-start.2
  26.1 0.0 copy-start.3
  26.1 0.0 copy-start.5
  26.1 0.0 copy-start.6
  26.1 0.0 copy-start.8
  26.1 0.9 own.1
  27.0 0.1 collective-permute-done.other_ref
  27.0 0.0 copy-done
  27.1 0.0 copy-done.2
  27.1 0.0 copy-done.3
  27.1 0.0 copy-done.5
  27.1 0.0 copy-done.6
  27.1 0.0 copy-done.8
  27.1 2.9 %train.1 = (f32[128,2,128]{2,1,0:T(2,128)S(1)}, bf16[320,2176]{1,0:T(8,128)(2,1)S(1)}, bf16[320,2176]{1,0:T(8,128)(2,1)S(1)}) custom-call(s32[2]{0:T(128)S(1)} %copy-done.6, s32[320,8]{1,0:T(8,128)S(1)} %copy-done, s32[8,320]{1,0:T(8,128)S(1)} %copy-done.2, bf16[320,128]{1,0:T(8,128)(2,1)S(1)} %copy-done.8, bf16[320,512]{1,0:T(8,128)(2,1)S(1)} %copy-done.7, ...), custom_call_target="tpu_custom_call" | custom-call | flops 2500000000 | bytes 10000000 | tf_op jit(solution)/shard_map/train/pallas_call | solution.py:382
  30.1 2.4 %collective-permute-start.1 = (bf16[320,2176]{1,0:T(8,128)(2,1)S(1)}, bf16[320,2176]{1,0:T(8,128)(2,1)S(1)}, u32[]{:S(2)}, u32[]{:S(2)}) collective-permute-start(bf16[320,2176]{1,0:T(8,128)(2,1)S(1)} %get-tuple-element.24), channel_id=1, source_target_pairs={{0,4},{4,0},{1,5},{5,1},{2,6},{6,2},{3,7},{7,3},{8,12},{12,8},{9,1... | collective-permute-start | bytes 4177928 | tf_op jit(solution)/shard_map/ppermute | solution.py:389
  32.5 29.1 %all_to_all.20.got_ref = f32[128,2,128]{2,1,0:T(2,128)S(1)} all-to-all(f32[128,2,128]{2,1,0:T(2,128)S(1)} %get-tuple-element.25), channel_id=1, replica_groups=mesh['z'=8,'y'=8,'core'=2,'x'=4] {'z','y','core'}, dimensions={0} | all-to-all | bytes 262144 | tf_op jit(solution)/shard_map/all_to_all | solution.py:388
  61.6 0.0 collective-permute-done.1.other_ref
  61.6 1.2 %term.1 = (bf16[4,128,1024]{2,1,0:T(8,128)(2,1)S(1)}, f32[128,128]{1,0:T(8,128)S(1)}) custom-call(bf16[320,2176]{1,0:T(8,128)(2,1)S(1)} %get-tuple-element.23.keep_ref, bf16[320,2176]{1,0:T(8,128)(2,1)S(1)} %collective-permute-done.1.other_ref, f32[128,2,128]{2,1,0:T(2,128)S(1)} %all_to_all.20.got_ref), custom_call_target="tpu_custom_call" | custom-call | flops 2000000000 | bytes 8000000 | tf_op jit(solution)/shard_map/term/pallas_call | solution.py:390
  62.8 12.4 %all_to_all.21.got_ref = bf16[4,128,1024]{2,1,0:T(8,128)(2,1)S(1)} all-to-all(bf16[4,128,1024]{2,1,0:T(8,128)(2,1)S(1)} %get-tuple-element.26), channel_id=1, replica_groups={{0,8,64,72},{1,9,65,73},{2,10,66,74},{3,11,67,75},{16,24,80,88},{17,25,..., dimensions={0} | all-to-all | bytes 2097152 | tf_op jit(solution)/shard_map/all_to_all | solution.py:396
  75.2 0.0 copy-start.4
  75.2 0.5 middle.1
  75.7 20.1 %all_to_all.22.got_ref = bf16[64,16,128]{2,1,0:T(8,128)(2,1)S(1)} all-to-all(bf16[64,16,128]{2,1,0:T(8,128)(2,1)S(1)} %middle.1), channel_id=1, replica_groups={{0,1,2,3,16,17,18,19,32,33,34,35,48,49,50,51,128,129,130,131,144,145,14..., dimensions={0} | all-to-all | bytes 524288 | tf_op jit(solution)/shard_map/all_to_all | solution.py:400
  95.8 0.0 copy-done.4
  95.8 0.9 final.1
  (5 shorter events, 0.1 us)
Async XLA Ops:
  2.9 4.5 %copy-start.13 = (s32[300,1]{0,1:T(1,128)S(1)}, s32[300,1]{0,1:T(1,128)}, u32[]{:S(2)}) copy-start(s32[300,1]{0,1:T(1,128)} %param.21) | copy-start | bytes 3604
  2.9 4.8 %copy-start.12 = (s32[2,5,31]{2,0,1:T(2,128)S(1)}, s32[2,5,31]{2,0,1:T(2,128)}, u32[]{:S(2)}) copy-start(s32[2,5,31]{2,0,1:T(2,128)} %param.19) | copy-start | bytes 3724
  3.0 5.9 %copy-start.10 = (bf16[2,150,512]{2,0,1:T(2,128)(2,1)S(1)}, bf16[2,150,512]{2,0,1:T(2,128)(2,1)}, u32[]{:S(2)}) copy-start(bf16[2,150,512]{2,0,1:T(2,128)(2,1)} %param.22) | copy-start | bytes 921604
  3.0 6.7 %copy-start.11 = (bf16[2,150,512]{2,0,1:T(2,128)(2,1)S(1)}, bf16[2,150,512]{2,0,1:T(2,128)(2,1)}, u32[]{:S(2)}) copy-start(bf16[2,150,512]{2,0,1:T(2,128)(2,1)} %param.23) | copy-start | bytes 921604
  3.0 19.5 %all-to-all-start = ((bf16[4,2,128,512]{3,2,1,0:T(8,128)(2,1)}), bf16[4,2,128,512]{3,2,1,0:T(8,128)(2,1)S(1)}, u32[]{:S(2)}, u32[]{:S(2)}) async-start(bf16[4,2,128,512]{3,2,1,0:T(8,128)(2,1)} %prepare.1), calls=%async_computation | async-start | bytes 2097152 | tf_op jit(solution)/shard_map/all_to_all | solution.py:353
  8.1 2.3 %copy-start.1 = (s32[8,320]{1,0:T(8,128)}, s32[8,320]{1,0:T(8,128)S(1)}, u32[]{:S(2)}) copy-start(s32[8,320]{1,0:T(8,128)S(1)} %stack.3.rows_ref) | copy-start | bytes 30724
  22.5 4.5 %collective-permute-start = (bf16[4,2,128,512]{3,2,1,0:T(8,128)(2,1)S(1)}, bf16[4,2,128,512]{3,2,1,0:T(8,128)(2,1)S(1)}, u32[]{:S(2)}, u32[]{:S(2)}) collective-permute-start(bf16[4,2,128,512]{3,2,1,0:T(8,128)(2,1)S(1)} %all-to-all-done.weights_ref.own_ref), channel_id=1, source_target_pairs={{0,4},{4,0},{1,5},{5,1},{2,6},{6,2},{3,7},{7,3},{8,12},{12,8},{9,1... | collective-permute-start | bytes 3145736 | tf_op jit(solution)/shard_map/ppermute | solution.py:376
  24.4 1.0 %copy-start.7 = (bf16[320,512]{1,0:T(8,128)(2,1)S(1)}, bf16[320,512]{1,0:T(8,128)(2,1)}, u32[]{:S(2)}) copy-start(bf16[320,512]{1,0:T(8,128)(2,1)} %get-tuple-element.16.states_ref) | copy-start | bytes 983044
  25.4 0.7 copy-start.9
  26.1 1.0 copy-start
  26.1 1.0 %copy-start.2 = (s32[8,320]{1,0:T(8,128)S(1)}, s32[8,320]{1,0:T(8,128)}, u32[]{:S(2)}) copy-start(s32[8,320]{1,0:T(8,128)} %copy-done.1) | copy-start | bytes 30724
  26.1 1.0 %copy-start.3 = (bf16[512,28]{0,1:T(8,128)(2,1)S(1)}, bf16[512,28]{0,1:T(8,128)(2,1)}, u32[]{:S(2)}) copy-start(bf16[512,28]{0,1:T(8,128)(2,1)} %param.36) | copy-start | bytes 86020
  26.1 1.0 %copy-start.5 = (f32[512]{0:T(512)S(1)}, f32[512]{0:T(512)}, u32[]{:S(2)}) copy-start(f32[512]{0:T(512)} %param.35) | copy-start | bytes 6148
  26.1 1.0 %copy-start.6 = (s32[2]{0:T(128)S(1)}, s32[2]{0:T(128)}, u32[]{:S(2)}) copy-start(s32[2]{0:T(128)} %accept_ref.1) | copy-start | bytes 28
  26.1 1.0 %copy-start.8 = (bf16[320,128]{1,0:T(8,128)(2,1)S(1)}, bf16[320,128]{1,0:T(8,128)(2,1)}, u32[]{:S(2)}) copy-start(bf16[320,128]{1,0:T(8,128)(2,1)} %get-tuple-element.15.at_rank_ref) | copy-start | bytes 245764
  30.1 31.5 %collective-permute-start.1 = (bf16[320,2176]{1,0:T(8,128)(2,1)S(1)}, bf16[320,2176]{1,0:T(8,128)(2,1)S(1)}, u32[]{:S(2)}, u32[]{:S(2)}) collective-permute-start(bf16[320,2176]{1,0:T(8,128)(2,1)S(1)} %get-tuple-element.24), channel_id=1, source_target_pairs={{0,4},{4,0},{1,5},{5,1},{2,6},{6,2},{3,7},{7,3},{8,12},{12,8},{9,1... | collective-permute-start | bytes 4177928 | tf_op jit(solution)/shard_map/ppermute | solution.py:389
  75.2 20.6 %copy-start.4 = (f32[2,1024]{1,0:T(2,128)S(1)}, f32[2,1024]{1,0:T(2,128)}, u32[]{:S(2)}) copy-start(f32[2,1024]{1,0:T(2,128)} %momentum_ref.1) | copy-start | bytes 24580

commit v11 on v10

--- a/solution.py
+++ b/solution.py
@@ -285,10 +285,14 @@
         ref[:, 4 * WIDTH :] = dest
 
 
-def term_body(keep_ref, other_ref, got_ref, term_ref, loss_ref, all_ref):
+def first_body(got_ref, inverse_ref, loss_ref):
     sums = jnp.sum(got_ref[:, 0, :], 0, keepdims=True)
+    inverse_ref[...] = jnp.broadcast_to(1.0 / jnp.maximum(sums, 1.0), (8, LANES))
     loss_ref[...] = got_ref[:, 1, :]
-    inverse = 1.0 / jnp.maximum(sums, 1.0)
+
+
+def term_body(keep_ref, other_ref, inverse_ref, term_ref, all_ref):
+    inverse = inverse_ref[0:1, :]
     lane = iota((ROWS, LANES), 1).astype(f32)
     for place, ref in ((0, keep_ref), (1, other_ref)):
         rows = slice(place * ROWS, (place + 1) * ROWS)
@@ -383,16 +387,17 @@
         train_body,
         [((N_DP, 2, LANES), f32), ((ROWS, PAY), bf16), ((ROWS, PAY), bf16)],
         scratch=[pltpu.VMEM(half, bf16), pltpu.VMEM(half, f32), pltpu.VMEM((ROWS, WIDTH), f32)],
-        n_smem=1, n_in=11, cost=5, name="train",
+        n_smem=1, n_in=11, limit=51500000, cost=5, name="train",
     )(accept, cols, rows, at_rank, states, partial, hidden, slope, own_w, other_w, gain, head)
     got = lax.all_to_all(message, DP, 0, 0)
     other = lax.ppermute(send, "core", swap)
-    term, loss = call(
+    inverse, loss = call(first_body, [((8, LANES), f32), ((N_DP, LANES), f32)], n_in=1, cost=40, name="first")(got)
+    term = call(
         term_body,
-        [((N_X, LANES, 2 * WIDTH), bf16), ((N_DP, LANES), f32)],
+        [((N_X, LANES, 2 * WIDTH), bf16)],
         scratch=[pltpu.VMEM((2 * ROWS, 4 * WIDTH), bf16)],
         n_in=3, cost=4, name="term",
-    )(keep, other, got)
+    )(keep, other, inverse)
     got = lax.all_to_all(term, EVERY, 0, 0, axis_index_groups=STAGE_1)
     middle = call(
         middle_body, [((64, 16, LANES), bf16)], scratch=[pltpu.VMEM((64, 16, LANES), f32)], n_in=1, cost=1, name="middle"

time: 97.2 us -> 97.8 us (level)
  the two profiles are of different devices: /device:TPU:8 before, /device:TPU:6 now
where the time goes in v11:
time: 97.8 us; the launch traced here: 97.3 us
  blocking collectives  34.5 us (35%)
  starting transfers between devices  29.3 us (30%)
  Pallas kernels  17.5 us (18%)
  waiting for transfers between devices  10.2 us (10%)
  local copies, waits for them, and re-layouts  4.83 us (5%)
    all_to_all x1, blocking collectives, per_device(): got = lax.all_to_all(middle, EVERY, 0, 0, axis_index_groups=STAGE_2)  22.1 us
    all_to_all x1, starting transfers between devices, per_device(): got = lax.all_to_all(message, DP, 0, 0)  15.9 us
    all_to_all x1, blocking collectives, per_device(): got = lax.all_to_all(term, EVERY, 0, 0, axis_index_groups=STAGE_1)  12.4 us
    all_to_all x1, waiting for transfers between devices, per_device(): got = lax.all_to_all(message, DP, 0, 0)  10.2 us
    all_to_all x1, starting transfers between devices, per_device(): own_w = lax.all_to_all(mine, 'x', 0, 0)  9.48 us
    pallas_call x1, Pallas kernels, per_device(): call(attend_body, [((ROWS, WIDTH), bf16), ((ROWS, LANES), bf16), ((16, LA...  7.43 us
    pallas_call x1, Pallas kernels, per_device(): call(train_body, [((N_DP, 2, LANES), f32), ((ROWS, PAY), bf16), ((ROWS, P...  4.48 us
    unnamed x35, local copies, waits for them, and re-layouts  3.41 us
  transfers between devices with their start and end apart: 4, of which 2 were waited for; matrix products, arithmetic and copies ran while one was open for 3% of the time, Pallas kernels for 9%

profile of v11, /device:TPU:6, one launch (start us, length us, event | category | flops | bytes accessed | tf_op | source)
XLA Modules:
  0.0 97.3 jit_solution(1371078942942991208)
XLA Ops:
  0.6 2.3 %prepare.1 = bf16[4,2,128,512]{3,2,1,0:T(8,128)(2,1)} custom-call(s32[1]{0:T(128)} %bitcast.3.core_ref, bf16[512,256]{1,0:T(8,128)(2,1)} %w_in_hbm.1, bf16[256,512]{1,0:T(8,128)(2,1)} %w_down_hbm.1), custom_call_target="tpu_custom_call" | custom-call | flops 500000000 | bytes 2000000 | tf_op jit(solution)/shard_map/prepare/pallas_call | solution.py:346
  2.9 0.0 copy-start.15
  2.9 0.0 copy-start.14
  2.9 0.0 copy-start.12
  2.9 0.0 copy-start.13
  2.9 9.5 %all-to-all-start = ((bf16[4,2,128,512]{3,2,1,0:T(8,128)(2,1)}), bf16[4,2,128,512]{3,2,1,0:T(8,128)(2,1)S(1)}, u32[]{:S(2)}, u32[]{:S(2)}) async-start(bf16[4,2,128,512]{3,2,1,0:T(8,128)(2,1)} %prepare.1), calls=%async_computation | async-start | bytes 2097152 | tf_op jit(solution)/shard_map/all_to_all | solution.py:357
  12.4 0.0 copy-done.15
  12.5 0.1 reshape.26
  12.5 0.1 reshape.27
  12.6 0.1 stack_reshape.16
  12.7 0.0 copy-done.14
  12.7 0.1 reshape.25
  12.8 0.1 pad_slice_fusion
  12.9 0.1 stack_reshape.7
  13.0 0.1 stack_reshape.6
  13.1 0.0 copy-start.1
  13.1 0.8 copy.29.cols_ref
  13.9 0.0 copy-done.12
  13.9 0.8 copy.27.keys_ref
  14.7 0.0 copy-done.13
  14.7 0.8 copy.28.values_ref
  15.4 0.0 copy-done.1
  15.5 7.4 %attend.1 = (bf16[320,512]{1,0:T(8,128)(2,1)}, bf16[320,128]{1,0:T(8,128)(2,1)}, bf16[16,128]{1,0:T(8,128)(2,1)}) custom-call(s32[320,8]{1,0:T(8,128)} %copy.29.cols_ref, s32[8,320]{1,0:T(8,128)} %copy-done.1, bf16[2,150,512]{2,1,0:T(8,128)(2,1)} %copy.27.keys_ref, bf16[2,150,512]{2,1,0:T(8,128)(2,1)} %copy.28.values_ref, bf16[28,512]{1,0:T(8,128)(2,1)} %embed_ref.1, ...), custom_call_target="tpu_custom_call" | custom-call | flops 4000000000 | bytes 16000000 | tf_op jit(solution)/shard_map/attend/pallas_call | solution.py:366
  22.9 0.0 all-to-all-done.weights_ref.own_ref
  22.9 1.9 %collective-permute-start = (bf16[4,2,128,512]{3,2,1,0:T(8,128)(2,1)S(1)}, bf16[4,2,128,512]{3,2,1,0:T(8,128)(2,1)S(1)}, u32[]{:S(2)}, u32[]{:S(2)}) collective-permute-start(bf16[4,2,128,512]{3,2,1,0:T(8,128)(2,1)S(1)} %all-to-all-done.weights_ref.own_ref), channel_id=1, source_target_pairs={{0,4},{4,0},{1,5},{5,1},{2,6},{6,2},{3,7},{7,3},{8,12},{12,8},{9,1... | collective-permute-start | bytes 3145736 | tf_op jit(solution)/shard_map/ppermute | solution.py:380
  24.8 0.0 copy-start.8
  24.8 1.0 copy-done.8
  25.8 0.0 copy-start.11
  25.8 0.7 copy-done.11
  26.5 0.0 copy-start
  26.5 0.0 copy-start.2
  26.5 0.0 copy-start.3
  26.5 0.0 copy-start.5
  26.5 0.0 copy-start.6
  26.5 0.0 copy-start.9
  26.5 0.0 copy-start.10
  26.5 0.8 own.1
  27.4 0.1 collective-permute-done.other_ref
  27.5 0.0 copy-done
  27.5 0.0 copy-done.2
  27.5 0.0 copy-done.3
  27.5 0.0 copy-done.5
  27.5 0.0 copy-done.6
  27.5 0.1 copy-done.9
  27.6 0.0 copy-done.10
  27.6 4.5 %train.1 = (f32[128,2,128]{2,1,0:T(2,128)}, bf16[320,2176]{1,0:T(8,128)(2,1)}, bf16[320,2176]{1,0:T(8,128)(2,1)}) custom-call(s32[2]{0:T(128)S(1)} %copy-done.6, s32[320,8]{1,0:T(8,128)S(1)} %copy-done, s32[8,320]{1,0:T(8,128)S(1)} %copy-done.2, bf16[320,128]{1,0:T(8,128)(2,1)S(1)} %copy-done.10, bf16[320,512]{1,0:T(8,128)(2,1)S(1)} %copy-done.9, ...), custom_call_target="tpu_custom_call" | custom-call | flops 2500000000 | bytes 10000000 | tf_op jit(solution)/shard_map/train/pallas_call | solution.py:386
  32.1 15.9 %all-to-all-start.1 = ((f32[128,2,128]{2,1,0:T(2,128)}), f32[128,2,128]{2,1,0:T(2,128)S(1)}, u32[]{:S(2)}, u32[]{:S(2)}) async-start(f32[128,2,128]{2,1,0:T(2,128)} %get-tuple-element.25), calls=%async_computation.1 | async-start | bytes 262144 | tf_op jit(solution)/shard_map/all_to_all | solution.py:392
  48.0 0.0 copy-start.7
  48.0 2.1 %collective-permute-start.1 = (bf16[320,2176]{1,0:T(8,128)(2,1)}, bf16[320,2176]{1,0:T(8,128)(2,1)S(1)}, u32[]{:S(2)}, u32[]{:S(2)}) collective-permute-start(bf16[320,2176]{1,0:T(8,128)(2,1)} %get-tuple-element.24), channel_id=1, source_target_pairs={{0,4},{4,0},{1,5},{5,1},{2,6},{6,2},{3,7},{7,3},{8,12},{12,8},{9,1... | collective-permute-start | bytes 4177928 | tf_op jit(solution)/shard_map/ppermute | solution.py:393
  50.1 10.2 %all-to-all-done.1.got_ref = f32[128,2,128]{2,1,0:T(2,128)S(1)} async-done(((f32[128,2,128]{2,1,0:T(2,128)}), f32[128,2,128]{2,1,0:T(2,128)S(1)}, u32[]{:S(2)}, u32[]{:S(2)}) %all-to-all-start.1) | async-done | bytes 131104 | tf_op jit(solution)/shard_map/all_to_all | solution.py:392
  60.2 0.1 first.1
  60.3 0.0 collective-permute-done.1.other_ref
  60.3 0.0 copy-done.7
  60.3 1.1 %term.1 = bf16[4,128,1024]{2,1,0:T(8,128)(2,1)S(1)} custom-call(bf16[320,2176]{1,0:T(8,128)(2,1)S(1)} %copy-done.7, bf16[320,2176]{1,0:T(8,128)(2,1)S(1)} %collective-permute-done.1.other_ref, f32[8,128]{1,0:T(8,128)S(1)} %get-tuple-element.26.inverse_ref), custom_call_target="tpu_custom_call" | custom-call | flops 2000000000 | bytes 8000000 | tf_op jit(solution)/shard_map/term/pallas_call | solution.py:395
  61.4 12.4 %all_to_all.20.got_ref = bf16[4,128,1024]{2,1,0:T(8,128)(2,1)S(1)} all-to-all(bf16[4,128,1024]{2,1,0:T(8,128)(2,1)S(1)} %term.1), channel_id=1, replica_groups={{0,8,64,72},{1,9,65,73},{2,10,66,74},{3,11,67,75},{16,24,80,88},{17,25,..., dimensions={0} | all-to-all | bytes 2097152 | tf_op jit(solution)/shard_map/all_to_all | solution.py:401
  73.8 0.0 copy-start.4
  73.8 0.4 middle.1
  74.3 22.1 %all_to_all.21.got_ref = bf16[64,16,128]{2,1,0:T(8,128)(2,1)S(1)} all-to-all(bf16[64,16,128]{2,1,0:T(8,128)(2,1)S(1)} %middle.1), channel_id=1, replica_groups={{0,1,2,3,16,17,18,19,32,33,34,35,48,49,50,51,128,129,130,131,144,145,14..., dimensions={0} | all-to-all | bytes 524288 | tf_op jit(solution)/shard_map/all_to_all | solution.py:405
  96.4 0.0 copy-done.4
  96.4 0.9 final.1
  (5 shorter events, 0.1 us)
Async XLA Ops:
  2.9 9.5 %copy-start.15 = (s32[300,1]{0,1:T(1,128)S(1)}, s32[300,1]{0,1:T(1,128)}, u32[]{:S(2)}) copy-start(s32[300,1]{0,1:T(1,128)} %param.21) | copy-start | bytes 3604
  2.9 9.8 %copy-start.14 = (s32[2,5,31]{2,0,1:T(2,128)S(1)}, s32[2,5,31]{2,0,1:T(2,128)}, u32[]{:S(2)}) copy-start(s32[2,5,31]{2,0,1:T(2,128)} %param.19) | copy-start | bytes 3724
  2.9 11.0 %copy-start.12 = (bf16[2,150,512]{2,0,1:T(2,128)(2,1)S(1)}, bf16[2,150,512]{2,0,1:T(2,128)(2,1)}, u32[]{:S(2)}) copy-start(bf16[2,150,512]{2,0,1:T(2,128)(2,1)} %param.22) | copy-start | bytes 921604
  2.9 11.7 %copy-start.13 = (bf16[2,150,512]{2,0,1:T(2,128)(2,1)S(1)}, bf16[2,150,512]{2,0,1:T(2,128)(2,1)}, u32[]{:S(2)}) copy-start(bf16[2,150,512]{2,0,1:T(2,128)(2,1)} %param.23) | copy-start | bytes 921604
  2.9 19.9 %all-to-all-start = ((bf16[4,2,128,512]{3,2,1,0:T(8,128)(2,1)}), bf16[4,2,128,512]{3,2,1,0:T(8,128)(2,1)S(1)}, u32[]{:S(2)}, u32[]{:S(2)}) async-start(bf16[4,2,128,512]{3,2,1,0:T(8,128)(2,1)} %prepare.1), calls=%async_computation | async-start | bytes 2097152 | tf_op jit(solution)/shard_map/all_to_all | solution.py:357
  13.1 2.4 %copy-start.1 = (s32[8,320]{1,0:T(8,128)}, s32[8,320]{1,0:T(8,128)S(1)}, u32[]{:S(2)}) copy-start(s32[8,320]{1,0:T(8,128)S(1)} %stack.3.rows_ref) | copy-start | bytes 30724
  22.9 4.6 %collective-permute-start = (bf16[4,2,128,512]{3,2,1,0:T(8,128)(2,1)S(1)}, bf16[4,2,128,512]{3,2,1,0:T(8,128)(2,1)S(1)}, u32[]{:S(2)}, u32[]{:S(2)}) collective-permute-start(bf16[4,2,128,512]{3,2,1,0:T(8,128)(2,1)S(1)} %all-to-all-done.weights_ref.own_ref), channel_id=1, source_target_pairs={{0,4},{4,0},{1,5},{5,1},{2,6},{6,2},{3,7},{7,3},{8,12},{12,8},{9,1... | collective-permute-start | bytes 3145736 | tf_op jit(solution)/shard_map/ppermute | solution.py:380
  24.8 1.0 %copy-start.8 = (bf16[320,512]{1,0:T(8,128)(2,1)S(1)}, bf16[320,512]{1,0:T(8,128)(2,1)}, u32[]{:S(2)}) copy-start(bf16[320,512]{1,0:T(8,128)(2,1)} %get-tuple-element.16.states_ref) | copy-start | bytes 983044
  25.8 0.7 copy-start.11
  26.5 1.0 copy-start
  26.5 1.0 copy-start.2
  26.5 1.0 copy-start.3
  26.5 1.0 copy-start.5
  26.5 1.0 %copy-start.6 = (s32[2]{0:T(128)S(1)}, s32[2]{0:T(128)}, u32[]{:S(2)}) copy-start(s32[2]{0:T(128)} %accept_ref.1) | copy-start | bytes 28
  26.5 1.1 %copy-start.9 = (bf16[320,512]{1,0:T(8,128)(2,1)S(1)}, bf16[320,512]{1,0:T(8,128)(2,1)}, u32[]{:S(2)}) copy-start(bf16[320,512]{1,0:T(8,128)(2,1)} %get-tuple-element.16.states_ref) | copy-start | bytes 983044
  26.5 1.1 %copy-start.10 = (bf16[320,128]{1,0:T(8,128)(2,1)S(1)}, bf16[320,128]{1,0:T(8,128)(2,1)}, u32[]{:S(2)}) copy-start(bf16[320,128]{1,0:T(8,128)(2,1)} %get-tuple-element.15.at_rank_ref) | copy-start | bytes 245764
  32.1 28.1 %all-to-all-start.1 = ((f32[128,2,128]{2,1,0:T(2,128)}), f32[128,2,128]{2,1,0:T(2,128)S(1)}, u32[]{:S(2)}, u32[]{:S(2)}) async-start(f32[128,2,128]{2,1,0:T(2,128)} %get-tuple-element.25), calls=%async_computation.1 | async-start | bytes 262144 | tf_op jit(solution)/shard_map/all_to_all | solution.py:392
  48.0 12.3 %copy-start.7 = (bf16[320,2176]{1,0:T(8,128)(2,1)S(1)}, bf16[320,2176]{1,0:T(8,128)(2,1)}, u32[]{:S(2)}) copy-start(bf16[320,2176]{1,0:T(8,128)(2,1)} %get-tuple-element.23.keep_ref) | copy-start | bytes 4177924
  48.0 12.3 %collective-permute-start.1 = (bf16[320,2176]{1,0:T(8,128)(2,1)}, bf16[320,2176]{1,0:T(8,128)(2,1)S(1)}, u32[]{:S(2)}, u32[]{:S(2)}) collective-permute-start(bf16[320,2176]{1,0:T(8,128)(2,1)} %get-tuple-element.24), channel_id=1, source_target_pairs={{0,4},{4,0},{1,5},{5,1},{2,6},{6,2},{3,7},{7,3},{8,12},{12,8},{9,1... | collective-permute-start | bytes 4177928 | tf_op jit(solution)/shard_map/ppermute | solution.py:393
  73.8 22.6 %copy-start.4 = (f32[2,1024]{1,0:T(2,128)S(1)}, f32[2,1024]{1,0:T(2,128)}, u32[]{:S(2)}) copy-start(f32[2,1024]{1,0:T(2,128)} %momentum_ref.1) | copy-start | bytes 24580

commit v12 on v10

--- a/solution.py
+++ b/solution.py
@@ -49,10 +49,11 @@
             two.append([index(2 * a + z, 2 * b + y, 0, x) for a in half for b in half for x in ring])
     one += [[index(z, y, 1, x) for x in ring] for z in side for y in side]
     two += [[index(z, y, 1, x) for z in side for y in side] for x in ring]
-    return one, two
-
-
-STAGE_1, STAGE_2 = stages()
+    weights = [[index(z, y, core, x) for core in pair for z in side for y in side] for x in ring]
+    return one, two, weights
+
+
+STAGE_1, STAGE_2, SUMS = stages()
 
 
 def mm(a, b):
@@ -324,7 +325,7 @@
             lanes = slice(c * LANES, (c + 1) * LANES)
             out_ref[r : r + 1, lanes] = 0.9 * momentum_ref[r : r + 1, lanes] + total[r * 8 + c : r * 8 + c + 1]
     slot, source = iota((N_DP, N_DP * CAP), 1), iota((N_DP, N_DP * CAP), 0)
-    offset = slot - source * CAP
+    offset = slot - (source % (N_DP // 2) * 2 + source // (N_DP // 2)) * CAP
     spread = jnp.zeros((N_DP, N_DP * CAP), f32)
     for k in range(CAP):
         spread = jnp.where(offset == k, loss_ref[:, k : k + 1], spread)
@@ -355,6 +356,7 @@
     flat = tokens.reshape(2, SEG)
     nexts = lax.pad(flat, jnp.int32(0), ((0, 0, 0), (-1, PAD - SEG + 1, 0))).reshape(ROWS)
     flat = jnp.pad(flat, ((0, 0), (0, PAD - SEG))).reshape(ROWS)
+    dest = dest % 2 * (N_DP // 2) + dest // 2
     place = jnp.pad(dest.reshape(2, BEAM, STEPS), ((0, 0), (0, 0), (0, 1)), constant_values=-1).reshape(2, SEG)
     place = jnp.pad(place, ((0, 0), (0, PAD - SEG)), constant_values=-1).reshape(ROWS)
     rows = jnp.stack([flat, nexts, place, place, place, place, place, place])
@@ -385,7 +387,7 @@
         scratch=[pltpu.VMEM(half, bf16), pltpu.VMEM(half, f32), pltpu.VMEM((ROWS, WIDTH), f32)],
         n_smem=1, n_in=11, cost=5, name="train",
     )(accept, cols, rows, at_rank, states, partial, hidden, slope, own_w, other_w, gain, head)
-    got = lax.all_to_all(message, DP, 0, 0)
+    got = lax.all_to_all(message, EVERY, 0, 0, axis_index_groups=SUMS)
     other = lax.ppermute(send, "core", swap)
     term, loss = call(
         term_body,

time: 97.2 us -> 97.8 us (level)
  the two profiles are of different devices: /device:TPU:8 before, /device:TPU:6 now
where the time goes in v12:
time: 97.8 us; the launch traced here: 97.3 us
  blocking collectives  61.8 us (63%)
  Pallas kernels  16 us (16%)
  starting transfers between devices  13.8 us (14%)
  local copies, waits for them, and re-layouts  4.7 us (5%)
    all_to_all x1, blocking collectives, per_device(): got = lax.all_to_all(message, EVERY, 0, 0, axis_index_groups=SUMS)  29 us
    all_to_all x1, blocking collectives, per_device(): got = lax.all_to_all(middle, EVERY, 0, 0, axis_index_groups=STAGE_2)  20.5 us
    all_to_all x1, blocking collectives, per_device(): got = lax.all_to_all(term, EVERY, 0, 0, axis_index_groups=STAGE_1)  12.4 us
    all_to_all x1, starting transfers between devices, per_device(): own_w = lax.all_to_all(mine, 'x', 0, 0)  9.48 us
    pallas_call x1, Pallas kernels, per_device(): call(attend_body, [((ROWS, WIDTH), bf16), ((ROWS, LANES), bf16), ((16, LA...  7.43 us
    unnamed x31, local copies, waits for them, and re-layouts  3.27 us
    pallas_call x1, Pallas kernels, per_device(): call(train_body, [((N_DP, 2, LANES), f32), ((ROWS, PAY), bf16), ((ROWS, P...  2.92 us
    ppermute x1, starting transfers between devices, per_device(): other = lax.ppermute(send, 'core', swap)  2.41 us
  transfers between devices with their start and end apart: 3, of which 1 were waited for; matrix products, arithmetic and copies ran while one was open for 3% of the time, Pallas kernels for 9%

profile of v12, /device:TPU:6, one launch (start us, length us, event | category | flops | bytes accessed | tf_op | source)
XLA Modules:
  0.0 97.3 jit_solution(10234182035131178921)
XLA Ops:
  0.6 2.3 %prepare.1 = bf16[4,2,128,512]{3,2,1,0:T(8,128)(2,1)} custom-call(s32[1]{0:T(128)} %bitcast.3.core_ref, bf16[512,256]{1,0:T(8,128)(2,1)} %w_in_hbm.1, bf16[256,512]{1,0:T(8,128)(2,1)} %w_down_hbm.1), custom_call_target="tpu_custom_call" | custom-call | flops 500000000 | bytes 2000000 | tf_op jit(solution)/shard_map/prepare/pallas_call | solution.py:343
  2.9 0.0 copy-start.13
  2.9 0.0 copy-start.12
  3.0 0.0 copy-start.10
  3.0 0.0 copy-start.11
  3.0 9.5 %all-to-all-start = ((bf16[4,2,128,512]{3,2,1,0:T(8,128)(2,1)}), bf16[4,2,128,512]{3,2,1,0:T(8,128)(2,1)S(1)}, u32[]{:S(2)}, u32[]{:S(2)}) async-start(bf16[4,2,128,512]{3,2,1,0:T(8,128)(2,1)} %prepare.1), calls=%async_computation | async-start | bytes 2097152 | tf_op jit(solution)/shard_map/all_to_all | solution.py:354
  12.5 0.0 copy-done.13
  12.5 0.1 reshape.26
  12.6 0.1 reshape.27
  12.7 0.1 stack_reshape.16
  12.8 0.0 copy-done.12
  12.8 0.1 reshape.25
  12.9 0.1 pad_slice_fusion
  12.9 0.1 stack_reshape.7
  13.0 0.1 stack_reshape.6
  13.1 0.0 copy-start.1
  13.1 0.8 copy.29.cols_ref
  14.0 0.0 copy-done.10
  14.0 0.7 copy.27.keys_ref
  14.7 0.0 copy-done.11
  14.7 0.8 copy.28.values_ref
  15.5 0.0 copy-done.1
  15.5 7.4 %attend.1 = (bf16[320,512]{1,0:T(8,128)(2,1)}, bf16[320,128]{1,0:T(8,128)(2,1)}, bf16[16,128]{1,0:T(8,128)(2,1)}) custom-call(s32[320,8]{1,0:T(8,128)} %copy.29.cols_ref, s32[8,320]{1,0:T(8,128)} %copy-done.1, bf16[2,150,512]{2,1,0:T(8,128)(2,1)} %copy.27.keys_ref, bf16[2,150,512]{2,1,0:T(8,128)(2,1)} %copy.28.values_ref, bf16[28,512]{1,0:T(8,128)(2,1)} %embed_ref.1, ...), custom_call_target="tpu_custom_call" | custom-call | flops 4000000000 | bytes 16000000 | tf_op jit(solution)/shard_map/attend/pallas_call | solution.py:364
  22.9 0.0 all-to-all-done.weights_ref.own_ref
  22.9 1.9 %collective-permute-start = (bf16[4,2,128,512]{3,2,1,0:T(8,128)(2,1)S(1)}, bf16[4,2,128,512]{3,2,1,0:T(8,128)(2,1)S(1)}, u32[]{:S(2)}, u32[]{:S(2)}) collective-permute-start(bf16[4,2,128,512]{3,2,1,0:T(8,128)(2,1)S(1)} %all-to-all-done.weights_ref.own_ref), channel_id=1, source_target_pairs={{0,4},{4,0},{1,5},{5,1},{2,6},{6,2},{3,7},{7,3},{8,12},{12,8},{9,1... | collective-permute-start | bytes 3145736 | tf_op jit(solution)/shard_map/ppermute | solution.py:378
  24.9 0.0 copy-start.7
  24.9 1.0 copy-done.7
  25.8 0.0 copy-start.9
  25.8 0.7 copy-done.9
  26.5 0.0 copy-start
  26.5 0.0 copy-start.2
  26.5 0.0 copy-start.3
  26.5 0.0 copy-start.5
  26.5 0.0 copy-start.6
  26.5 0.0 copy-start.8
  26.6 0.8 own.1
  27.4 0.1 collective-permute-done.other_ref
  27.5 0.0 copy-done
  27.5 0.0 copy-done.2
  27.5 0.0 copy-done.3
  27.5 0.0 copy-done.5
  27.5 0.0 copy-done.6
  27.5 0.0 copy-done.8
  27.6 2.9 %train.1 = (f32[128,2,128]{2,1,0:T(2,128)S(1)}, bf16[320,2176]{1,0:T(8,128)(2,1)S(1)}, bf16[320,2176]{1,0:T(8,128)(2,1)S(1)}) custom-call(s32[2]{0:T(128)S(1)} %copy-done.6, s32[320,8]{1,0:T(8,128)S(1)} %copy-done, s32[8,320]{1,0:T(8,128)S(1)} %copy-done.2, bf16[320,128]{1,0:T(8,128)(2,1)S(1)} %copy-done.8, bf16[320,512]{1,0:T(8,128)(2,1)S(1)} %copy-done.7, ...), custom_call_target="tpu_custom_call" | custom-call | flops 2500000000 | bytes 10000000 | tf_op jit(solution)/shard_map/train/pallas_call | solution.py:384
  30.5 2.4 %collective-permute-start.1 = (bf16[320,2176]{1,0:T(8,128)(2,1)S(1)}, bf16[320,2176]{1,0:T(8,128)(2,1)S(1)}, u32[]{:S(2)}, u32[]{:S(2)}) collective-permute-start(bf16[320,2176]{1,0:T(8,128)(2,1)S(1)} %get-tuple-element.24), channel_id=1, source_target_pairs={{0,4},{4,0},{1,5},{5,1},{2,6},{6,2},{3,7},{7,3},{8,12},{12,8},{9,1... | collective-permute-start | bytes 4177928 | tf_op jit(solution)/shard_map/ppermute | solution.py:391
  32.9 29.0 %all_to_all.20.got_ref = f32[128,2,128]{2,1,0:T(2,128)S(1)} all-to-all(f32[128,2,128]{2,1,0:T(2,128)S(1)} %get-tuple-element.25), channel_id=1, replica_groups={{0,8,16,24,32,40,48,56,64,72,80,88,96,104,112,120,128,136,144,152,160,1..., dimensions={0} | all-to-all | bytes 262144 | tf_op jit(solution)/shard_map/all_to_all | solution.py:390
  61.9 0.0 collective-permute-done.1.other_ref
  61.9 1.2 %term.1 = (bf16[4,128,1024]{2,1,0:T(8,128)(2,1)S(1)}, f32[128,128]{1,0:T(8,128)S(1)}) custom-call(bf16[320,2176]{1,0:T(8,128)(2,1)S(1)} %get-tuple-element.23.keep_ref, bf16[320,2176]{1,0:T(8,128)(2,1)S(1)} %collective-permute-done.1.other_ref, f32[128,2,128]{2,1,0:T(2,128)S(1)} %all_to_all.20.got_ref), custom_call_target="tpu_custom_call" | custom-call | flops 2000000000 | bytes 8000000 | tf_op jit(solution)/shard_map/term/pallas_call | solution.py:392
  63.0 12.4 %all_to_all.21.got_ref = bf16[4,128,1024]{2,1,0:T(8,128)(2,1)S(1)} all-to-all(bf16[4,128,1024]{2,1,0:T(8,128)(2,1)S(1)} %get-tuple-element.26), channel_id=1, replica_groups={{0,8,64,72},{1,9,65,73},{2,10,66,74},{3,11,67,75},{16,24,80,88},{17,25,..., dimensions={0} | all-to-all | bytes 2097152 | tf_op jit(solution)/shard_map/all_to_all | solution.py:398
  75.4 0.0 copy-start.4
  75.4 0.5 middle.1
  75.9 20.5 %all_to_all.22.got_ref = bf16[64,16,128]{2,1,0:T(8,128)(2,1)S(1)} all-to-all(bf16[64,16,128]{2,1,0:T(8,128)(2,1)S(1)} %middle.1), channel_id=1, replica_groups={{0,1,2,3,16,17,18,19,32,33,34,35,48,49,50,51,128,129,130,131,144,145,14..., dimensions={0} | all-to-all | bytes 524288 | tf_op jit(solution)/shard_map/all_to_all | solution.py:402
  96.4 0.0 copy-done.4
  96.4 0.9 final.1
  (5 shorter events, 0.1 us)
Async XLA Ops:
  2.9 9.5 %copy-start.13 = (s32[300,1]{0,1:T(1,128)S(1)}, s32[300,1]{0,1:T(1,128)}, u32[]{:S(2)}) copy-start(s32[300,1]{0,1:T(1,128)} %param.21) | copy-start | bytes 3604
  2.9 9.8 %copy-start.12 = (s32[2,5,31]{2,0,1:T(2,128)S(1)}, s32[2,5,31]{2,0,1:T(2,128)}, u32[]{:S(2)}) copy-start(s32[2,5,31]{2,0,1:T(2,128)} %param.19) | copy-start | bytes 3724
  3.0 11.0 %copy-start.10 = (bf16[2,150,512]{2,0,1:T(2,128)(2,1)S(1)}, bf16[2,150,512]{2,0,1:T(2,128)(2,1)}, u32[]{:S(2)}) copy-start(bf16[2,150,512]{2,0,1:T(2,128)(2,1)} %param.22) | copy-start | bytes 921604
  3.0 11.7 %copy-start.11 = (bf16[2,150,512]{2,0,1:T(2,128)(2,1)S(1)}, bf16[2,150,512]{2,0,1:T(2,128)(2,1)}, u32[]{:S(2)}) copy-start(bf16[2,150,512]{2,0,1:T(2,128)(2,1)} %param.23) | copy-start | bytes 921604
  3.0 19.9 %all-to-all-start = ((bf16[4,2,128,512]{3,2,1,0:T(8,128)(2,1)}), bf16[4,2,128,512]{3,2,1,0:T(8,128)(2,1)S(1)}, u32[]{:S(2)}, u32[]{:S(2)}) async-start(bf16[4,2,128,512]{3,2,1,0:T(8,128)(2,1)} %prepare.1), calls=%async_computation | async-start | bytes 2097152 | tf_op jit(solution)/shard_map/all_to_all | solution.py:354
  13.1 2.3 %copy-start.1 = (s32[8,320]{1,0:T(8,128)}, s32[8,320]{1,0:T(8,128)S(1)}, u32[]{:S(2)}) copy-start(s32[8,320]{1,0:T(8,128)S(1)} %stack.3.rows_ref) | copy-start | bytes 30724
  22.9 4.6 %collective-permute-start = (bf16[4,2,128,512]{3,2,1,0:T(8,128)(2,1)S(1)}, bf16[4,2,128,512]{3,2,1,0:T(8,128)(2,1)S(1)}, u32[]{:S(2)}, u32[]{:S(2)}) collective-permute-start(bf16[4,2,128,512]{3,2,1,0:T(8,128)(2,1)S(1)} %all-to-all-done.weights_ref.own_ref), channel_id=1, source_target_pairs={{0,4},{4,0},{1,5},{5,1},{2,6},{6,2},{3,7},{7,3},{8,12},{12,8},{9,1... | collective-permute-start | bytes 3145736 | tf_op jit(solution)/shard_map/ppermute | solution.py:378
  24.9 1.0 %copy-start.7 = (bf16[320,512]{1,0:T(8,128)(2,1)S(1)}, bf16[320,512]{1,0:T(8,128)(2,1)}, u32[]{:S(2)}) copy-start(bf16[320,512]{1,0:T(8,128)(2,1)} %get-tuple-element.16.states_ref) | copy-start | bytes 983044
  25.8 0.7 copy-start.9
  26.5 1.0 copy-start
  26.5 1.0 copy-start.2
  26.5 1.0 copy-start.3
  26.5 1.0 copy-start.5
  26.5 1.0 %copy-start.6 = (s32[2]{0:T(128)S(1)}, s32[2]{0:T(128)}, u32[]{:S(2)}) copy-start(s32[2]{0:T(128)} %accept_ref.1) | copy-start | bytes 28
  26.5 1.0 %copy-start.8 = (bf16[320,128]{1,0:T(8,128)(2,1)S(1)}, bf16[320,128]{1,0:T(8,128)(2,1)}, u32[]{:S(2)}) copy-start(bf16[320,128]{1,0:T(8,128)(2,1)} %get-tuple-element.15.at_rank_ref) | copy-start | bytes 245764
  30.5 31.4 %collective-permute-start.1 = (bf16[320,2176]{1,0:T(8,128)(2,1)S(1)}, bf16[320,2176]{1,0:T(8,128)(2,1)S(1)}, u32[]{:S(2)}, u32[]{:S(2)}) collective-permute-start(bf16[320,2176]{1,0:T(8,128)(2,1)S(1)} %get-tuple-element.24), channel_id=1, source_target_pairs={{0,4},{4,0},{1,5},{5,1},{2,6},{6,2},{3,7},{7,3},{8,12},{12,8},{9,1... | collective-permute-start | bytes 4177928 | tf_op jit(solution)/shard_map/ppermute | solution.py:391
  75.4 21.0 %copy-start.4 = (f32[2,1024]{1,0:T(2,128)S(1)}, f32[2,1024]{1,0:T(2,128)}, u32[]{:S(2)}) copy-start(f32[2,1024]{1,0:T(2,128)} %momentum_ref.1) | copy-start | bytes 24580
